TPU v7x, 32 devices: a whole 2x2x4 slice. The times are simulated.
32 devices in a mesh: row: 8 (over z, y), col: 4 (over x, core).
Axes of the slice: x: 2, y: 2, z: 4, core: 2. Of those that a mesh axis runs over, the one named last changes fastest.
Arguments:
- fractions_source: float32 [12, 512, 512], P('col', 'row'), may hold values from 0 to 1, as said below
- x_source_edges: int32 [513], replicated, may hold values from 0 to 24576, as said below
- x_target_edges: int32 [385], replicated, may hold values from 0 to 24576, as said below
- y_source_edges: int32 [513], replicated, may hold values from 0 to 24576, as said below
- y_target_edges: int32 [385], replicated, may hold values from 0 to 24576, as said below
- conductivity_table: int32 [6], replicated, may hold values from 4 to 64
- capacity: float32 [6], replicated, may hold values from 0.5 to 4
- thermal_source_term: float32 [2, 384, 384], P(None, 'row', 'col'), may hold values from -40 to 40
Outputs:
- rezoned_occupancy_shares: float32 [12, 384, 384], P(None, 'row', 'col')
- thermal_iterate: float32 [2, 384, 384], P(None, 'row', 'col')
- remaining_defect: float32 [2, 384, 384], P(None, 'row', 'col')
Inputs may be any that keep to these rules, and one draw needn't show every extreme that they name: `fractions_source`: positive; for every z layer and source cell the 6 materials' fractions sum to one. `x_source_edges`: strictly increasing; every 64-th source edge along x coincides with every 48-th target edge along x, at multiples of 3072; the first edge is 0 and the last is the largest value. `x_target_edges`: strictly increasing; shares the walls of x_source_edges at every 48-th edge; the first edge is 0 and the last is the largest value. `y_source_edges`: strictly increasing; every 64-th source edge along y coincides with every 48-th target edge along y, at multiples of 3072; the first edge is 0 and the last is the largest value. `y_target_edges`: strictly increasing; shares the walls of y_source_edges at every 48-th edge; the first edge is 0 and the last is the largest value.
All inputs are finite; a program needn't handle non-finite values.
Results may differ from a plain program's by a relative error of at most 0.0003.
Values sent between devices are 32-bit elements; how exact they have to be, the bound alone decides.
No kernel may reach another device: no remote copies, remote signals or barrier semaphores. Data moves between devices by JAX's collectives and lax.ppermute only.
A program may use at most 64 MiB of HBM per device.

v0:
```python
import jax
import jax.numpy as jnp
from jax import lax
from jax.sharding import PartitionSpec as P

M = 6
SBLK = 64
TBLK = 48
ITERS = 3


def extended(cells, sides, width):
    for axis, dim in sides:
        count = lax.axis_size(axis)
        ends = count - 1
        head = lax.slice_in_dim(cells, 0, width, axis=dim)
        tail = lax.slice_in_dim(cells, cells.shape[dim] - width, cells.shape[dim], axis=dim)
        cells = jnp.concatenate(
            [
                lax.ppermute(tail, axis, [(i, (i + 1) % count) for i in range(ends)]),
                cells,
                lax.ppermute(head, axis, [((i + 1) % count, i) for i in range(ends)]),
            ],
            axis=dim,
        )
    return cells


def margin_blocks(source_edges, target_mesh_edges, source_block, target_block):
    block_list = (source_edges.shape[0] - 1) // source_block
    src_lo = source_edges[:-1].reshape(block_list, 1, source_block)
    src_hi = source_edges[1:].reshape(block_list, 1, source_block)
    tgt_lo = target_mesh_edges[:-1].reshape(block_list, target_block, 1)
    tgt_hi = target_mesh_edges[1:].reshape(block_list, target_block, 1)
    shared = jnp.maximum(jnp.minimum(src_hi, tgt_hi) - jnp.maximum(src_lo, tgt_lo), 0)
    return shared.astype(jnp.float32) / (tgt_hi - tgt_lo).astype(jnp.float32)


def face_weights(padded_array):
    center = padded_array[1:-1, 1:-1, 1:-1]
    neighbours = (
        padded_array[2:, 1:-1, 1:-1],
        padded_array[:-2, 1:-1, 1:-1],
        padded_array[1:-1, 2:, 1:-1],
        padded_array[1:-1, :-2, 1:-1],
        padded_array[1:-1, 1:-1, 2:],
        padded_array[1:-1, 1:-1, :-2],
    )
    return tuple((2.0 * center * beside / (center + beside) for beside in neighbours))


def stencil(padded_field, face_list, cell_capacity):
    center = padded_field[1:-1, 1:-1, 1:-1]
    neighbours = (
        padded_field[2:, 1:-1, 1:-1],
        padded_field[:-2, 1:-1, 1:-1],
        padded_field[1:-1, 2:, 1:-1],
        padded_field[1:-1, :-2, 1:-1],
        padded_field[1:-1, 1:-1, 2:],
        padded_field[1:-1, 1:-1, :-2],
    )
    result = cell_capacity * center
    for weight, beside in zip(face_list, neighbours):
        result = result + weight * (center - beside)
    return result


def two_products(remaining_defect, applied):
    return lax.psum(
        (jnp.sum(remaining_defect * remaining_defect), jnp.sum(remaining_defect * applied)),
        ("row", "col"),
    )


def per_device(
    fractions_source,
    x_source_edges,
    x_target_edges,
    y_source_edges,
    y_target_edges,
    conductivity_table,
    capacity,
    thermal_source_term,
):
    weight_x = margin_blocks(x_source_edges, x_target_edges, SBLK, TBLK)
    vertical_factor = margin_blocks(y_source_edges, y_target_edges, SBLK, TBLK)
    my_pairs = fractions_source.shape[0]
    block_list = vertical_factor.shape[0]
    source_grid = fractions_source.reshape(my_pairs, SBLK, block_list, SBLK)
    along_y = jnp.einsum(
        "psbu,bvu->psbv", source_grid, vertical_factor, precision=lax.Precision.HIGHEST
    )
    along_y = along_y.reshape(my_pairs, SBLK, block_list * TBLK)
    regrouped = lax.all_to_all(along_y, "row", split_axis=2, concat_axis=1, tiled=True)
    column_count = regrouped.reshape(my_pairs, block_list, SBLK, TBLK)
    rezoned = jnp.einsum("pasv,ats->pvat", column_count, weight_x, precision=lax.Precision.HIGHEST)
    rezoned = rezoned.reshape(my_pairs, TBLK, block_list * TBLK)
    rezoned_occupancy_shares = lax.all_to_all(
        rezoned, "col", split_axis=2, concat_axis=0, tiled=True
    )
    zlayers = thermal_source_term.shape[0]
    stacked = rezoned_occupancy_shares.reshape(
        zlayers, M, rezoned_occupancy_shares.shape[1], rezoned_occupancy_shares.shape[2]
    )
    substance_diffusivity = conductivity_table.astype(jnp.float32) / 16.0
    inverse = jnp.sum(stacked / substance_diffusivity[None, :, None, None], axis=1)
    cell_k = 1.0 / inverse
    cell_capacity = jnp.sum(stacked * capacity[None, :, None, None], axis=1)
    padded_k = extended(cell_k, (("row", 1), ("col", 2)), 1)
    padded_k = jnp.pad(padded_k, ((1, 1), (0, 0), (0, 0)))
    face_list = face_weights(padded_k)

    def operate(field):
        padded_field = extended(field, (("row", 1), ("col", 2)), 1)
        padded_field = jnp.pad(padded_field, ((1, 1), (0, 0), (0, 0)))
        return stencil(padded_field, face_list, cell_capacity)

    thermal_iterate = jnp.zeros_like(thermal_source_term)
    remaining_defect = thermal_source_term
    applied = operate(remaining_defect)
    norm_now, product = two_products(remaining_defect, applied)
    line_minimizer_alpha = norm_now / product
    conjugate_update_vector = remaining_defect
    along_dir = applied
    for iteration in range(ITERS):
        thermal_iterate = thermal_iterate + line_minimizer_alpha * conjugate_update_vector
        remaining_defect = remaining_defect - line_minimizer_alpha * along_dir
        if iteration + 1 < ITERS:
            applied = operate(remaining_defect)
            norm_next, product = two_products(remaining_defect, applied)
            gain_ratio = norm_next / norm_now
            line_minimizer_alpha = norm_next / (
                product - gain_ratio * norm_next / line_minimizer_alpha
            )
            conjugate_update_vector = remaining_defect + gain_ratio * conjugate_update_vector
            along_dir = applied + gain_ratio * along_dir
            norm_now = norm_next
    return (rezoned_occupancy_shares, thermal_iterate, remaining_defect)


def solution(mesh):
    placed = (P("col", "row", None), P(), P(), P(), P(), P(), P(), P(None, "row", "col"))
    return jax.shard_map(
        per_device,
        mesh=mesh,
        in_specs=placed,
        out_specs=(P(None, "row", "col"), P(None, "row", "col"), P(None, "row", "col")),
        check_vma=False,
    )
```

profile of v0, /device:TPU:0, one launch (start us, length us, event | category | flops | bytes accessed | tf_op | source)
XLA Modules:
  0.0 226.8 jit_solution(12837429503914555716)
XLA Ops:
  0.6 1.2 reshape.75
  2.1 0.6 copy-done.3
  2.9 1.8 convolution_bitcast_fusion.1
  5.0 1.3 reshape.80
  6.3 7.4 %all-to-all-start = ((f32[8,1,9216]{2,1,0:T(1,128)}), f32[8,1,9216]{2,1,0:T(1,128)S(1)}, u32[]{:S(2)}, u32[]{:S(2)}) async-start(f32[8,1,9216]{2,1,0:T(1,128)} %reshape.80), calls=%async_computation | async-start | bytes 589824 | tf_op jit(solution)/shard_map/all_to_all | solution.py:94
  13.8 1.3 collective-permute-start.5
  15.1 4.5 %collective-permute-start.4 = (f32[2,1,96]{2,1,0:T(1,128)S(1)}, f32[2,1,96]{2,1,0:T(1,128)S(1)}, u32[]{:S(2)}, u32[]{:S(2)}) collective-permute-start(f32[2,1,96]{2,1,0:T(1,128)S(1)} %get-tuple-element.41), channel_id=1, source_target_pairs={{0,4},{4,8},{8,12},{12,16},{16,20},{20,24},{24,28},{1,5},{5,9},{9,... | collective-permute-start | bytes 2312 | tf_op jit(solution)/shard_map/ppermute | solution.py:20
  19.9 0.6 copy-done.4
  20.7 2.7 %all-to-all-done = f32[8,1,9216]{2,1,0:T(1,128)S(1)} async-done(((f32[8,1,9216]{2,1,0:T(1,128)}), f32[8,1,9216]{2,1,0:T(1,128)S(1)}, u32[]{:S(2)}, u32[]{:S(2)}) %all-to-all-start) | async-done | bytes 294944 | tf_op jit(solution)/shard_map/all_to_all | solution.py:94
  23.4 0.5 broadcast.153
  23.9 1.3 reduce.4
  25.2 0.4 reshape.81
  25.7 1.6 convolution_bitcast_fusion
  27.3 0.3 copy.85
  27.6 1.4 reshape.82
  29.1 3.5 %all-to-all-start.1 = ((f32[4,1,13824]{2,1,0:T(1,128)}), f32[4,1,13824]{2,1,0:T(1,128)S(1)}, u32[]{:S(2)}, u32[]{:S(2)}) async-start(f32[4,1,13824]{2,1,0:T(1,128)} %reshape.82), calls=%async_computation.1 | async-start | bytes 442368 | tf_op jit(solution)/shard_map/all_to_all | solution.py:98
  32.6 0.6 copy-done.6
  33.6 4.5 %all-to-all-done.1 = f32[4,1,13824]{2,1,0:T(1,128)S(1)} async-done(((f32[4,1,13824]{2,1,0:T(1,128)}), f32[4,1,13824]{2,1,0:T(1,128)S(1)}, u32[]{:S(2)}, u32[]{:S(2)}) %all-to-all-start.1) | async-done | bytes 221216 | tf_op jit(solution)/shard_map/all_to_all | solution.py:98
  38.1 1.3 reduce.5
  39.4 0.6 reshape.83
  40.7 3.3 %collective-permute-start = (f32[2,1,96]{2,1,0:T(1,128)S(1)}, f32[2,1,96]{2,1,0:T(1,128)S(1)}, u32[]{:S(2)}, u32[]{:S(2)}) collective-permute-start(f32[2,1,96]{2,1,0:T(1,128)S(1)} %get-tuple-element.40), channel_id=1, source_target_pairs={{0,4},{4,8},{8,12},{12,16},{16,20},{20,24},{24,28},{1,5},{5,9},{9,... | collective-permute-start | bytes 2312 | tf_op jit(solution)/shard_map/ppermute | solution.py:20
  44.0 1.3 collective-permute-start.1
  45.4 1.3 collective-permute-start.6
  46.7 1.3 collective-permute-start.7
  48.0 1.5 collective-permute-done.1
  49.6 1.3 collective-permute-start.3
  50.9 3.0 %collective-permute-start.2 = (f32[2,50,1]{2,1,0:T(8,128)S(1)}, f32[2,50,1]{2,1,0:T(8,128)S(1)}, u32[]{:S(2)}, u32[]{:S(2)}) collective-permute-start(f32[2,50,1]{2,1,0:T(8,128)S(1)} %get-tuple-element.29), channel_id=1, source_target_pairs={{0,1},{1,2},{2,3},{4,5},{5,6},{6,7},{8,9},{9,10},{10,11},{12,13},{... | collective-permute-start | bytes 1208 | tf_op jit(solution)/shard_map/ppermute | solution.py:20
  54.2 0.6 collective-permute-done.2
  54.9 0.8 multiply_reduce_fusion.4
  55.7 43.2 %all-reduce.6 = (f32[]{:T(128)}, f32[]{:T(128)}) all-reduce(f32[]{:T(128)} %get-tuple-element.13, f32[]{:T(128)} %get-tuple-element.12), channel_id=1, replica_groups=mesh['row'=8,'col'=4] {'row','col'}, use_global_device_ids=true, to_apply=%region_1.0 | all-reduce | flops 2 | bytes 16 | tf_op jit(solution)/shard_map/psum | solution.py:69
  100.3 1.3 collective-permute-start.9
  101.6 5.0 %collective-permute-start.8 = (f32[2,1,96]{2,1,0:T(1,128)S(1)}, f32[2,1,96]{2,1,0:T(1,128)S(1)}, u32[]{:S(2)}, u32[]{:S(2)}) collective-permute-start(f32[2,1,96]{2,1,0:T(1,128)S(1)} %get-tuple-element.37), channel_id=1, source_target_pairs={{0,4},{4,8},{8,12},{12,16},{16,20},{20,24},{24,28},{1,5},{5,9},{9,... | collective-permute-start | bytes 2312 | tf_op jit(solution)/shard_map/ppermute | solution.py:20
  106.6 1.3 collective-permute-done.8
  108.0 1.3 collective-permute-start.10
  109.3 1.3 collective-permute-start.11
  110.6 4.0 %collective-permute-done.11 = f32[2,50,1]{2,1,0:T(8,128)S(1)} collective-permute-done((f32[2,50,1]{2,1,0:T(8,128)S(1)}, f32[2,50,1]{2,1,0:T(8,128)S(1)}, u32[]{:S(2)}, u32[]{:S(2)}) %collective-permute-start.11) | collective-permute-done | bytes 432 | tf_op jit(solution)/shard_map/ppermute | solution.py:22
  114.7 0.8 multiply_reduce_fusion.2
  115.6 43.5 %all-reduce.5 = (f32[]{:T(128)}, f32[]{:T(128)}) all-reduce(f32[]{:T(128)} %get-tuple-element.11, f32[]{:T(128)} %get-tuple-element.10), channel_id=1, replica_groups=mesh['row'=8,'col'=4] {'row','col'}, use_global_device_ids=true, to_apply=%region_9.10 | all-reduce | flops 2 | bytes 16 | tf_op jit(solution)/shard_map/psum | solution.py:69
  163.6 1.3 collective-permute-start.13
  164.9 5.0 %collective-permute-start.12 = (f32[2,1,96]{2,1,0:T(1,128)S(1)}, f32[2,1,96]{2,1,0:T(1,128)S(1)}, u32[]{:S(2)}, u32[]{:S(2)}) collective-permute-start(f32[2,1,96]{2,1,0:T(1,128)S(1)} %get-tuple-element.35), channel_id=1, source_target_pairs={{0,4},{4,8},{8,12},{12,16},{16,20},{20,24},{24,28},{1,5},{5,9},{9,... | collective-permute-start | bytes 2312 | tf_op jit(solution)/shard_map/ppermute | solution.py:20
  169.9 1.3 collective-permute-done.12
  171.3 1.3 collective-permute-start.14
  172.6 1.3 collective-permute-start.15
  173.9 0.9 copy.73
  174.8 3.1 %collective-permute-done.15 = f32[2,50,1]{2,1,0:T(8,128)S(1)} collective-permute-done((f32[2,50,1]{2,1,0:T(8,128)S(1)}, f32[2,50,1]{2,1,0:T(8,128)S(1)}, u32[]{:S(2)}, u32[]{:S(2)}) %collective-permute-start.15) | collective-permute-done | bytes 432 | tf_op jit(solution)/shard_map/ppermute | solution.py:22
  178.0 0.8 multiply_reduce_fusion
  178.8 43.5 %all-reduce.4 = (f32[]{:T(128)}, f32[]{:T(128)}) all-reduce(f32[]{:T(128)} %get-tuple-element.9, f32[]{:T(128)} %get-tuple-element.8), channel_id=1, replica_groups=mesh['row'=8,'col'=4] {'row','col'}, use_global_device_ids=true, to_apply=%region_13.14 | all-reduce | flops 2 | bytes 16 | tf_op jit(solution)/shard_map/psum | solution.py:69
  226.2 0.7 multiply_subtract_fusion
  (66 shorter events, 3.2 us)
Async XLA Ops:
  0.6 1.2 copy-start.1
  2.0 0.7 copy-start.3
  6.3 7.4 %copy-start = (f32[2,48,96]{2,1,0:T(8,128)S(1)}, f32[2,48,96]{2,1,0:T(8,128)}, u32[]{:S(2)}) copy-start(f32[2,48,96]{2,1,0:T(8,128)} %param.15) | copy-start | bytes 110596
  6.3 17.0 %all-to-all-start = ((f32[8,1,9216]{2,1,0:T(1,128)}), f32[8,1,9216]{2,1,0:T(1,128)S(1)}, u32[]{:S(2)}, u32[]{:S(2)}) async-start(f32[8,1,9216]{2,1,0:T(1,128)} %reshape.80), calls=%async_computation | async-start | bytes 589824 | tf_op jit(solution)/shard_map/all_to_all | solution.py:94
  13.8 5.9 %copy-start.2 = (s32[385]{0:T(512)S(1)}, s32[385]{0:T(512)}, u32[]{:S(2)}) copy-start(s32[385]{0:T(512)} %param.10) | copy-start | bytes 4624
  13.8 19.8 %collective-permute-start.5 = (f32[2,1,96]{2,1,0:T(1,128)S(1)}, f32[2,1,96]{2,1,0:T(1,128)S(1)}, u32[]{:S(2)}, u32[]{:S(2)}) collective-permute-start(f32[2,1,96]{2,1,0:T(1,128)S(1)} %get-tuple-element.42), channel_id=1, source_target_pairs={{4,0},{8,4},{12,8},{16,12},{20,16},{24,20},{28,24},{5,1},{9,5},{13... | collective-permute-start | bytes 2312 | tf_op jit(solution)/shard_map/ppermute | solution.py:22
  15.1 18.5 %collective-permute-start.4 = (f32[2,1,96]{2,1,0:T(1,128)S(1)}, f32[2,1,96]{2,1,0:T(1,128)S(1)}, u32[]{:S(2)}, u32[]{:S(2)}) collective-permute-start(f32[2,1,96]{2,1,0:T(1,128)S(1)} %get-tuple-element.41), channel_id=1, source_target_pairs={{0,4},{4,8},{8,12},{12,16},{16,20},{20,24},{24,28},{1,5},{5,9},{9,... | collective-permute-start | bytes 2312 | tf_op jit(solution)/shard_map/ppermute | solution.py:20
  19.8 0.7 copy-start.4
  29.1 3.5 %copy-start.5 = (s32[6]{0:T(128)S(1)}, s32[6]{0:T(128)}, u32[]{:S(2)}) copy-start(s32[6]{0:T(128)} %param.13) | copy-start | bytes 76
  29.1 9.1 %all-to-all-start.1 = ((f32[4,1,13824]{2,1,0:T(1,128)}), f32[4,1,13824]{2,1,0:T(1,128)S(1)}, u32[]{:S(2)}, u32[]{:S(2)}) async-start(f32[4,1,13824]{2,1,0:T(1,128)} %reshape.82), calls=%async_computation.1 | async-start | bytes 442368 | tf_op jit(solution)/shard_map/all_to_all | solution.py:98
  32.6 0.7 copy-start.6
  40.7 7.3 %collective-permute-start = (f32[2,1,96]{2,1,0:T(1,128)S(1)}, f32[2,1,96]{2,1,0:T(1,128)S(1)}, u32[]{:S(2)}, u32[]{:S(2)}) collective-permute-start(f32[2,1,96]{2,1,0:T(1,128)S(1)} %get-tuple-element.40), channel_id=1, source_target_pairs={{0,4},{4,8},{8,12},{12,16},{16,20},{20,24},{24,28},{1,5},{5,9},{9,... | collective-permute-start | bytes 2312 | tf_op jit(solution)/shard_map/ppermute | solution.py:20
  44.0 5.5 %collective-permute-start.1 = (f32[2,1,96]{2,1,0:T(1,128)S(1)}, f32[2,1,96]{2,1,0:T(1,128)S(1)}, u32[]{:S(2)}, u32[]{:S(2)}) collective-permute-start(f32[2,1,96]{2,1,0:T(1,128)S(1)} %get-tuple-element.39), channel_id=1, source_target_pairs={{4,0},{8,4},{12,8},{16,12},{20,16},{24,20},{28,24},{5,1},{9,5},{13... | collective-permute-start | bytes 2312 | tf_op jit(solution)/shard_map/ppermute | solution.py:22
  45.4 8.5 %collective-permute-start.6 = (f32[2,50,1]{2,1,0:T(8,128)S(1)}, f32[2,50,1]{2,1,0:T(8,128)S(1)}, u32[]{:S(2)}, u32[]{:S(2)}) collective-permute-start(f32[2,50,1]{2,1,0:T(8,128)S(1)} %get-tuple-element.32), channel_id=1, source_target_pairs={{0,1},{1,2},{2,3},{4,5},{5,6},{6,7},{8,9},{9,10},{10,11},{12,13},{... | collective-permute-start | bytes 1208 | tf_op jit(solution)/shard_map/ppermute | solution.py:20
  46.7 7.2 %collective-permute-start.7 = (f32[2,50,1]{2,1,0:T(8,128)S(1)}, f32[2,50,1]{2,1,0:T(8,128)S(1)}, u32[]{:S(2)}, u32[]{:S(2)}) collective-permute-start(f32[2,50,1]{2,1,0:T(8,128)S(1)} %get-tuple-element.31), channel_id=1, source_target_pairs={{1,0},{2,1},{3,2},{5,4},{6,5},{7,6},{9,8},{10,9},{11,10},{13,12},{... | collective-permute-start | bytes 1208 | tf_op jit(solution)/shard_map/ppermute | solution.py:22
  49.6 4.6 %collective-permute-start.3 = (f32[2,50,1]{2,1,0:T(8,128)S(1)}, f32[2,50,1]{2,1,0:T(8,128)S(1)}, u32[]{:S(2)}, u32[]{:S(2)}) collective-permute-start(f32[2,50,1]{2,1,0:T(8,128)S(1)} %get-tuple-element.30), channel_id=1, source_target_pairs={{1,0},{2,1},{3,2},{5,4},{6,5},{7,6},{9,8},{10,9},{11,10},{13,12},{... | collective-permute-start | bytes 1208 | tf_op jit(solution)/shard_map/ppermute | solution.py:22
  50.9 3.9 %collective-permute-start.2 = (f32[2,50,1]{2,1,0:T(8,128)S(1)}, f32[2,50,1]{2,1,0:T(8,128)S(1)}, u32[]{:S(2)}, u32[]{:S(2)}) collective-permute-start(f32[2,50,1]{2,1,0:T(8,128)S(1)} %get-tuple-element.29), channel_id=1, source_target_pairs={{0,1},{1,2},{2,3},{4,5},{5,6},{6,7},{8,9},{9,10},{10,11},{12,13},{... | collective-permute-start | bytes 1208 | tf_op jit(solution)/shard_map/ppermute | solution.py:20
  100.3 6.3 %collective-permute-start.9 = (f32[2,1,96]{2,1,0:T(1,128)S(1)}, f32[2,1,96]{2,1,0:T(1,128)S(1)}, u32[]{:S(2)}, u32[]{:S(2)}) collective-permute-start(f32[2,1,96]{2,1,0:T(1,128)S(1)} %get-tuple-element.38), channel_id=1, source_target_pairs={{4,0},{8,4},{12,8},{16,12},{20,16},{24,20},{28,24},{5,1},{9,5},{13... | collective-permute-start | bytes 2312 | tf_op jit(solution)/shard_map/ppermute | solution.py:22
  101.6 6.3 %collective-permute-start.8 = (f32[2,1,96]{2,1,0:T(1,128)S(1)}, f32[2,1,96]{2,1,0:T(1,128)S(1)}, u32[]{:S(2)}, u32[]{:S(2)}) collective-permute-start(f32[2,1,96]{2,1,0:T(1,128)S(1)} %get-tuple-element.37), channel_id=1, source_target_pairs={{0,4},{4,8},{8,12},{12,16},{16,20},{20,24},{24,28},{1,5},{5,9},{9,... | collective-permute-start | bytes 2312 | tf_op jit(solution)/shard_map/ppermute | solution.py:20
  108.0 2.6 %collective-permute-start.10 = (f32[2,50,1]{2,1,0:T(8,128)S(1)}, f32[2,50,1]{2,1,0:T(8,128)S(1)}, u32[]{:S(2)}, u32[]{:S(2)}) collective-permute-start(f32[2,50,1]{2,1,0:T(8,128)S(1)} %get-tuple-element.28), channel_id=1, source_target_pairs={{0,1},{1,2},{2,3},{4,5},{5,6},{6,7},{8,9},{9,10},{10,11},{12,13},{... | collective-permute-start | bytes 1208 | tf_op jit(solution)/shard_map/ppermute | solution.py:20
  109.3 5.3 %collective-permute-start.11 = (f32[2,50,1]{2,1,0:T(8,128)S(1)}, f32[2,50,1]{2,1,0:T(8,128)S(1)}, u32[]{:S(2)}, u32[]{:S(2)}) collective-permute-start(f32[2,50,1]{2,1,0:T(8,128)S(1)} %get-tuple-element.27), channel_id=1, source_target_pairs={{1,0},{2,1},{3,2},{5,4},{6,5},{7,6},{9,8},{10,9},{11,10},{13,12},{... | collective-permute-start | bytes 1208 | tf_op jit(solution)/shard_map/ppermute | solution.py:22
  163.6 6.3 %collective-permute-start.13 = (f32[2,1,96]{2,1,0:T(1,128)S(1)}, f32[2,1,96]{2,1,0:T(1,128)S(1)}, u32[]{:S(2)}, u32[]{:S(2)}) collective-permute-start(f32[2,1,96]{2,1,0:T(1,128)S(1)} %get-tuple-element.36), channel_id=1, source_target_pairs={{4,0},{8,4},{12,8},{16,12},{20,16},{24,20},{28,24},{5,1},{9,5},{13... | collective-permute-start | bytes 2312 | tf_op jit(solution)/shard_map/ppermute | solution.py:22
  164.9 6.3 %collective-permute-start.12 = (f32[2,1,96]{2,1,0:T(1,128)S(1)}, f32[2,1,96]{2,1,0:T(1,128)S(1)}, u32[]{:S(2)}, u32[]{:S(2)}) collective-permute-start(f32[2,1,96]{2,1,0:T(1,128)S(1)} %get-tuple-element.35), channel_id=1, source_target_pairs={{0,4},{4,8},{8,12},{12,16},{16,20},{20,24},{24,28},{1,5},{5,9},{9,... | collective-permute-start | bytes 2312 | tf_op jit(solution)/shard_map/ppermute | solution.py:20
  171.3 3.5 %collective-permute-start.14 = (f32[2,50,1]{2,1,0:T(8,128)S(1)}, f32[2,50,1]{2,1,0:T(8,128)S(1)}, u32[]{:S(2)}, u32[]{:S(2)}) collective-permute-start(f32[2,50,1]{2,1,0:T(8,128)S(1)} %get-tuple-element.26), channel_id=1, source_target_pairs={{0,1},{1,2},{2,3},{4,5},{5,6},{6,7},{8,9},{9,10},{10,11},{12,13},{... | collective-permute-start | bytes 1208 | tf_op jit(solution)/shard_map/ppermute | solution.py:20
  172.6 5.3 %collective-permute-start.15 = (f32[2,50,1]{2,1,0:T(8,128)S(1)}, f32[2,50,1]{2,1,0:T(8,128)S(1)}, u32[]{:S(2)}, u32[]{:S(2)}) collective-permute-start(f32[2,50,1]{2,1,0:T(8,128)S(1)} %get-tuple-element.25), channel_id=1, source_target_pairs={{1,0},{2,1},{3,2},{5,4},{6,5},{7,6},{9,8},{10,9},{11,10},{13,12},{... | collective-permute-start | bytes 1208 | tf_op jit(solution)/shard_map/ppermute | solution.py:22
where the time goes:
time: 228 us; the launch traced here: 227 us
  blocking collectives  130 us (57%)
  starting transfers between devices  46 us (20%)
  waiting for transfers between devices  18.9 us (8%)
  between operations  10.8 us (5%)
  local copies, waits for them, and re-layouts  10.7 us (5%)
  other arithmetic  6.74 us (3%)
  matrix products  3.47 us (2%)
    psum x3, blocking collectives, two_products(): lax.psum((jnp.sum(remaining_defect * remaining_defect), jnp.sum(remaining...  130 us
    ppermute x8, starting transfers between devices, extended(): lax.ppermute(tail, axis, [(i, (i + 1) % count) for i in range(ends)])  24.8 us
    ppermute x8, starting transfers between devices, extended(): lax.ppermute(head, axis, [((i + 1) % count, i) for i in range(ends)])  10.3 us
    ppermute x8, waiting for transfers between devices, extended(): lax.ppermute(head, axis, [((i + 1) % count, i) for i in range(ends)])  8.64 us
    all_to_all x1, starting transfers between devices, per_device(): lax.all_to_all(along_y, 'row', split_axis=2, concat_axis=1, tiled=True)  7.41 us
    unnamed x18, local copies, waits for them, and re-layouts  5.62 us
  transfers between devices with their start and end apart: 18, of which 8 were waited for; matrix products, arithmetic and copies ran while one was open for 3% of the time, Pallas kernels for 0%

commit v1 on v0

v1 whole, which is shorter than its diff:
```python
import functools

import jax
import jax.numpy as jnp
from jax import lax
from jax.experimental import pallas as pl
from jax.experimental.pallas import tpu as pltpu
from jax.sharding import PartitionSpec as P

M = 6
SBLK = 64
TBLK = 48
ITERS = 3
RIM = ITERS
ROWS = 56
LANES = 128
GROUPS = ROWS // 8
TAIL = LANES // GROUPS // 8 * 8
VMEM = 48 * 1024 * 1024
TINY = 1e-30
F32 = jnp.float32
EXACT = lax.Precision.HIGHEST


def tiles(cells):
    return -(-cells // LANES)


def overlap(src_lo, src_hi, tgt_lo, tgt_hi):
    shared = jnp.maximum(jnp.minimum(src_hi, tgt_hi) - jnp.maximum(src_lo, tgt_lo), 0.0)
    return shared / jnp.maximum(tgt_hi - tgt_lo, 1.0)


def window_rows(row_count):
    count = row_count // 2 - 1
    rows = [[2 * q + 1, 2 * q + 2] for q in range(count)]
    rows[0] = [0] + rows[0]
    rows[-1] = rows[-1] + [row_count - 1]
    return rows


def rezone_kernel(row_count, src_ref, tgt_ref, xedge_ref, frac_ref, field_ref, out_ref, along_ref):
    me = lax.axis_index("row")
    pairs = frac_ref.shape[0]
    cols = jnp.transpose(xedge_ref[:, LANES:])
    weight_x = overlap(
        xedge_ref[0:1, 0:SBLK], xedge_ref[1:2, 0:SBLK], cols[0:TBLK, 0:1], cols[0:TBLK, 1:2]
    )
    along_ref[pairs * TBLK :, :] = jnp.zeros_like(along_ref[pairs * TBLK :, :])
    for p in range(pairs):
        along_ref[p * TBLK : (p + 1) * TBLK, :] = jnp.dot(
            weight_x, frac_ref[p], precision=EXACT, preferred_element_type=F32
        )
    width = 4 * SBLK
    for q, rows in enumerate(window_rows(row_count)):
        span = pl.ds(2 * q * SBLK, width)
        parts = []
        for r in rows:
            edges = jnp.transpose(tgt_ref[:, r * LANES : (r + 1) * LANES])
            parts.append(
                overlap(
                    src_ref[0:1, span], src_ref[1:2, span], edges[0:ROWS, 0:1], edges[0:ROWS, 1:2]
                )
            )
        weight_y = jnp.concatenate(parts, axis=0)
        block = lax.dot_general(
            weight_y,
            along_ref[:, span],
            (((1,), (1,)), ((), ())),
            precision=EXACT,
            preferred_element_type=F32,
        )
        for n, r in enumerate(rows):
            mine = block[n * ROWS : (n + 1) * ROWS]
            out_ref[r, 0:ROWS, :] = mine[:, 0:LANES]
            packed = mine[0:8, LANES:]
            for g in range(1, GROUPS):
                packed = packed + pltpu.roll(mine[8 * g : 8 * g + 8, LANES:], TAIL * g, 1)
            out_ref[r, ROWS : ROWS + 8, :] = packed
    zlayers, height, breadth = field_ref.shape
    base = ROWS + 8
    for r in range(row_count):
        for t in range(tiles(breadth)):
            lo, hi = t * LANES, min((t + 1) * LANES, breadth)
            if hi - lo < LANES:
                out_ref[r, base + 8 * t : base + 8 * t + 8, :] = jnp.zeros((8, LANES), F32)
            for layer in range(zlayers):
                rim = jnp.where(
                    r > me,
                    field_ref[layer, height - RIM :, lo:hi],
                    field_ref[layer, :RIM, lo:hi],
                )
                at = base + 8 * t + RIM * layer
                out_ref[r, at : at + RIM, 0 : hi - lo] = rim


def regroup_kernel(row_count, col_count, got_ref, field_ref, out_ref, ext_ref):
    my_row, my_col = lax.axis_index("row"), lax.axis_index("col")
    zlayers, height, breadth = field_ref.shape
    pairs, width = out_ref.shape[1], out_ref.shape[3]
    per_col = row_count // col_count
    base = ROWS + 8
    ext_ref[...] = jnp.zeros_like(ext_ref)
    below, above = jnp.maximum(my_row - 1, 0), jnp.minimum(my_row + 1, row_count - 1)
    for layer in range(zlayers):
        ext_ref[layer, 0:height, 0:breadth] = field_ref[layer]
        for t in range(tiles(breadth)):
            lo, hi = t * LANES, min((t + 1) * LANES, breadth)
            at = base + 8 * t + RIM * layer
            after = got_ref[above, at : at + RIM, 0 : hi - lo]
            before = got_ref[below, at : at + RIM, 0 : hi - lo]
            ext_ref[layer, height : height + RIM, lo:hi] = jnp.where(
                my_row < row_count - 1, after, 0.0
            )
            ext_ref[layer, ROWS - RIM : ROWS, lo:hi] = jnp.where(my_row > 0, before, 0.0)

    def piece(block, pair, first, last):
        start = pair * TBLK
        lo, hi = start + first, start + last
        parts = []
        if lo < LANES:
            parts.append(got_ref[block, 0:ROWS, lo : min(hi, LANES)])
        if hi > LANES:
            a, b = max(lo, LANES) - LANES, hi - LANES
            tail = got_ref[block, ROWS : ROWS + 8, :]
            parts.append(
                jnp.concatenate([tail[:, TAIL * g + a : TAIL * g + b] for g in range(GROUPS)], axis=0)
            )
        return parts[0] if len(parts) == 1 else jnp.concatenate(parts, axis=1)

    for c in range(col_count):
        for p in range(pairs):
            parts = [piece(c * per_col + j, p, 0, TBLK) for j in range(per_col)]
            if c + 1 < col_count:
                parts.append(piece((c + 1) * per_col, p, 0, RIM))
            else:
                parts.append(jnp.zeros((ROWS, RIM), F32))
            if p < zlayers:
                whole = ext_ref[p]
                parts.append(
                    jnp.where(c > my_col, whole[:, breadth - RIM : breadth], whole[:, 0:RIM])
                )
            else:
                parts.append(jnp.zeros((ROWS, RIM), F32))
            parts.append(jnp.zeros((ROWS, width - breadth - 3 * RIM), F32))
            if c:
                parts.append(piece(c * per_col - 1, p, TBLK - RIM, TBLK))
            else:
                parts.append(jnp.zeros((ROWS, RIM), F32))
            out_ref[c, p] = jnp.concatenate(parts, axis=1)


def basis_kernel(
    col_count, height, breadth, table_ref, got_ref, ext_ref, shares_ref, basis_ref, sums_ref
):
    my_col = lax.axis_index("col")
    zlayers = ext_ref.shape[0]
    pairs, rows, width = got_ref.shape[1:]
    lane = lax.broadcasted_iota(jnp.int32, (rows, width), 1)
    before, after = jnp.maximum(my_col - 1, 0), jnp.minimum(my_col + 1, col_count - 1)

    def ahead(array, axis):
        return pltpu.roll(array, array.shape[axis] - 1, axis)

    def behind(array, axis):
        return pltpu.roll(array, 1, axis)

    def face(one, other):
        return 2.0 * one * other / jnp.maximum(one + other, TINY)

    cell_k, heat, field = [], [], []
    for z in range(zlayers):
        inverse = jnp.zeros((rows, width), F32)
        total = jnp.zeros((rows, width), F32)
        for m in range(M):
            c, p = divmod(z * M + m, pairs)
            share = got_ref[c, p]
            shares_ref[z * M + m] = share[0:height, 0:breadth]
            inside = jnp.where((lane < breadth + RIM) | (lane >= width - RIM), share, 0.0)
            inverse = inverse + inside * table_ref[m]
            total = total + inside * table_ref[M + m]
        cell_k.append(jnp.where(inverse > 0.0, 1.0 / jnp.where(inverse > 0.0, inverse, 1.0), 0.0))
        heat.append(total)
        left, right = got_ref[before, z], got_ref[after, z]
        left = pltpu.roll(left, width - (breadth + 2 * RIM), 1)
        right = pltpu.roll(right, width - RIM, 1)
        value = ext_ref[z]
        value = jnp.where(
            (lane >= breadth) & (lane < breadth + RIM) & (my_col < col_count - 1), right, value
        )
        value = jnp.where((lane >= width - RIM) & (my_col > 0), left, value)
        field.append(value)
    face_x = [face(k, ahead(k, 1)) for k in cell_k]
    face_y = [face(k, ahead(k, 0)) for k in cell_k]
    face_z = [face(cell_k[z], cell_k[z + 1]) for z in range(zlayers - 1)]

    def operate(w):
        result = []
        for z in range(zlayers):
            flow_x = face_x[z] * (w[z] - ahead(w[z], 1))
            flow_y = face_y[z] * (w[z] - ahead(w[z], 0))
            value = heat[z] * w[z] + (flow_x - behind(flow_x, 1)) + (flow_y - behind(flow_y, 0))
            if z + 1 < zlayers:
                value = value + face_z[z] * (w[z] - w[z + 1])
            if z:
                value = value - face_z[z - 1] * (w[z - 1] - w[z])
            result.append(value)
        return result

    shift, scale = table_ref[2 * M], table_ref[2 * M + 1]

    def shifted(w):
        return [(a - shift * b) * scale for a, b in zip(operate(w), w)]

    basis = [field, shifted(field)]
    for _ in range(ITERS - 1):
        basis.append([2.0 * a - b for a, b in zip(shifted(basis[-1]), basis[-2])])
    own = [
        [jnp.where(lane < breadth, layer, 0.0)[0:height] for layer in vector] for vector in basis
    ]
    for n in range(ITERS):
        for z in range(zlayers):
            basis_ref[n, z] = own[n + 1][z][:, 0:breadth]
    slot = lax.broadcasted_iota(jnp.int32, (1, LANES), 1)
    packed = jnp.zeros((1, LANES), F32)
    at = 0
    for a in range(ITERS + 1):
        for b in range(a, ITERS + 1):
            product = own[a][0] * own[b][0]
            for z in range(1, zlayers):
                product = product + own[a][z] * own[b][z]
            value = jnp.sum(product, axis=0, keepdims=True)
            value = jnp.sum(value, axis=1, keepdims=True)
            packed = packed + jnp.where(slot == at, value, 0.0)
            at += 1
    sums_ref[...] = jnp.broadcast_to(packed[None], sums_ref.shape)


def finish_kernel(table_ref, sums_ref, field_ref, basis_ref, iterate_ref, defect_ref):
    total = jnp.sum(sums_ref[...], axis=0)
    gram = {}
    at = 0
    for a in range(ITERS + 1):
        for b in range(a, ITERS + 1):
            gram[a, b] = gram[b, a] = total[:, at : at + 1]
            at += 1
    shift, scale = table_ref[2 * M], table_ref[2 * M + 2]

    def inner(left, right):
        value = None
        for a, one in left.items():
            for b, other in right.items():
                term = one * other * gram[a, b]
                value = term if value is None else value + term
        return value

    def combine(left, factor, right):
        result = dict(left)
        for a, one in right.items():
            result[a] = result[a] + factor * one if a in result else factor * one
        return result

    def apply(vector):
        result = {}
        for a, one in vector.items():
            if a:
                moved = {a - 1: 0.5 * scale * one, a: shift * one, a + 1: 0.5 * scale * one}
            else:
                moved = {0: shift * one, 1: scale * one}
            for b, other in moved.items():
                result[b] = result[b] + other if b in result else other
        return result

    one = jnp.ones((1, 1), F32)
    iterate, defect, direction = {}, {0: one}, {0: one}
    norm = gram[0, 0]
    for iteration in range(ITERS):
        applied = apply(direction)
        step = norm / inner(direction, applied)
        iterate = combine(iterate, step, direction)
        defect = combine(defect, -step, applied)
        if iteration + 1 < ITERS:
            following = inner(defect, defect)
            direction = combine(defect, following / norm, direction)
            norm = following
    for z in range(field_ref.shape[0]):
        vectors = [field_ref[z]] + [basis_ref[n, z] for n in range(ITERS)]
        iterate_ref[z] = sum(weight * vectors[a] for a, weight in iterate.items())
        defect_ref[z] = sum(weight * vectors[a] for a, weight in defect.items())


def per_device(
    row_count,
    col_count,
    fractions_source,
    x_source_edges,
    x_target_edges,
    y_source_edges,
    y_target_edges,
    conductivity_table,
    capacity,
    thermal_source_term,
):
    pairs, _, source_cells = fractions_source.shape
    zlayers, height, breadth = thermal_source_term.shape
    width = LANES * tiles(breadth + 4 * RIM)
    send_rows = ROWS + 8 + 8 * tiles(breadth)
    params = pltpu.CompilerParams(vmem_limit_bytes=VMEM)

    source = jnp.stack([y_source_edges[:-1], y_source_edges[1:]]).astype(F32)

    def by_block(edges):
        own = edges.reshape(row_count, TBLK)
        edge = jnp.zeros((1, RIM), edges.dtype)
        return jnp.concatenate(
            [
                own,
                jnp.concatenate([own[1:, :RIM], edge]),
                jnp.zeros((row_count, ROWS - TBLK - 2 * RIM), edges.dtype),
                jnp.concatenate([edge, own[:-1, TBLK - RIM :]]),
                jnp.zeros((row_count, LANES - ROWS), edges.dtype),
            ],
            axis=1,
        ).reshape(-1)

    target = jnp.stack([by_block(y_target_edges[:-1]), by_block(y_target_edges[1:])]).astype(F32)
    target = jnp.pad(target, ((0, 6), (0, 0)))
    me = lax.axis_index("row")
    x_source = lax.dynamic_slice(x_source_edges, (me * SBLK,), (SBLK + 1,))
    x_target = lax.dynamic_slice(x_target_edges, (me * TBLK,), (TBLK + 1,))
    x_edges = jnp.concatenate(
        [
            jnp.pad(jnp.stack([x_source[:-1], x_source[1:]]), ((0, 6), (0, LANES - SBLK))),
            jnp.pad(jnp.stack([x_target[:-1], x_target[1:]]), ((0, 6), (0, LANES - TBLK))),
        ],
        axis=1,
    ).astype(F32)
    resistance = 16.0 / conductivity_table.astype(F32)
    middle = 5.0 * M / jnp.sum(resistance)
    table = jnp.concatenate(
        [
            resistance,
            capacity,
            jnp.stack([jnp.mean(capacity) + middle, 1.0 / middle, middle]),
        ]
    )

    smem = pl.BlockSpec(memory_space=pltpu.SMEM)
    vmem = pl.BlockSpec(memory_space=pltpu.VMEM)
    along_rows = -(-pairs * TBLK // LANES) * LANES
    outgoing = pl.pallas_call(
        functools.partial(rezone_kernel, row_count),
        out_shape=jax.ShapeDtypeStruct((row_count, send_rows, LANES), F32),
        in_specs=[vmem] * 5,
        out_specs=vmem,
        scratch_shapes=[pltpu.VMEM((along_rows, source_cells), F32)],
        compiler_params=params,
        name="rezone",
    )(source, target, x_edges, fractions_source, thermal_source_term)
    arrived = lax.all_to_all(outgoing, "row", split_axis=0, concat_axis=0, tiled=True)
    regrouped, extended = pl.pallas_call(
        functools.partial(regroup_kernel, row_count, col_count),
        out_shape=[
            jax.ShapeDtypeStruct((col_count, pairs, ROWS, width), F32),
            jax.ShapeDtypeStruct((zlayers, ROWS, width), F32),
        ],
        in_specs=[vmem] * 2,
        out_specs=[vmem] * 2,
        compiler_params=params,
        name="regroup",
    )(arrived, thermal_source_term)
    gathered = lax.all_to_all(regrouped, "col", split_axis=0, concat_axis=0, tiled=True)
    rezoned_occupancy_shares, basis, sums = pl.pallas_call(
        functools.partial(basis_kernel, col_count, height, breadth),
        out_shape=[
            jax.ShapeDtypeStruct((zlayers * M, height, breadth), F32),
            jax.ShapeDtypeStruct((ITERS, zlayers, height, breadth), F32),
            jax.ShapeDtypeStruct((row_count * col_count, 1, LANES), F32),
        ],
        in_specs=[smem, vmem, vmem],
        out_specs=[vmem] * 3,
        compiler_params=params,
        name="basis",
    )(table, gathered, extended)
    sums = lax.all_to_all(sums, ("row", "col"), split_axis=0, concat_axis=0, tiled=True)
    thermal_iterate, remaining_defect = pl.pallas_call(
        finish_kernel,
        out_shape=[jax.ShapeDtypeStruct((zlayers, height, breadth), F32)] * 2,
        in_specs=[smem, vmem, vmem, vmem],
        out_specs=[vmem] * 2,
        compiler_params=params,
        name="finish",
    )(table, sums, thermal_source_term, basis)
    return rezoned_occupancy_shares, thermal_iterate, remaining_defect


def solution(mesh):
    placed = (P("col", "row", None), P(), P(), P(), P(), P(), P(), P(None, "row", "col"))
    return jax.shard_map(
        functools.partial(per_device, mesh.shape["row"], mesh.shape["col"]),
        mesh=mesh,
        in_specs=placed,
        out_specs=(P(None, "row", "col"), P(None, "row", "col"), P(None, "row", "col")),
        check_vma=False,
    )
```

time: 228 us -> 49 us (0.21)
  blocking collectives: 130 us -> 26.3 us
  starting transfers between devices: 46 us -> 3.59 us
  waiting for transfers between devices: 18.9 us -> 3.54 us
  between operations: 10.8 us -> 2.73 us
  Pallas kernels: 0 us -> 6.39 us
  local copies, waits for them, and re-layouts: 10.7 us -> 4.74 us
  other arithmetic: 6.74 us -> 1.26 us
  matrix products: 3.47 us -> 0 us
    psum x3 -> x0, blocking collectives: 130 us -> none  [two_products(): lax.psum((jnp.sum(remaining_defect * remaining_defect), jnp.sum(remaining...]
    ppermute x16 -> x0, starting transfers between devices: 35.1 us -> none  [the longest x8 24.8 us: extended(): lax.ppermute(tail, axis, [(i, (i + 1) % count) for i in range(ends)])]
    all_to_all x0 -> x2, blocking collectives: none -> 26.3 us  [the longest x1 17.4 us: per_device(): lax.all_to_all(outgoing, 'row', split_axis=0, concat_axis=0, tiled=True)]
    ppermute x16 -> x0, waiting for transfers between devices: 11.8 us -> none  [the longest x8 8.64 us: extended(): lax.ppermute(head, axis, [((i + 1) % count, i) for i in range(ends)])]
    all_to_all x2 -> x1, starting transfers between devices: 10.9 us -> 3.59 us  [per_device(): lax.all_to_all(regrouped, 'col', split_axis=0, concat_axis=0, tiled=True)]
    pallas_call x0 -> x4, Pallas kernels: none -> 6.39 us  [the longest x1 1.99 us: per_device(): pl.pallas_call(functools.partial(regroup_kernel, row_count, col_count), o...]
    all_to_all x2 -> x1, waiting for transfers between devices: 7.16 us -> 3.54 us  [per_device(): lax.all_to_all(regrouped, 'col', split_axis=0, concat_axis=0, tiled=True)]
    dot_general x2 -> x0, matrix products: 3.47 us -> none  [the longest x1 1.82 us: per_device(): jnp.einsum('psbu,bvu->psbv', source_grid, vertical_factor, precision=lax....]
  transfers between devices with their start and end apart: 18 -> 1, of which waited for: 8 -> 1; matrix products, arithmetic and copies ran while one was open for 3% -> 3% of each run, Pallas kernels for 0% -> 0%
where the time goes in v1:
time: 49 us; the launch traced here: 48.6 us
  blocking collectives  26.3 us (54%)
  Pallas kernels  6.39 us (13%)
  local copies, waits for them, and re-layouts  4.74 us (10%)
  starting transfers between devices  3.59 us (7%)
  waiting for transfers between devices  3.54 us (7%)
  between operations  2.73 us (6%)
  other arithmetic  1.26 us (3%)
    all_to_all x1, blocking collectives, per_device(): lax.all_to_all(outgoing, 'row', split_axis=0, concat_axis=0, tiled=True)  17.4 us
    all_to_all x1, blocking collectives, per_device(): lax.all_to_all(sums, ('row', 'col'), split_axis=0, concat_axis=0, tiled=T...  8.9 us
    all_to_all x1, starting transfers between devices, per_device(): lax.all_to_all(regrouped, 'col', split_axis=0, concat_axis=0, tiled=True)  3.59 us
    all_to_all x1, waiting for transfers between devices, per_device(): lax.all_to_all(regrouped, 'col', split_axis=0, concat_axis=0, tiled=True)  3.54 us
    unnamed x12, local copies, waits for them, and re-layouts  2.35 us
    pallas_call x1, Pallas kernels, per_device(): pl.pallas_call(functools.partial(regroup_kernel, row_count, col_count), o...  1.99 us
    pallas_call x1, Pallas kernels, per_device(): pl.pallas_call(functools.partial(basis_kernel, col_count, height, breadth...  1.8 us
    pallas_call x1, Pallas kernels, per_device(): pl.pallas_call(finish_kernel, out_shape=[jax.ShapeDtypeStruct((zlayers, h...  1.4 us
  transfers between devices with their start and end apart: 1, of which 1 were waited for; matrix products, arithmetic and copies ran while one was open for 3% of the time, Pallas kernels for 0%

profile of v1, /device:TPU:0, one launch (start us, length us, event | category | flops | bytes accessed | tf_op | source)
XLA Modules:
  0.0 48.6 jit_solution(16699154966885790221)
XLA Ops:
  0.6 0.8 %dynamic_slice.6 = s32[65]{0:T(128)S(1)} dynamic-slice(s32[513]{0:T(1024)} %param.9, s32[]{:T(128)S(6)} %select_n.6), dynamic_slice_sizes={65} | dynamic-slice | bytes 524 | tf_op jit(solution)/shard_map/dynamic_slice | solution.py:329
  1.4 0.0 copy-start.3
  1.4 0.1 slice_bitcast_fusion.3
  1.5 0.8 %dynamic_slice.7 = s32[49]{0:T(128)S(1)} dynamic-slice(s32[385]{0:T(512)} %param.10, s32[]{:T(128)S(6)} %select_n.7), dynamic_slice_sizes={49} | dynamic-slice | bytes 396 | tf_op jit(solution)/shard_map/dynamic_slice | solution.py:330
  2.2 0.1 slice_bitcast_fusion.1
  2.3 0.0 copy-done.3
  2.3 0.0 copy-start.2
  2.3 0.1 fusion.4
  2.4 0.6 %copy-done.2 = s32[385]{0:T(512)S(1)} copy-done((s32[385]{0:T(512)S(1)}, s32[385]{0:T(512)}, u32[]{:S(2)}) %copy-start.2) | copy-done | bytes 1564
  3.0 0.1 fusion.5
  3.1 0.1 reshape.12
  3.1 0.1 reshape.13
  3.2 0.1 fusion.3
  3.3 0.1 fusion.2
  3.5 0.1 concatenate.30
  3.6 0.0 copy-start
  3.6 0.1 concatenate.27
  3.7 0.7 %copy-done = f32[2,48,96]{2,1,0:T(8,128)S(1)} copy-done((f32[2,48,96]{2,1,0:T(8,128)S(1)}, f32[2,48,96]{2,1,0:T(8,128)}, u32[]{:S(2)}) %copy-start) | copy-done | bytes 36888
  4.4 0.0 copy-start.1
  4.4 1.0 %copy-done.1 = f32[3,64,512]{2,1,0:T(8,128)S(1)} copy-done((f32[3,64,512]{2,1,0:T(8,128)S(1)}, f32[3,64,512]{2,1,0:T(8,128)}, u32[]{:S(2)}) %copy-start.1) | copy-done | bytes 393240
  5.4 1.2 %rezone.1 = f32[8,72,128]{2,1,0:T(8,128)S(1)} custom-call(f32[2,512]{1,0:T(2,128)S(1)} %add_convert_fusion.1.src_ref, f32[8,1024]{1,0:T(8,128)S(1)} %pad.16.tgt_ref, f32[8,256]{1,0:T(8,128)S(1)} %fusion.xedge_ref, f32[3,64,512]{2,1,0:T(8,128)S(1)} %copy-done.1, f32[2,48,96]{2,1,0:T(8,128)S(1)} %copy-done), custom_call_target="tpu_custom_call" | custom-call | tf_op jit(solution)/shard_map/rezone/pallas_call | solution.py:351
  6.6 17.4 %all_to_all.15.got_ref = f32[8,72,128]{2,1,0:T(8,128)S(1)} all-to-all(f32[8,72,128]{2,1,0:T(8,128)S(1)} %rezone.1), channel_id=1, replica_groups=mesh['row'=8,'col'=4] {'row'}, dimensions={0} | all-to-all | bytes 589824 | tf_op jit(solution)/shard_map/all_to_all | solution.py:360
  24.0 2.0 %regroup.1 = (f32[4,3,56,128]{3,2,1,0:T(8,128)}, f32[2,56,128]{2,1,0:T(8,128)S(1)}) custom-call(f32[8,72,128]{2,1,0:T(8,128)S(1)} %all_to_all.15.got_ref, f32[2,48,96]{2,1,0:T(8,128)S(1)} %copy-done), custom_call_target="tpu_custom_call" | custom-call | tf_op jit(solution)/shard_map/regroup/pallas_call | solution.py:361
  26.0 0.0 copy-start.4
  26.0 3.6 %all-to-all-start.1 = ((f32[4,3,56,128]{3,2,1,0:T(8,128)}), f32[4,3,56,128]{3,2,1,0:T(8,128)S(1)}, u32[]{:S(2)}, u32[]{:S(2)}) async-start(f32[4,3,56,128]{3,2,1,0:T(8,128)} %get-tuple-element.10), calls=%async_computation.1 | async-start | bytes 688128 | tf_op jit(solution)/shard_map/all_to_all | solution.py:372
  29.6 0.0 copy-done.4
  29.6 0.0 copy-start.5
  29.6 0.6 %reduce_sum.18 = f32[]{:T(128)} reduce(f32[6]{0:T(128)S(1)} %copy-done.4, f32[]{:T(128)} %constant.13.clone.1), dimensions={0}, to_apply=%region_0.1 | reduce | flops 5 | bytes 32 | tf_op jit(solution)/shard_map/reduce_sum | solution.py:344
  30.2 0.0 copy-done.5
  30.2 0.6 %fusion.1 = (f32[]{:T(128)}, f32[6]{0:T(128)S(1)}) fusion(s32[6]{0:T(128)S(1)} %copy-done.5), kind=kLoop, calls=%fused_computation.11 | loop fusion | flops 17 | bytes 52 | tf_op jit(solution)/shard_map/reduce_sum | solution.py:339
  32.8 0.1 concatenate.24.table_ref
  32.9 3.5 %all-to-all-done.1.got_ref = f32[4,3,56,128]{3,2,1,0:T(8,128)S(1)} async-done(((f32[4,3,56,128]{3,2,1,0:T(8,128)}), f32[4,3,56,128]{3,2,1,0:T(8,128)S(1)}, u32[]{:S(2)}, u32[]{:S(2)}) %all-to-all-start.1) | async-done | bytes 344096 | tf_op jit(solution)/shard_map/all_to_all | solution.py:372
  36.5 1.8 %basis.1 = (f32[12,48,96]{2,1,0:T(8,128)}, f32[3,2,48,96]{3,2,1,0:T(8,128)S(1)}, f32[32,1,128]{2,1,0:T(1,128)S(1)}) custom-call(f32[15]{0:T(128)S(1)} %concatenate.24.table_ref, f32[4,3,56,128]{3,2,1,0:T(8,128)S(1)} %all-to-all-done.1.got_ref, f32[2,56,128]{2,1,0:T(8,128)S(1)} %get-tuple-element.11.ext_ref), custom_call_target="tpu_custom_call" | custom-call | tf_op jit(solution)/shard_map/basis/pallas_call | solution.py:373
  38.2 8.9 %all_to_all.16.sums_ref = f32[32,1,128]{2,1,0:T(1,128)S(1)} all-to-all(f32[32,1,128]{2,1,0:T(1,128)S(1)} %get-tuple-element.13), channel_id=1, replica_groups=mesh['row'=8,'col'=4] {'row','col'}, dimensions={0} | all-to-all | bytes 32768 | tf_op jit(solution)/shard_map/all_to_all | solution.py:385
  47.2 1.4 %finish.1 = (f32[2,48,96]{2,1,0:T(8,128)}, f32[2,48,96]{2,1,0:T(8,128)}) custom-call(f32[15]{0:T(128)S(1)} %concatenate.24.table_ref, f32[32,1,128]{2,1,0:T(1,128)S(1)} %all_to_all.16.sums_ref, f32[2,48,96]{2,1,0:T(8,128)S(1)} %copy-done, f32[3,2,48,96]{3,2,1,0:T(8,128)S(1)} %get-tuple-element.14.basis_ref), custom_call_target="tpu_custom_call" | custom-call | tf_op jit(solution)/shard_map/finish/pallas_call | solution.py:386
  (12 shorter events, 0.1 us)
Async XLA Ops:
  1.4 0.9 %copy-start.3 = (s32[513]{0:T(1024)S(1)}, s32[513]{0:T(1024)}, u32[]{:S(2)}) copy-start(s32[513]{0:T(1024)} %param.11) | copy-start | bytes 6160
  2.3 0.7 %copy-start.2 = (s32[385]{0:T(512)S(1)}, s32[385]{0:T(512)}, u32[]{:S(2)}) copy-start(s32[385]{0:T(512)} %param.12) | copy-start | bytes 4624
  3.6 0.8 %copy-start = (f32[2,48,96]{2,1,0:T(8,128)S(1)}, f32[2,48,96]{2,1,0:T(8,128)}, u32[]{:S(2)}) copy-start(f32[2,48,96]{2,1,0:T(8,128)} %field_ref.5) | copy-start | bytes 110596
  4.4 1.0 %copy-start.1 = (f32[3,64,512]{2,1,0:T(8,128)S(1)}, f32[3,64,512]{2,1,0:T(8,128)}, u32[]{:S(2)}) copy-start(f32[3,64,512]{2,1,0:T(8,128)} %frac_ref.1) | copy-start | bytes 1179652
  26.0 3.6 %copy-start.4 = (f32[6]{0:T(128)S(1)}, f32[6]{0:T(128)}, u32[]{:S(2)}) copy-start(f32[6]{0:T(128)} %param.14) | copy-start | bytes 76
  26.0 10.5 %all-to-all-start.1 = ((f32[4,3,56,128]{3,2,1,0:T(8,128)}), f32[4,3,56,128]{3,2,1,0:T(8,128)S(1)}, u32[]{:S(2)}, u32[]{:S(2)}) async-start(f32[4,3,56,128]{3,2,1,0:T(8,128)} %get-tuple-element.10), calls=%async_computation.1 | async-start | bytes 688128 | tf_op jit(solution)/shard_map/all_to_all | solution.py:372
  29.6 0.7 %copy-start.5 = (s32[6]{0:T(128)S(1)}, s32[6]{0:T(128)}, u32[]{:S(2)}) copy-start(s32[6]{0:T(128)} %param.13) | copy-start | bytes 76

commit v2 on v1

--- a/solution.py
+++ b/solution.py
@@ -17,6 +17,7 @@
 GROUPS = ROWS // 8
 TAIL = LANES // GROUPS // 8 * 8
 VMEM = 48 * 1024 * 1024
+FULL = 63 * 1024 * 1024
 TINY = 1e-30
 F32 = jnp.float32
 EXACT = lax.Precision.HIGHEST
@@ -39,33 +40,113 @@
     return rows
 
 
-def rezone_kernel(row_count, src_ref, tgt_ref, xedge_ref, frac_ref, field_ref, out_ref, along_ref):
+def rezone_kernel(
+    row_count,
+    xs_hbm,
+    xt_hbm,
+    ys_hbm,
+    yt_hbm,
+    frac_hbm,
+    field_hbm,
+    out_ref,
+    xs_ref,
+    xt_ref,
+    ys_ref,
+    yt_ref,
+    frac_ref,
+    field_ref,
+    edges_ref,
+    along_ref,
+    sems,
+):
     me = lax.axis_index("row")
     pairs = frac_ref.shape[0]
-    cols = jnp.transpose(xedge_ref[:, LANES:])
+    moves = [
+        pltpu.make_async_copy(here, there, sems.at[n])
+        for n, (here, there) in enumerate(
+            (
+                (xs_hbm, xs_ref),
+                (xt_hbm, xt_ref),
+                (ys_hbm, ys_ref),
+                (yt_hbm, yt_ref),
+                (field_hbm, field_ref),
+            )
+        )
+    ]
+    loads = [
+        pltpu.make_async_copy(frac_hbm.at[p], frac_ref.at[p], sems.at[len(moves) + p])
+        for p in range(pairs)
+    ]
+    for move in moves + loads:
+        move.start()
+    edges_ref[...] = jnp.zeros_like(edges_ref)
+    along_ref[pairs * TBLK :, :] = jnp.zeros_like(along_ref[pairs * TBLK :, :])
+    for n, ref in enumerate((xs_ref, xt_ref, ys_ref, yt_ref)):
+        moves[n].wait()
+        edges_ref[n : n + 1, 0 : ref.shape[0]] = ref[...].astype(F32)[None, :]
+
+    def from_here(row, start, lane):
+        base = start // LANES * LANES
+        if not isinstance(base, int):
+            base = pl.multiple_of(base, LANES)
+        window = edges_ref[row : row + 1, pl.ds(base, 2 * LANES)]
+        return pltpu.roll(window, (lane - (start - base) + 2 * LANES) % (2 * LANES), 1)
+
+    def following(turned):
+        return pltpu.roll(turned, 2 * LANES - 1, 1)
+
+    x_lo = from_here(0, me * SBLK, 0)
+    x_hi = following(x_lo)
+    mine = from_here(1, me * TBLK, 0)
+    lane = lax.broadcasted_iota(jnp.int32, (1, LANES), 1)
+    lows, highs = [mine[:, 0:LANES]], [following(mine)[:, 0:LANES]]
+    for r in range(row_count):
+        own = from_here(3, r * TBLK, 0)
+        upper = TBLK if r + 1 == row_count else TBLK + RIM
+        if r:
+            rim = from_here(3, r * TBLK - RIM, ROWS - RIM)
+            rims = rim, following(rim)
+        else:
+            rims = (jnp.zeros((1, 2 * LANES), F32),) * 2
+        for rows, value, edge in ((lows, own, rims[0]), (highs, following(own), rims[1])):
+            value = jnp.where(lane < upper, value[:, 0:LANES], 0.0)
+            inside = (lane >= ROWS - RIM) & (lane < ROWS)
+            rows.append(jnp.where(inside, edge[:, 0:LANES], value))
+    count = row_count + 1
+    spare = jnp.zeros((-2 * count % 8, LANES), F32)
+    columns = jnp.transpose(jnp.concatenate(lows + highs + [spare], axis=0))
+
     weight_x = overlap(
-        xedge_ref[0:1, 0:SBLK], xedge_ref[1:2, 0:SBLK], cols[0:TBLK, 0:1], cols[0:TBLK, 1:2]
+        x_lo[:, 0:SBLK], x_hi[:, 0:SBLK], columns[0:TBLK, 0:1], columns[0:TBLK, count : count + 1]
     )
-    along_ref[pairs * TBLK :, :] = jnp.zeros_like(along_ref[pairs * TBLK :, :])
+    width = 4 * SBLK
+    weights_y = []
+    for q, rows in enumerate(window_rows(row_count)):
+        src_lo = edges_ref[2:3, 2 * q * SBLK : 2 * q * SBLK + width]
+        src_hi = edges_ref[2:3, 2 * q * SBLK + 1 : 2 * q * SBLK + width + 1]
+        weights_y.append(
+            jnp.concatenate(
+                [
+                    overlap(
+                        src_lo,
+                        src_hi,
+                        columns[0:ROWS, 1 + r : 2 + r],
+                        columns[0:ROWS, count + 1 + r : count + 2 + r],
+                    )
+                    for r in rows
+                ],
+                axis=0,
+            )
+        )
     for p in range(pairs):
+        loads[p].wait()
         along_ref[p * TBLK : (p + 1) * TBLK, :] = jnp.dot(
             weight_x, frac_ref[p], precision=EXACT, preferred_element_type=F32
         )
-    width = 4 * SBLK
     for q, rows in enumerate(window_rows(row_count)):
-        span = pl.ds(2 * q * SBLK, width)
-        parts = []
-        for r in rows:
-            edges = jnp.transpose(tgt_ref[:, r * LANES : (r + 1) * LANES])
-            parts.append(
-                overlap(
-                    src_ref[0:1, span], src_ref[1:2, span], edges[0:ROWS, 0:1], edges[0:ROWS, 1:2]
-                )
-            )
-        weight_y = jnp.concatenate(parts, axis=0)
         block = lax.dot_general(
-            weight_y,
-            along_ref[:, span],
+            weights_y[q],
+            along_ref[:, 2 * q * SBLK : 2 * q * SBLK + width],
             (((1,), (1,)), ((), ())),
             precision=EXACT,
             preferred_element_type=F32,
@@ -77,13 +158,12 @@
             for g in range(1, GROUPS):
                 packed = packed + pltpu.roll(mine[8 * g : 8 * g + 8, LANES:], TAIL * g, 1)
             out_ref[r, ROWS : ROWS + 8, :] = packed
+    moves[4].wait()
     zlayers, height, breadth = field_ref.shape
     base = ROWS + 8
     for r in range(row_count):
         for t in range(tiles(breadth)):
             lo, hi = t * LANES, min((t + 1) * LANES, breadth)
-            if hi - lo < LANES:
-                out_ref[r, base + 8 * t : base + 8 * t + 8, :] = jnp.zeros((8, LANES), F32)
             for layer in range(zlayers):
                 rim = jnp.where(
                     r > me,
@@ -94,10 +174,10 @@
                 out_ref[r, at : at + RIM, 0 : hi - lo] = rim
 
 
-def regroup_kernel(row_count, col_count, got_ref, field_ref, out_ref, ext_ref):
+def regroup_kernel(row_count, col_count, got_ref, field_ref, ext_ref, *out_refs):
     my_row, my_col = lax.axis_index("row"), lax.axis_index("col")
     zlayers, height, breadth = field_ref.shape
-    pairs, width = out_ref.shape[1], out_ref.shape[3]
+    pairs, _, width = out_refs[0].shape
     per_col = row_count // col_count
     base = ROWS + 8
     ext_ref[...] = jnp.zeros_like(ext_ref)
@@ -128,14 +208,14 @@
             )
         return parts[0] if len(parts) == 1 else jnp.concatenate(parts, axis=1)
 
-    for c in range(col_count):
+    for mask, out_ref in enumerate(out_refs):
+        c = my_col ^ mask
+        first = c * per_col
+        left, right = jnp.maximum(first - 1, 0), jnp.minimum(first + per_col, row_count - 1)
         for p in range(pairs):
-            parts = [piece(c * per_col + j, p, 0, TBLK) for j in range(per_col)]
-            if c + 1 < col_count:
-                parts.append(piece((c + 1) * per_col, p, 0, RIM))
-            else:
-                parts.append(jnp.zeros((ROWS, RIM), F32))
-            if p < zlayers:
+            parts = [piece(first + j, p, 0, TBLK) for j in range(per_col)]
+            parts.append(jnp.where(c < col_count - 1, piece(right, p, 0, RIM), 0.0))
+            if p < zlayers and mask:
                 whole = ext_ref[p]
                 parts.append(
                     jnp.where(c > my_col, whole[:, breadth - RIM : breadth], whole[:, 0:RIM])
@@ -143,17 +223,15 @@
             else:
                 parts.append(jnp.zeros((ROWS, RIM), F32))
             parts.append(jnp.zeros((ROWS, width - breadth - 3 * RIM), F32))
-            if c:
-                parts.append(piece(c * per_col - 1, p, TBLK - RIM, TBLK))
-            else:
-                parts.append(jnp.zeros((ROWS, RIM), F32))
-            out_ref[c, p] = jnp.concatenate(parts, axis=1)
-
-
-def basis_kernel(
-    col_count, height, breadth, table_ref, got_ref, ext_ref, shares_ref, basis_ref, sums_ref
-):
+            parts.append(jnp.where(c > 0, piece(left, p, TBLK - RIM, TBLK), 0.0))
+            out_ref[p] = jnp.concatenate(parts, axis=1)
+
+
+def basis_kernel(col_count, height, breadth, table_ref, ext_ref, *refs):
+    arrivals, (shares_ref, basis_ref, sums_ref, got_ref) = refs[:col_count], refs[col_count:]
     my_col = lax.axis_index("col")
+    for mask, arrival in enumerate(arrivals):
+        got_ref[my_col ^ mask] = arrival[...]
     zlayers = ext_ref.shape[0]
     pairs, rows, width = got_ref.shape[1:]
     lane = lax.broadcasted_iota(jnp.int32, (rows, width), 1)
@@ -307,34 +385,6 @@
     send_rows = ROWS + 8 + 8 * tiles(breadth)
     params = pltpu.CompilerParams(vmem_limit_bytes=VMEM)
 
-    source = jnp.stack([y_source_edges[:-1], y_source_edges[1:]]).astype(F32)
-
-    def by_block(edges):
-        own = edges.reshape(row_count, TBLK)
-        edge = jnp.zeros((1, RIM), edges.dtype)
-        return jnp.concatenate(
-            [
-                own,
-                jnp.concatenate([own[1:, :RIM], edge]),
-                jnp.zeros((row_count, ROWS - TBLK - 2 * RIM), edges.dtype),
-                jnp.concatenate([edge, own[:-1, TBLK - RIM :]]),
-                jnp.zeros((row_count, LANES - ROWS), edges.dtype),
-            ],
-            axis=1,
-        ).reshape(-1)
-
-    target = jnp.stack([by_block(y_target_edges[:-1]), by_block(y_target_edges[1:])]).astype(F32)
-    target = jnp.pad(target, ((0, 6), (0, 0)))
-    me = lax.axis_index("row")
-    x_source = lax.dynamic_slice(x_source_edges, (me * SBLK,), (SBLK + 1,))
-    x_target = lax.dynamic_slice(x_target_edges, (me * TBLK,), (TBLK + 1,))
-    x_edges = jnp.concatenate(
-        [
-            jnp.pad(jnp.stack([x_source[:-1], x_source[1:]]), ((0, 6), (0, LANES - SBLK))),
-            jnp.pad(jnp.stack([x_target[:-1], x_target[1:]]), ((0, 6), (0, LANES - TBLK))),
-        ],
-        axis=1,
-    ).astype(F32)
     resistance = 16.0 / conductivity_table.astype(F32)
     middle = 5.0 * M / jnp.sum(resistance)
     table = jnp.concatenate(
@@ -347,29 +397,39 @@
 
     smem = pl.BlockSpec(memory_space=pltpu.SMEM)
     vmem = pl.BlockSpec(memory_space=pltpu.VMEM)
+    hbm = pl.BlockSpec(memory_space=pltpu.HBM)
     along_rows = -(-pairs * TBLK // LANES) * LANES
+    edges = [x_source_edges, x_target_edges, y_source_edges, y_target_edges]
     outgoing = pl.pallas_call(
         functools.partial(rezone_kernel, row_count),
         out_shape=jax.ShapeDtypeStruct((row_count, send_rows, LANES), F32),
-        in_specs=[vmem] * 5,
+        in_specs=[hbm] * 6,
         out_specs=vmem,
-        scratch_shapes=[pltpu.VMEM((along_rows, source_cells), F32)],
-        compiler_params=params,
+        scratch_shapes=[pltpu.VMEM(e.shape, e.dtype) for e in edges]
+        + [
+            pltpu.VMEM(fractions_source.shape, F32),
+            pltpu.VMEM(thermal_source_term.shape, F32),
+            pltpu.VMEM((8, LANES * (tiles(source_cells + 1) + 1)), F32),
+            pltpu.VMEM((along_rows, source_cells), F32),
+            pltpu.SemaphoreType.DMA((5 + pairs,)),
+        ],
+        compiler_params=pltpu.CompilerParams(vmem_limit_bytes=FULL),
         name="rezone",
-    )(source, target, x_edges, fractions_source, thermal_source_term)
+    )(*edges, fractions_source, thermal_source_term)
     arrived = lax.all_to_all(outgoing, "row", split_axis=0, concat_axis=0, tiled=True)
-    regrouped, extended = pl.pallas_call(
+    message = jax.ShapeDtypeStruct((pairs, ROWS, width), F32)
+    extended, *parts = pl.pallas_call(
         functools.partial(regroup_kernel, row_count, col_count),
-        out_shape=[
-            jax.ShapeDtypeStruct((col_count, pairs, ROWS, width), F32),
-            jax.ShapeDtypeStruct((zlayers, ROWS, width), F32),
-        ],
+        out_shape=[jax.ShapeDtypeStruct((zlayers, ROWS, width), F32)] + [message] * col_count,
         in_specs=[vmem] * 2,
-        out_specs=[vmem] * 2,
+        out_specs=[vmem] * (1 + col_count),
         compiler_params=params,
         name="regroup",
     )(arrived, thermal_source_term)
-    gathered = lax.all_to_all(regrouped, "col", split_axis=0, concat_axis=0, tiled=True)
+    parts = [parts[0]] + [
+        lax.ppermute(parts[mask], "col", [(c, c ^ mask) for c in range(col_count)])
+        for mask in range(1, col_count)
+    ]
     rezoned_occupancy_shares, basis, sums = pl.pallas_call(
         functools.partial(basis_kernel, col_count, height, breadth),
         out_shape=[
@@ -377,11 +437,12 @@
             jax.ShapeDtypeStruct((ITERS, zlayers, height, breadth), F32),
             jax.ShapeDtypeStruct((row_count * col_count, 1, LANES), F32),
         ],
-        in_specs=[smem, vmem, vmem],
+        in_specs=[smem] + [vmem] * (1 + col_count),
         out_specs=[vmem] * 3,
+        scratch_shapes=[pltpu.VMEM((col_count, *message.shape), F32)],
         compiler_params=params,
         name="basis",
-    )(table, gathered, extended)
+    )(table, extended, *parts)
     sums = lax.all_to_all(sums, ("row", "col"), split_axis=0, concat_axis=0, tiled=True)
     thermal_iterate, remaining_defect = pl.pallas_call(
         finish_kernel,

time: 49 us -> 43.3 us (0.88)
  local copies, waits for them, and re-layouts: 4.74 us -> 0.11 us
  waiting for transfers between devices: 3.54 us -> 1.18 us
  Pallas kernels: 6.39 us -> 8.29 us
  starting transfers between devices: 3.59 us -> 1.92 us
  blocking collectives: 26.3 us -> 27.5 us
    all_to_all x1 -> x0, starting transfers between devices: 3.59 us -> none  [per_device(): lax.all_to_all(regrouped, 'col', split_axis=0, concat_axis=0, tiled=True)]
    all_to_all x1 -> x0, waiting for transfers between devices: 3.54 us -> none  [per_device(): lax.all_to_all(regrouped, 'col', split_axis=0, concat_axis=0, tiled=True)]
    pallas_call x1, Pallas kernels: 1.2 us -> 3.78 us  [per_device(): pl.pallas_call(functools.partial(rezone_kernel, row_count), out_shape=jax...]
    unnamed x12 -> x6, local copies, waits for them, and re-layouts: 2.35 us -> 0.02 us
    ppermute x0 -> x3, starting transfers between devices: none -> 1.92 us  [per_device(): lax.ppermute(parts[mask], 'col', [(c, c ^ mask) for c in range(col_count)])]
    dynamic_slice x2 -> x0, local copies, waits for them, and re-layouts: 1.52 us -> none  [the longest x1 0.76 us: per_device(): x_source = lax.dynamic_slice(x_source_edges, (me * SBLK,), (SBLK + 1,))]
    ppermute x0 -> x3, waiting for transfers between devices: none -> 1.18 us  [per_device(): lax.ppermute(parts[mask], 'col', [(c, c ^ mask) for c in range(col_count)])]
    all_to_all x1, blocking collectives: 8.9 us -> 9.77 us  [per_device(): lax.all_to_all(sums, ('row', 'col'), split_axis=0, concat_axis=0, tiled=T...]
  transfers between devices with their start and end apart: 1 -> 3, of which waited for: 1 -> 2; matrix products, arithmetic and copies ran while one was open for 3% -> 3% of each run, Pallas kernels for 0% -> 0%
where the time goes in v2:
time: 43.3 us; the launch traced here: 42.9 us
  blocking collectives  27.5 us (64%)
  Pallas kernels  8.29 us (19%)
  between operations  2.7 us (6%)
  starting transfers between devices  1.92 us (4%)
  other arithmetic  1.21 us (3%)
  waiting for transfers between devices  1.18 us (3%)
    all_to_all x1, blocking collectives, per_device(): lax.all_to_all(outgoing, 'row', split_axis=0, concat_axis=0, tiled=True)  17.8 us
    all_to_all x1, blocking collectives, per_device(): lax.all_to_all(sums, ('row', 'col'), split_axis=0, concat_axis=0, tiled=T...  9.77 us
    pallas_call x1, Pallas kernels, per_device(): pl.pallas_call(functools.partial(rezone_kernel, row_count), out_shape=jax...  3.78 us
    ppermute x3, starting transfers between devices, per_device(): lax.ppermute(parts[mask], 'col', [(c, c ^ mask) for c in range(col_count)])  1.92 us
    pallas_call x1, Pallas kernels, per_device(): pl.pallas_call(functools.partial(basis_kernel, col_count, height, breadth...  1.82 us
    pallas_call x1, Pallas kernels, per_device(): pl.pallas_call(finish_kernel, out_shape=[jax.ShapeDtypeStruct((zlayers, h...  1.4 us
    pallas_call x1, Pallas kernels, per_device(): pl.pallas_call(functools.partial(regroup_kernel, row_count, col_count), o...  1.29 us
    ppermute x3, waiting for transfers between devices, per_device(): lax.ppermute(parts[mask], 'col', [(c, c ^ mask) for c in range(col_count)])  1.18 us
  transfers between devices with their start and end apart: 3, of which 2 were waited for; matrix products, arithmetic and copies ran while one was open for 3% of the time, Pallas kernels for 0%

profile of v2, /device:TPU:0, one launch (start us, length us, event | category | flops | bytes accessed | tf_op | source)
XLA Modules:
  0.0 42.9 jit_solution(10827251562195579063)
XLA Ops:
  0.6 3.8 %rezone.1 = f32[8,72,128]{2,1,0:T(8,128)} custom-call(s32[513]{0:T(1024)} %xs_hbm.1, s32[385]{0:T(512)} %xt_hbm.1, s32[513]{0:T(1024)} %ys_hbm.1, s32[385]{0:T(512)} %yt_hbm.1, f32[3,64,512]{2,1,0:T(8,128)} %frac_hbm.1, f32[2,48,96]{2,1,0:T(8,128)} %field_ref.3), custom_call_target="tpu_custom_call" | custom-call | tf_op jit(solution)/shard_map/rezone/pallas_call | solution.py:403
  4.4 0.0 copy-start
  4.4 17.8 %all_to_all.10.got_ref = f32[8,72,128]{2,1,0:T(8,128)S(1)} all-to-all(f32[8,72,128]{2,1,0:T(8,128)} %rezone.1), channel_id=1, replica_groups=mesh['row'=8,'col'=4] {'row'}, dimensions={0} | all-to-all | bytes 589824 | tf_op jit(solution)/shard_map/all_to_all | solution.py:419
  22.2 0.0 copy-done
  22.2 1.3 %regroup.1 = (f32[2,56,128]{2,1,0:T(8,128)S(1)}, f32[3,56,128]{2,1,0:T(8,128)S(1)}, f32[3,56,128]{2,1,0:T(8,128)S(1)}, f32[3,56,128]{2,1,0:T(8,128)S(1)}, f32[3,56,128]{2,1,0:T(8,128)S(1)}) custom-call(f32[8,72,128]{2,1,0:T(8,128)S(1)} %all_to_all.10.got_ref, f32[2,48,96]{2,1,0:T(8,128)S(1)} %copy-done), custom_call_target="tpu_custom_call" | custom-call | tf_op jit(solution)/shard_map/regroup/pallas_call | solution.py:421
  23.5 0.1 collective-permute-start
  23.6 0.0 copy-start.2
  23.6 1.6 %collective-permute-start.1 = (f32[3,56,128]{2,1,0:T(8,128)S(1)}, f32[3,56,128]{2,1,0:T(8,128)S(1)}, u32[]{:S(2)}, u32[]{:S(2)}) collective-permute-start(f32[3,56,128]{2,1,0:T(8,128)S(1)} %get-tuple-element.16), channel_id=1, source_target_pairs={{0,2},{1,3},{2,0},{3,1},{4,6},{5,7},{6,4},{7,5},{8,10},{9,11},{10,... | collective-permute-start | bytes 258056 | tf_op jit(solution)/shard_map/ppermute | solution.py:430
  25.1 0.3 collective-permute-start.2
  25.4 0.0 copy-done.2
  25.4 0.6 %fusion = (f32[]{:T(128)}, f32[6]{0:T(128)S(1)}) fusion(s32[6]{0:T(128)S(1)} %copy-done.2), kind=kLoop, calls=%fused_computation.1 | loop fusion | flops 17 | bytes 52 | tf_op jit(solution)/shard_map/reduce_sum | solution.py:389
  26.7 0.0 copy-start.1
  27.4 0.0 copy-done.1
  27.4 0.6 %reduce_sum.18 = f32[]{:T(128)} reduce(f32[6]{0:T(128)S(1)} %copy-done.1, f32[]{:T(128)} %constant.3.clone.1), dimensions={0}, to_apply=%region_0.0 | reduce | flops 5 | bytes 32 | tf_op jit(solution)/shard_map/reduce_sum | solution.py:394
  28.7 0.1 concatenate.3.table_ref
  28.8 0.0 collective-permute-done.refs_1_
  28.8 0.2 collective-permute-done.1.refs_2_
  28.9 1.0 %collective-permute-done.2.refs_3_ = f32[3,56,128]{2,1,0:T(8,128)S(1)} collective-permute-done((f32[3,56,128]{2,1,0:T(8,128)S(1)}, f32[3,56,128]{2,1,0:T(8,128)S(1)}, u32[]{:S(2)}, u32[]{:S(2)}) %collective-permute-start.2) | collective-permute-done | bytes 86048 | tf_op jit(solution)/shard_map/ppermute | solution.py:430
  29.9 1.8 %basis.1 = (f32[12,48,96]{2,1,0:T(8,128)}, f32[3,2,48,96]{3,2,1,0:T(8,128)S(1)}, f32[32,1,128]{2,1,0:T(1,128)S(1)}) custom-call(f32[15]{0:T(128)S(1)} %concatenate.3.table_ref, f32[2,56,128]{2,1,0:T(8,128)S(1)} %get-tuple-element.13.ext_ref, f32[3,56,128]{2,1,0:T(8,128)S(1)} %get-tuple-element.14.refs_0_, f32[3,56,128]{2,1,0:T(8,128)S(1)} %collective-permute-done.refs_1_, ...), custom_call_target="tpu_custom_call" | custom-call | tf_op jit(solution)/shard_map/basis/pallas_call | solution.py:433
  31.8 9.8 %all_to_all.11.sums_ref = f32[32,1,128]{2,1,0:T(1,128)S(1)} all-to-all(f32[32,1,128]{2,1,0:T(1,128)S(1)} %get-tuple-element.19), channel_id=1, replica_groups=mesh['row'=8,'col'=4] {'row','col'}, dimensions={0} | all-to-all | bytes 32768 | tf_op jit(solution)/shard_map/all_to_all | solution.py:446
  41.5 1.4 %finish.1 = (f32[2,48,96]{2,1,0:T(8,128)}, f32[2,48,96]{2,1,0:T(8,128)}) custom-call(f32[15]{0:T(128)S(1)} %concatenate.3.table_ref, f32[32,1,128]{2,1,0:T(1,128)S(1)} %all_to_all.11.sums_ref, f32[2,48,96]{2,1,0:T(8,128)S(1)} %copy-done, f32[3,2,48,96]{3,2,1,0:T(8,128)S(1)} %get-tuple-element.20.basis_ref), custom_call_target="tpu_custom_call" | custom-call | tf_op jit(solution)/shard_map/finish/pallas_call | solution.py:447
Async XLA Ops:
  4.4 17.8 %copy-start = (f32[2,48,96]{2,1,0:T(8,128)S(1)}, f32[2,48,96]{2,1,0:T(8,128)}, u32[]{:S(2)}) copy-start(f32[2,48,96]{2,1,0:T(8,128)} %field_ref.3) | copy-start | bytes 110596
  23.5 5.3 %collective-permute-start = (f32[3,56,128]{2,1,0:T(8,128)S(1)}, f32[3,56,128]{2,1,0:T(8,128)S(1)}, u32[]{:S(2)}, u32[]{:S(2)}) collective-permute-start(f32[3,56,128]{2,1,0:T(8,128)S(1)} %get-tuple-element.15), channel_id=1, source_target_pairs={{0,1},{1,0},{2,3},{3,2},{4,5},{5,4},{6,7},{7,6},{8,9},{9,8},{10,11... | collective-permute-start | bytes 258056 | tf_op jit(solution)/shard_map/ppermute | solution.py:430
  23.6 1.9 %copy-start.2 = (s32[6]{0:T(128)S(1)}, s32[6]{0:T(128)}, u32[]{:S(2)}) copy-start(s32[6]{0:T(128)} %param.13) | copy-start | bytes 76
  23.6 5.3 %collective-permute-start.1 = (f32[3,56,128]{2,1,0:T(8,128)S(1)}, f32[3,56,128]{2,1,0:T(8,128)S(1)}, u32[]{:S(2)}, u32[]{:S(2)}) collective-permute-start(f32[3,56,128]{2,1,0:T(8,128)S(1)} %get-tuple-element.16), channel_id=1, source_target_pairs={{0,2},{1,3},{2,0},{3,1},{4,6},{5,7},{6,4},{7,5},{8,10},{9,11},{10,... | collective-permute-start | bytes 258056 | tf_op jit(solution)/shard_map/ppermute | solution.py:430
  25.1 4.8 %collective-permute-start.2 = (f32[3,56,128]{2,1,0:T(8,128)S(1)}, f32[3,56,128]{2,1,0:T(8,128)S(1)}, u32[]{:S(2)}, u32[]{:S(2)}) collective-permute-start(f32[3,56,128]{2,1,0:T(8,128)S(1)} %get-tuple-element.17), channel_id=1, source_target_pairs={{0,3},{1,2},{2,1},{3,0},{4,7},{5,6},{6,5},{7,4},{8,11},{9,10},{10,... | collective-permute-start | bytes 258056 | tf_op jit(solution)/shard_map/ppermute | solution.py:430
  26.7 0.7 %copy-start.1 = (f32[6]{0:T(128)S(1)}, f32[6]{0:T(128)}, u32[]{:S(2)}) copy-start(f32[6]{0:T(128)} %param.14) | copy-start | bytes 76

commit v3 on v2

--- a/solution.py
+++ b/solution.py
@@ -27,11 +27,6 @@
     return -(-cells // LANES)
 
 
-def overlap(src_lo, src_hi, tgt_lo, tgt_hi):
-    shared = jnp.maximum(jnp.minimum(src_hi, tgt_hi) - jnp.maximum(src_lo, tgt_lo), 0.0)
-    return shared / jnp.maximum(tgt_hi - tgt_lo, 1.0)
-
-
 def window_rows(row_count):
     count = row_count // 2 - 1
     rows = [[2 * q + 1, 2 * q + 2] for q in range(count)]
@@ -48,7 +43,7 @@
     yt_hbm,
     frac_hbm,
     field_hbm,
-    out_ref,
+    out_hbm,
     xs_ref,
     xt_ref,
     ys_ref,
@@ -57,7 +52,9 @@
     field_ref,
     edges_ref,
     along_ref,
+    out_ref,
     sems,
+    out_sems,
 ):
     me = lax.axis_index("row")
     pairs = frac_ref.shape[0]
@@ -65,23 +62,20 @@
         pltpu.make_async_copy(here, there, sems.at[n])
         for n, (here, there) in enumerate(
             (
+                (yt_hbm, yt_ref),
+                (xt_hbm, xt_ref),
                 (xs_hbm, xs_ref),
-                (xt_hbm, xt_ref),
                 (ys_hbm, ys_ref),
-                (yt_hbm, yt_ref),
+                (frac_hbm, frac_ref),
                 (field_hbm, field_ref),
             )
         )
     ]
-    loads = [
-        pltpu.make_async_copy(frac_hbm.at[p], frac_ref.at[p], sems.at[len(moves) + p])
-        for p in range(pairs)
-    ]
-    for move in moves + loads:
+    for move in moves:
         move.start()
     edges_ref[...] = jnp.zeros_like(edges_ref)
     along_ref[pairs * TBLK :, :] = jnp.zeros_like(along_ref[pairs * TBLK :, :])
-    for n, ref in enumerate((xs_ref, xt_ref, ys_ref, yt_ref)):
+    for n, ref in enumerate((yt_ref, xt_ref, xs_ref, ys_ref)):
         moves[n].wait()
         edges_ref[n : n + 1, 0 : ref.shape[0]] = ref[...].astype(F32)[None, :]
 
@@ -92,57 +86,66 @@
         window = edges_ref[row : row + 1, pl.ds(base, 2 * LANES)]
         return pltpu.roll(window, (lane - (start - base) + 2 * LANES) % (2 * LANES), 1)
 
-    def following(turned):
-        return pltpu.roll(turned, 2 * LANES - 1, 1)
-
-    x_lo = from_here(0, me * SBLK, 0)
-    x_hi = following(x_lo)
-    mine = from_here(1, me * TBLK, 0)
-    lane = lax.broadcasted_iota(jnp.int32, (1, LANES), 1)
-    lows, highs = [mine[:, 0:LANES]], [following(mine)[:, 0:LANES]]
-    for r in range(row_count):
-        own = from_here(3, r * TBLK, 0)
-        upper = TBLK if r + 1 == row_count else TBLK + RIM
-        if r:
-            rim = from_here(3, r * TBLK - RIM, ROWS - RIM)
-            rims = rim, following(rim)
-        else:
-            rims = (jnp.zeros((1, 2 * LANES), F32),) * 2
-        for rows, value, edge in ((lows, own, rims[0]), (highs, following(own), rims[1])):
-            value = jnp.where(lane < upper, value[:, 0:LANES], 0.0)
-            inside = (lane >= ROWS - RIM) & (lane < ROWS)
-            rows.append(jnp.where(inside, edge[:, 0:LANES], value))
-    count = row_count + 1
-    spare = jnp.zeros((-2 * count % 8, LANES), F32)
-    columns = jnp.transpose(jnp.concatenate(lows + highs + [spare], axis=0))
-
-    weight_x = overlap(
-        x_lo[:, 0:SBLK], x_hi[:, 0:SBLK], columns[0:TBLK, 0:1], columns[0:TBLK, count : count + 1]
+    starts = [from_here(0, max(r * TBLK - RIM, 0), 0 if r else RIM) for r in range(row_count)]
+    starts.append(from_here(1, me * TBLK, 0))
+    spare = jnp.zeros((-len(starts) % 8, LANES), F32)
+    columns = jnp.concatenate([start[:, 0:LANES] for start in starts] + [spare], axis=0)
+    columns = jnp.transpose(columns)[0 : ROWS + 8]
+    ends = pltpu.roll(columns, ROWS + 7, 0)
+    row = lax.broadcasted_iota(jnp.int32, (ROWS, columns.shape[1]), 0)
+    block = lax.broadcasted_iota(jnp.int32, (ROWS, columns.shape[1]), 1)
+    inside = (row < jnp.where(block == row_count - 1, TBLK, TBLK + RIM)) | (
+        (row >= ROWS - RIM) & (block > 0)
+    )
+    tgt_lo = jnp.where(inside, pltpu.roll(columns[0:ROWS], ROWS - RIM, 0), 0.0)
+    tgt_hi = jnp.where(inside, pltpu.roll(ends[0:ROWS], ROWS - RIM, 0), 0.0)
+    inverse = 1.0 / jnp.maximum(tgt_hi - tgt_lo, 1.0)
+
+    def weights(src_lo, src_hi, low, high, scale):
+        shared = jnp.maximum(jnp.minimum(src_hi, high) - jnp.maximum(src_lo, low), 0.0)
+        return shared * scale
+
+    mine = slice(row_count, row_count + 1)
+    x_lo = from_here(2, me * SBLK, 0)
+    x_hi = pltpu.roll(x_lo, 2 * LANES - 1, 1)
+    x_tgt_lo, x_tgt_hi = columns[0:TBLK, mine], ends[0:TBLK, mine]
+    weight_x = weights(
+        x_lo[:, 0:SBLK], x_hi[:, 0:SBLK], x_tgt_lo, x_tgt_hi, 1.0 / (x_tgt_hi - x_tgt_lo)
     )
     width = 4 * SBLK
     weights_y = []
     for q, rows in enumerate(window_rows(row_count)):
-        src_lo = edges_ref[2:3, 2 * q * SBLK : 2 * q * SBLK + width]
-        src_hi = edges_ref[2:3, 2 * q * SBLK + 1 : 2 * q * SBLK + width + 1]
+        src_lo = edges_ref[3:4, 2 * q * SBLK : 2 * q * SBLK + width]
+        src_hi = edges_ref[3:4, 2 * q * SBLK + 1 : 2 * q * SBLK + width + 1]
         weights_y.append(
             jnp.concatenate(
                 [
-                    overlap(
-                        src_lo,
-                        src_hi,
-                        columns[0:ROWS, 1 + r : 2 + r],
-                        columns[0:ROWS, count + 1 + r : count + 2 + r],
-                    )
+                    weights(src_lo, src_hi, *(a[:, r : r + 1] for a in (tgt_lo, tgt_hi, inverse)))
                     for r in rows
                 ],
                 axis=0,
             )
         )
+    moves[5].wait()
+    zlayers, height, breadth = field_ref.shape
+    base = ROWS + 8
+    for r in range(row_count):
+        for t in range(tiles(breadth)):
+            lo, hi = t * LANES, min((t + 1) * LANES, breadth)
+            for layer in range(zlayers):
+                rim = jnp.where(
+                    r > me,
+                    field_ref[layer, height - RIM :, lo:hi],
+                    field_ref[layer, :RIM, lo:hi],
+                )
+                at = base + 8 * t + RIM * layer
+                out_ref[r, at : at + RIM, 0 : hi - lo] = rim
+    moves[4].wait()
     for p in range(pairs):
-        loads[p].wait()
         along_ref[p * TBLK : (p + 1) * TBLK, :] = jnp.dot(
             weight_x, frac_ref[p], precision=EXACT, preferred_element_type=F32
         )
+    leaving = []
     for q, rows in enumerate(window_rows(row_count)):
         block = lax.dot_general(
             weights_y[q],
@@ -158,20 +161,21 @@
             for g in range(1, GROUPS):
                 packed = packed + pltpu.roll(mine[8 * g : 8 * g + 8, LANES:], TAIL * g, 1)
             out_ref[r, ROWS : ROWS + 8, :] = packed
-    moves[4].wait()
-    zlayers, height, breadth = field_ref.shape
-    base = ROWS + 8
-    for r in range(row_count):
-        for t in range(tiles(breadth)):
-            lo, hi = t * LANES, min((t + 1) * LANES, breadth)
-            for layer in range(zlayers):
-                rim = jnp.where(
-                    r > me,
-                    field_ref[layer, height - RIM :, lo:hi],
-                    field_ref[layer, :RIM, lo:hi],
-                )
-                at = base + 8 * t + RIM * layer
-                out_ref[r, at : at + RIM, 0 : hi - lo] = rim
+            leaving.append(pltpu.make_async_copy(out_ref.at[r], out_hbm.at[r], out_sems.at[r]))
+            leaving[-1].start()
+    for move in leaving:
+        move.wait()
+
+
+def table_kernel(cond_ref, heat_ref, table_ref):
+    resistance = 16.0 / cond_ref[...].astype(F32)[None, :]
+    heat = heat_ref[...][None, :]
+    middle = 5.0 * M / jnp.sum(resistance, axis=1, keepdims=True)
+    shift = jnp.sum(heat, axis=1, keepdims=True) / M + middle
+    rest = jnp.zeros((1, LANES - 2 * M - 3), F32)
+    table = jnp.concatenate([resistance, heat, shift, 1.0 / middle, middle, rest], axis=1)
+    table = jnp.transpose(jnp.broadcast_to(table, (LANES, LANES)))
+    table_ref[...] = table[0 : table_ref.shape[0]]
 
 
 def regroup_kernel(row_count, col_count, got_ref, field_ref, ext_ref, *out_refs):
@@ -228,10 +232,16 @@
 
 
 def basis_kernel(col_count, height, breadth, table_ref, ext_ref, *refs):
-    arrivals, (shares_ref, basis_ref, sums_ref, got_ref) = refs[:col_count], refs[col_count:]
+    arrivals, refs = refs[:col_count], refs[col_count:]
+    shares_hbm, basis_ref, sums_ref, got_ref, shares_ref, sem = refs
     my_col = lax.axis_index("col")
     for mask, arrival in enumerate(arrivals):
         got_ref[my_col ^ mask] = arrival[...]
+        for p in range(arrival.shape[0]):
+            at = (my_col ^ mask) * arrival.shape[0] + p
+            shares_ref[at] = arrival[p, 0:height, 0:breadth]
+    leaving = pltpu.make_async_copy(shares_ref, shares_hbm, sem)
+    leaving.start()
     zlayers = ext_ref.shape[0]
     pairs, rows, width = got_ref.shape[1:]
     lane = lax.broadcasted_iota(jnp.int32, (rows, width), 1)
@@ -245,6 +255,9 @@
 
     def face(one, other):
         return 2.0 * one * other / jnp.maximum(one + other, TINY)
+
+    def entry(n):
+        return table_ref[n : n + 1, 0:1]
 
     cell_k, heat, field = [], [], []
     for z in range(zlayers):
@@ -253,10 +266,9 @@
         for m in range(M):
             c, p = divmod(z * M + m, pairs)
             share = got_ref[c, p]
-            shares_ref[z * M + m] = share[0:height, 0:breadth]
             inside = jnp.where((lane < breadth + RIM) | (lane >= width - RIM), share, 0.0)
-            inverse = inverse + inside * table_ref[m]
-            total = total + inside * table_ref[M + m]
+            inverse = inverse + inside * entry(m)
+            total = total + inside * entry(M + m)
         cell_k.append(jnp.where(inverse > 0.0, 1.0 / jnp.where(inverse > 0.0, inverse, 1.0), 0.0))
         heat.append(total)
         left, right = got_ref[before, z], got_ref[after, z]
@@ -285,7 +297,7 @@
             result.append(value)
         return result
 
-    shift, scale = table_ref[2 * M], table_ref[2 * M + 1]
+    shift, scale = entry(2 * M), entry(2 * M + 1)
 
     def shifted(w):
         return [(a - shift * b) * scale for a, b in zip(operate(w), w)]
@@ -312,6 +324,7 @@
             packed = packed + jnp.where(slot == at, value, 0.0)
             at += 1
     sums_ref[...] = jnp.broadcast_to(packed[None], sums_ref.shape)
+    leaving.wait()
 
 
 def finish_kernel(table_ref, sums_ref, field_ref, basis_ref, iterate_ref, defect_ref):
@@ -322,15 +335,18 @@
         for b in range(a, ITERS + 1):
             gram[a, b] = gram[b, a] = total[:, at : at + 1]
             at += 1
-    shift, scale = table_ref[2 * M], table_ref[2 * M + 2]
+    shift, scale = (table_ref[n : n + 1, 0:1] for n in (2 * M, 2 * M + 2))
 
     def inner(left, right):
-        value = None
+        rows = []
         for a, one in left.items():
-            for b, other in right.items():
-                term = one * other * gram[a, b]
-                value = term if value is None else value + term
-        return value
+            rows.append(one * total_of([other * gram[a, b] for b, other in right.items()]))
+        return total_of(rows)
+
+    def total_of(terms):
+        while len(terms) > 1:
+            terms = [sum(terms[n : n + 2][1:], terms[n]) for n in range(0, len(terms), 2)]
+        return terms[0]
 
     def combine(left, factor, right):
         result = dict(left)
@@ -385,38 +401,38 @@
     send_rows = ROWS + 8 + 8 * tiles(breadth)
     params = pltpu.CompilerParams(vmem_limit_bytes=VMEM)
 
-    resistance = 16.0 / conductivity_table.astype(F32)
-    middle = 5.0 * M / jnp.sum(resistance)
-    table = jnp.concatenate(
-        [
-            resistance,
-            capacity,
-            jnp.stack([jnp.mean(capacity) + middle, 1.0 / middle, middle]),
-        ]
-    )
-
-    smem = pl.BlockSpec(memory_space=pltpu.SMEM)
     vmem = pl.BlockSpec(memory_space=pltpu.VMEM)
     hbm = pl.BlockSpec(memory_space=pltpu.HBM)
     along_rows = -(-pairs * TBLK // LANES) * LANES
     edges = [x_source_edges, x_target_edges, y_source_edges, y_target_edges]
+    outgoing = jax.ShapeDtypeStruct((row_count, send_rows, LANES), F32)
     outgoing = pl.pallas_call(
         functools.partial(rezone_kernel, row_count),
-        out_shape=jax.ShapeDtypeStruct((row_count, send_rows, LANES), F32),
+        out_shape=outgoing,
         in_specs=[hbm] * 6,
-        out_specs=vmem,
+        out_specs=hbm,
         scratch_shapes=[pltpu.VMEM(e.shape, e.dtype) for e in edges]
         + [
             pltpu.VMEM(fractions_source.shape, F32),
             pltpu.VMEM(thermal_source_term.shape, F32),
             pltpu.VMEM((8, LANES * (tiles(source_cells + 1) + 1)), F32),
             pltpu.VMEM((along_rows, source_cells), F32),
-            pltpu.SemaphoreType.DMA((5 + pairs,)),
+            pltpu.VMEM(outgoing.shape, F32),
+            pltpu.SemaphoreType.DMA((6,)),
+            pltpu.SemaphoreType.DMA((row_count,)),
         ],
         compiler_params=pltpu.CompilerParams(vmem_limit_bytes=FULL),
         name="rezone",
     )(*edges, fractions_source, thermal_source_term)
     arrived = lax.all_to_all(outgoing, "row", split_axis=0, concat_axis=0, tiled=True)
+    table = pl.pallas_call(
+        table_kernel,
+        out_shape=jax.ShapeDtypeStruct((-(-(2 * M + 3) // 8) * 8, LANES), F32),
+        in_specs=[vmem] * 2,
+        out_specs=vmem,
+        compiler_params=params,
+        name="table",
+    )(conductivity_table, capacity)
     message = jax.ShapeDtypeStruct((pairs, ROWS, width), F32)
     extended, *parts = pl.pallas_call(
         functools.partial(regroup_kernel, row_count, col_count),
@@ -437,9 +453,13 @@
             jax.ShapeDtypeStruct((ITERS, zlayers, height, breadth), F32),
             jax.ShapeDtypeStruct((row_count * col_count, 1, LANES), F32),
         ],
-        in_specs=[smem] + [vmem] * (1 + col_count),
-        out_specs=[vmem] * 3,
-        scratch_shapes=[pltpu.VMEM((col_count, *message.shape), F32)],
+        in_specs=[vmem] * (2 + col_count),
+        out_specs=[hbm, vmem, vmem],
+        scratch_shapes=[
+            pltpu.VMEM((col_count, *message.shape), F32),
+            pltpu.VMEM((zlayers * M, height, breadth), F32),
+            pltpu.SemaphoreType.DMA,
+        ],
         compiler_params=params,
         name="basis",
     )(table, extended, *parts)
@@ -447,7 +467,7 @@
     thermal_iterate, remaining_defect = pl.pallas_call(
         finish_kernel,
         out_shape=[jax.ShapeDtypeStruct((zlayers, height, breadth), F32)] * 2,
-        in_specs=[smem, vmem, vmem, vmem],
+        in_specs=[vmem] * 4,
         out_specs=[vmem] * 2,
         compiler_params=params,
         name="finish",

time: 43.3 us -> 41.7 us (0.963)
  waiting for transfers between devices: 1.18 us -> 4.37 us
  between operations: 2.7 us -> 0.69 us
  Pallas kernels: 8.29 us -> 6.9 us
  other arithmetic: 1.21 us -> 0 us
    ppermute x3, waiting for transfers between devices: 1.18 us -> 4.37 us  [per_device(): lax.ppermute(parts[mask], 'col', [(c, c ^ mask) for c in range(col_count)])]
    reduce_sum x2 -> x0, other arithmetic: 1.21 us -> none  [the longest x1 0.61 us: per_device(): middle = 5.0 * M / jnp.sum(resistance)]
    pallas_call x1, Pallas kernels: 1.4 us -> 0.85 us  [per_device(): pl.pallas_call(finish_kernel, out_shape=[jax.ShapeDtypeStruct((zlayers, h...]
    pallas_call x1, Pallas kernels: 1.82 us -> 1.31 us  [per_device(): pl.pallas_call(functools.partial(basis_kernel, col_count, height, breadth...]
    pallas_call x1 -> x2, Pallas kernels: 3.78 us -> 3.45 us  [the longest x1 3.31 us: per_device(): pl.pallas_call(functools.partial(rezone_kernel, row_count), out_shape=out...]
  transfers between devices with their start and end apart: 3 -> 3, of which waited for: 2 -> 2; matrix products, arithmetic and copies ran while one was open for 3% -> 0% of each run, Pallas kernels for 0% -> 0%
where the time goes in v3:
time: 41.7 us; the launch traced here: 41.4 us
  blocking collectives  27.5 us (66%)
  Pallas kernels  6.9 us (17%)
  waiting for transfers between devices  4.37 us (10%)
  starting transfers between devices  1.92 us (5%)
  between operations  0.69 us (2%)
    all_to_all x1, blocking collectives, per_device(): lax.all_to_all(outgoing, 'row', split_axis=0, concat_axis=0, tiled=True)  17.8 us
    all_to_all x1, blocking collectives, per_device(): lax.all_to_all(sums, ('row', 'col'), split_axis=0, concat_axis=0, tiled=T...  9.77 us
    ppermute x3, waiting for transfers between devices, per_device(): lax.ppermute(parts[mask], 'col', [(c, c ^ mask) for c in range(col_count)])  4.37 us
    pallas_call x1, Pallas kernels, per_device(): pl.pallas_call(functools.partial(rezone_kernel, row_count), out_shape=out...  3.31 us
    ppermute x3, starting transfers between devices, per_device(): lax.ppermute(parts[mask], 'col', [(c, c ^ mask) for c in range(col_count)])  1.92 us
    pallas_call x1, Pallas kernels, per_device(): pl.pallas_call(functools.partial(basis_kernel, col_count, height, breadth...  1.31 us
    pallas_call x1, Pallas kernels, per_device(): pl.pallas_call(functools.partial(regroup_kernel, row_count, col_count), o...  1.29 us
    pallas_call x1, Pallas kernels, per_device(): pl.pallas_call(finish_kernel, out_shape=[jax.ShapeDtypeStruct((zlayers, h...  0.85 us
  transfers between devices with their start and end apart: 3, of which 2 were waited for; matrix products, arithmetic and copies ran while one was open for 0% of the time, Pallas kernels for 0%

profile of v3, /device:TPU:0, one launch (start us, length us, event | category | flops | bytes accessed | tf_op | source)
XLA Modules:
  0.0 41.4 jit_solution(8237405904547394277)
XLA Ops:
  0.6 3.3 %rezone.1 = f32[8,72,128]{2,1,0:T(8,128)} custom-call(s32[513]{0:T(1024)} %xs_hbm.1, s32[385]{0:T(512)} %xt_hbm.1, s32[513]{0:T(1024)} %ys_hbm.1, s32[385]{0:T(512)} %yt_hbm.1, f32[3,64,512]{2,1,0:T(8,128)} %frac_hbm.1, f32[2,48,96]{2,1,0:T(8,128)} %field_ref.3), custom_call_target="tpu_custom_call" | custom-call | tf_op jit(solution)/shard_map/rezone/pallas_call | solution.py:409
  4.0 0.0 copy-start
  4.0 17.8 %all_to_all.10.got_ref = f32[8,72,128]{2,1,0:T(8,128)S(1)} all-to-all(f32[8,72,128]{2,1,0:T(8,128)} %rezone.1), channel_id=1, replica_groups=mesh['row'=8,'col'=4] {'row'}, dimensions={0} | all-to-all | bytes 589824 | tf_op jit(solution)/shard_map/all_to_all | solution.py:427
  21.7 0.0 copy-done
  21.7 1.3 %regroup.1 = (f32[2,56,128]{2,1,0:T(8,128)S(1)}, f32[3,56,128]{2,1,0:T(8,128)S(1)}, f32[3,56,128]{2,1,0:T(8,128)S(1)}, f32[3,56,128]{2,1,0:T(8,128)S(1)}, f32[3,56,128]{2,1,0:T(8,128)S(1)}) custom-call(f32[8,72,128]{2,1,0:T(8,128)S(1)} %all_to_all.10.got_ref, f32[2,48,96]{2,1,0:T(8,128)S(1)} %copy-done), custom_call_target="tpu_custom_call" | custom-call | tf_op jit(solution)/shard_map/regroup/pallas_call | solution.py:437
  23.0 0.1 collective-permute-start
  23.1 0.0 copy-start.1
  23.1 0.0 copy-start.2
  23.1 1.6 %collective-permute-start.1 = (f32[3,56,128]{2,1,0:T(8,128)S(1)}, f32[3,56,128]{2,1,0:T(8,128)S(1)}, u32[]{:S(2)}, u32[]{:S(2)}) collective-permute-start(f32[3,56,128]{2,1,0:T(8,128)S(1)} %get-tuple-element.16), channel_id=1, source_target_pairs={{0,2},{1,3},{2,0},{3,1},{4,6},{5,7},{6,4},{7,5},{8,10},{9,11},{10,... | collective-permute-start | bytes 258056 | tf_op jit(solution)/shard_map/ppermute | solution.py:446
  24.7 0.3 collective-permute-start.2
  25.0 0.0 copy-done.1
  25.0 0.0 copy-done.2
  25.0 0.1 table.1.table_ref
  25.1 0.0 collective-permute-done.refs_1_
  25.1 3.3 %collective-permute-done.1.refs_2_ = f32[3,56,128]{2,1,0:T(8,128)S(1)} collective-permute-done((f32[3,56,128]{2,1,0:T(8,128)S(1)}, f32[3,56,128]{2,1,0:T(8,128)S(1)}, u32[]{:S(2)}, u32[]{:S(2)}) %collective-permute-start.1) | collective-permute-done | bytes 86048 | tf_op jit(solution)/shard_map/ppermute | solution.py:446
  28.5 1.0 %collective-permute-done.2.refs_3_ = f32[3,56,128]{2,1,0:T(8,128)S(1)} collective-permute-done((f32[3,56,128]{2,1,0:T(8,128)S(1)}, f32[3,56,128]{2,1,0:T(8,128)S(1)}, u32[]{:S(2)}, u32[]{:S(2)}) %collective-permute-start.2) | collective-permute-done | bytes 86048 | tf_op jit(solution)/shard_map/ppermute | solution.py:446
  29.5 1.3 %basis.1 = (f32[12,48,96]{2,1,0:T(8,128)}, f32[3,2,48,96]{3,2,1,0:T(8,128)S(1)}, f32[32,1,128]{2,1,0:T(1,128)S(1)}) custom-call(f32[16,128]{1,0:T(8,128)S(1)} %table.1.table_ref, f32[2,56,128]{2,1,0:T(8,128)S(1)} %get-tuple-element.13.ext_ref, f32[3,56,128]{2,1,0:T(8,128)S(1)} %get-tuple-element.14.refs_0_, f32[3,56,128]{2,1,0:T(8,128)S(1)} %collective-permute-done.refs_1_, ...), custom_call_target="tpu_custom_call" | custom-call | tf_op jit(solution)/shard_map/basis/pallas_call | solution.py:449
  30.8 9.8 %all_to_all.11.sums_ref = f32[32,1,128]{2,1,0:T(1,128)S(1)} all-to-all(f32[32,1,128]{2,1,0:T(1,128)S(1)} %get-tuple-element.19), channel_id=1, replica_groups=mesh['row'=8,'col'=4] {'row','col'}, dimensions={0} | all-to-all | bytes 32768 | tf_op jit(solution)/shard_map/all_to_all | solution.py:466
  40.6 0.8 %finish.1 = (f32[2,48,96]{2,1,0:T(8,128)}, f32[2,48,96]{2,1,0:T(8,128)}) custom-call(f32[16,128]{1,0:T(8,128)S(1)} %table.1.table_ref, f32[32,1,128]{2,1,0:T(1,128)S(1)} %all_to_all.11.sums_ref, f32[2,48,96]{2,1,0:T(8,128)S(1)} %copy-done, f32[3,2,48,96]{3,2,1,0:T(8,128)S(1)} %get-tuple-element.20.basis_ref), custom_call_target="tpu_custom_call" | custom-call | tf_op jit(solution)/shard_map/finish/pallas_call | solution.py:467
Async XLA Ops:
  4.0 17.8 %copy-start = (f32[2,48,96]{2,1,0:T(8,128)S(1)}, f32[2,48,96]{2,1,0:T(8,128)}, u32[]{:S(2)}) copy-start(f32[2,48,96]{2,1,0:T(8,128)} %field_ref.3) | copy-start | bytes 110596
  23.0 2.1 %collective-permute-start = (f32[3,56,128]{2,1,0:T(8,128)S(1)}, f32[3,56,128]{2,1,0:T(8,128)S(1)}, u32[]{:S(2)}, u32[]{:S(2)}) collective-permute-start(f32[3,56,128]{2,1,0:T(8,128)S(1)} %get-tuple-element.15), channel_id=1, source_target_pairs={{0,1},{1,0},{2,3},{3,2},{4,5},{5,4},{6,7},{7,6},{8,9},{9,8},{10,11... | collective-permute-start | bytes 258056 | tf_op jit(solution)/shard_map/ppermute | solution.py:446
  23.1 1.9 %copy-start.1 = (s32[6]{0:T(128)S(1)}, s32[6]{0:T(128)}, u32[]{:S(2)}) copy-start(s32[6]{0:T(128)} %cond_ref.1) | copy-start | bytes 76
  23.1 1.9 %copy-start.2 = (f32[6]{0:T(128)S(1)}, f32[6]{0:T(128)}, u32[]{:S(2)}) copy-start(f32[6]{0:T(128)} %heat_ref.1) | copy-start | bytes 76
  23.1 5.3 %collective-permute-start.1 = (f32[3,56,128]{2,1,0:T(8,128)S(1)}, f32[3,56,128]{2,1,0:T(8,128)S(1)}, u32[]{:S(2)}, u32[]{:S(2)}) collective-permute-start(f32[3,56,128]{2,1,0:T(8,128)S(1)} %get-tuple-element.16), channel_id=1, source_target_pairs={{0,2},{1,3},{2,0},{3,1},{4,6},{5,7},{6,4},{7,5},{8,10},{9,11},{10,... | collective-permute-start | bytes 258056 | tf_op jit(solution)/shard_map/ppermute | solution.py:446
  24.7 4.8 %collective-permute-start.2 = (f32[3,56,128]{2,1,0:T(8,128)S(1)}, f32[3,56,128]{2,1,0:T(8,128)S(1)}, u32[]{:S(2)}, u32[]{:S(2)}) collective-permute-start(f32[3,56,128]{2,1,0:T(8,128)S(1)} %get-tuple-element.17), channel_id=1, source_target_pairs={{0,3},{1,2},{2,1},{3,0},{4,7},{5,6},{6,5},{7,4},{8,11},{9,10},{10,... | collective-permute-start | bytes 258056 | tf_op jit(solution)/shard_map/ppermute | solution.py:446

commit v4 on v3

--- a/solution.py
+++ b/solution.py
@@ -112,6 +112,11 @@
     weight_x = weights(
         x_lo[:, 0:SBLK], x_hi[:, 0:SBLK], x_tgt_lo, x_tgt_hi, 1.0 / (x_tgt_hi - x_tgt_lo)
     )
+    moves[4].wait()
+    for p in range(pairs):
+        along_ref[p * TBLK : (p + 1) * TBLK, :] = jnp.dot(
+            weight_x, frac_ref[p], precision=EXACT, preferred_element_type=F32
+        )
     width = 4 * SBLK
     weights_y = []
     for q, rows in enumerate(window_rows(row_count)):
@@ -140,11 +145,6 @@
                 )
                 at = base + 8 * t + RIM * layer
                 out_ref[r, at : at + RIM, 0 : hi - lo] = rim
-    moves[4].wait()
-    for p in range(pairs):
-        along_ref[p * TBLK : (p + 1) * TBLK, :] = jnp.dot(
-            weight_x, frac_ref[p], precision=EXACT, preferred_element_type=F32
-        )
     leaving = []
     for q, rows in enumerate(window_rows(row_count)):
         block = lax.dot_general(
@@ -161,8 +161,9 @@
             for g in range(1, GROUPS):
                 packed = packed + pltpu.roll(mine[8 * g : 8 * g + 8, LANES:], TAIL * g, 1)
             out_ref[r, ROWS : ROWS + 8, :] = packed
-            leaving.append(pltpu.make_async_copy(out_ref.at[r], out_hbm.at[r], out_sems.at[r]))
-            leaving[-1].start()
+        done = pl.ds(rows[0], len(rows))
+        leaving.append(pltpu.make_async_copy(out_ref.at[done], out_hbm.at[done], out_sems.at[q]))
+        leaving[-1].start()
     for move in leaving:
         move.wait()
 
@@ -178,11 +179,9 @@
     table_ref[...] = table[0 : table_ref.shape[0]]
 
 
-def regroup_kernel(row_count, col_count, got_ref, field_ref, ext_ref, *out_refs):
-    my_row, my_col = lax.axis_index("row"), lax.axis_index("col")
+def extend_rows(row_count, got_ref, field_ref, ext_ref):
+    my_row = lax.axis_index("row")
     zlayers, height, breadth = field_ref.shape
-    pairs, _, width = out_refs[0].shape
-    per_col = row_count // col_count
     base = ROWS + 8
     ext_ref[...] = jnp.zeros_like(ext_ref)
     below, above = jnp.maximum(my_row - 1, 0), jnp.minimum(my_row + 1, row_count - 1)
@@ -198,6 +197,16 @@
             )
             ext_ref[layer, ROWS - RIM : ROWS, lo:hi] = jnp.where(my_row > 0, before, 0.0)
 
+
+def regroup_kernel(row_count, col_count, masks, got_ref, field_ref, *refs):
+    my_col = lax.axis_index("col")
+    zlayers, _, breadth = field_ref.shape
+    ext_ref, out_refs = refs[0], refs[1:]
+    pairs, _, width = out_refs[0].shape
+    per_col = row_count // col_count
+    if col_count // 2 in masks:
+        extend_rows(row_count, got_ref, field_ref, ext_ref)
+
     def piece(block, pair, first, last):
         start = pair * TBLK
         lo, hi = start + first, start + last
@@ -212,7 +221,7 @@
             )
         return parts[0] if len(parts) == 1 else jnp.concatenate(parts, axis=1)
 
-    for mask, out_ref in enumerate(out_refs):
+    for mask, out_ref in zip(masks, out_refs):
         c = my_col ^ mask
         first = c * per_col
         left, right = jnp.maximum(first - 1, 0), jnp.minimum(first + per_col, row_count - 1)
@@ -233,15 +242,13 @@
 
 def basis_kernel(col_count, height, breadth, table_ref, ext_ref, *refs):
     arrivals, refs = refs[:col_count], refs[col_count:]
-    shares_hbm, basis_ref, sums_ref, got_ref, shares_ref, sem = refs
+    shares_ref, basis_ref, sums_ref, got_ref = refs
     my_col = lax.axis_index("col")
     for mask, arrival in enumerate(arrivals):
         got_ref[my_col ^ mask] = arrival[...]
         for p in range(arrival.shape[0]):
             at = (my_col ^ mask) * arrival.shape[0] + p
             shares_ref[at] = arrival[p, 0:height, 0:breadth]
-    leaving = pltpu.make_async_copy(shares_ref, shares_hbm, sem)
-    leaving.start()
     zlayers = ext_ref.shape[0]
     pairs, rows, width = got_ref.shape[1:]
     lane = lax.broadcasted_iota(jnp.int32, (rows, width), 1)
@@ -324,10 +331,24 @@
             packed = packed + jnp.where(slot == at, value, 0.0)
             at += 1
     sums_ref[...] = jnp.broadcast_to(packed[None], sums_ref.shape)
-    leaving.wait()
-
-
-def finish_kernel(table_ref, sums_ref, field_ref, basis_ref, iterate_ref, defect_ref):
+
+
+def finish_kernel(
+    table_ref,
+    sums_ref,
+    field_ref,
+    basis_ref,
+    shares_ref,
+    iterate_hbm,
+    defect_hbm,
+    shares_hbm,
+    iterate_ref,
+    defect_ref,
+    sems,
+):
+    pairs = (shares_ref, shares_hbm), (iterate_ref, iterate_hbm), (defect_ref, defect_hbm)
+    leaving = [pltpu.make_async_copy(*pair, sems.at[n]) for n, pair in enumerate(pairs)]
+    leaving[0].start()
     total = jnp.sum(sums_ref[...], axis=0)
     gram = {}
     at = 0
@@ -377,10 +398,13 @@
             following = inner(defect, defect)
             direction = combine(defect, following / norm, direction)
             norm = following
-    for z in range(field_ref.shape[0]):
-        vectors = [field_ref[z]] + [basis_ref[n, z] for n in range(ITERS)]
-        iterate_ref[z] = sum(weight * vectors[a] for a, weight in iterate.items())
-        defect_ref[z] = sum(weight * vectors[a] for a, weight in defect.items())
+    for ref, weights, move in ((iterate_ref, iterate, leaving[1]), (defect_ref, defect, leaving[2])):
+        for z in range(field_ref.shape[0]):
+            vectors = [field_ref[z]] + [basis_ref[n, z] for n in range(ITERS)]
+            ref[z] = total_of([weight * vectors[a] for a, weight in weights.items()])
+        move.start()
+    for move in leaving:
+        move.wait()
 
 
 def per_device(
@@ -419,7 +443,7 @@
             pltpu.VMEM((along_rows, source_cells), F32),
             pltpu.VMEM(outgoing.shape, F32),
             pltpu.SemaphoreType.DMA((6,)),
-            pltpu.SemaphoreType.DMA((row_count,)),
+            pltpu.SemaphoreType.DMA((row_count // 2 - 1,)),
         ],
         compiler_params=pltpu.CompilerParams(vmem_limit_bytes=FULL),
         name="rezone",
@@ -434,19 +458,32 @@
         name="table",
     )(conductivity_table, capacity)
     message = jax.ShapeDtypeStruct((pairs, ROWS, width), F32)
-    extended, *parts = pl.pallas_call(
-        functools.partial(regroup_kernel, row_count, col_count),
-        out_shape=[jax.ShapeDtypeStruct((zlayers, ROWS, width), F32)] + [message] * col_count,
+    half = col_count // 2
+    near, far = range(half), range(half, col_count)
+    extended, *far_parts = pl.pallas_call(
+        functools.partial(regroup_kernel, row_count, col_count, far),
+        out_shape=[jax.ShapeDtypeStruct((zlayers, ROWS, width), F32)] + [message] * half,
         in_specs=[vmem] * 2,
-        out_specs=[vmem] * (1 + col_count),
+        out_specs=[vmem] * (1 + half),
         compiler_params=params,
-        name="regroup",
+        name="regroup_far",
     )(arrived, thermal_source_term)
-    parts = [parts[0]] + [
-        lax.ppermute(parts[mask], "col", [(c, c ^ mask) for c in range(col_count)])
-        for mask in range(1, col_count)
-    ]
-    rezoned_occupancy_shares, basis, sums = pl.pallas_call(
+
+    def swap(part, mask):
+        return lax.ppermute(part, "col", [(c, c ^ mask) for c in range(col_count)])
+
+    far_parts = [swap(part, mask) for part, mask in zip(far_parts, far)]
+    near_parts = pl.pallas_call(
+        functools.partial(regroup_kernel, row_count, col_count, near),
+        out_shape=[message] * half,
+        in_specs=[vmem] * 3,
+        out_specs=[vmem] * half,
+        compiler_params=params,
+        cost_estimate=pl.CostEstimate(flops=10**6, bytes_accessed=2 * 10**6, transcendentals=0),
+        name="regroup_near",
+    )(arrived, thermal_source_term, extended)
+    parts = [swap(part, mask) if mask else part for part, mask in zip(near_parts, near)] + far_parts
+    shares, basis, sums = pl.pallas_call(
         functools.partial(basis_kernel, col_count, height, breadth),
         out_shape=[
             jax.ShapeDtypeStruct((zlayers * M, height, breadth), F32),
@@ -454,24 +491,23 @@
             jax.ShapeDtypeStruct((row_count * col_count, 1, LANES), F32),
         ],
         in_specs=[vmem] * (2 + col_count),
-        out_specs=[hbm, vmem, vmem],
-        scratch_shapes=[
-            pltpu.VMEM((col_count, *message.shape), F32),
-            pltpu.VMEM((zlayers * M, height, breadth), F32),
-            pltpu.SemaphoreType.DMA,
-        ],
+        out_specs=[vmem] * 3,
+        scratch_shapes=[pltpu.VMEM((col_count, *message.shape), F32)],
         compiler_params=params,
         name="basis",
     )(table, extended, *parts)
     sums = lax.all_to_all(sums, ("row", "col"), split_axis=0, concat_axis=0, tiled=True)
-    thermal_iterate, remaining_defect = pl.pallas_call(
+    thermal_iterate, remaining_defect, rezoned_occupancy_shares = pl.pallas_call(
         finish_kernel,
-        out_shape=[jax.ShapeDtypeStruct((zlayers, height, breadth), F32)] * 2,
-        in_specs=[vmem] * 4,
-        out_specs=[vmem] * 2,
+        out_shape=[jax.ShapeDtypeStruct((zlayers, height, breadth), F32)] * 2
+        + [jax.ShapeDtypeStruct(shares.shape, F32)],
+        in_specs=[vmem] * 5,
+        out_specs=[hbm] * 3,
+        scratch_shapes=[pltpu.VMEM((zlayers, height, breadth), F32)] * 2
+        + [pltpu.SemaphoreType.DMA((3,))],
         compiler_params=params,
         name="finish",
-    )(table, sums, thermal_source_term, basis)
+    )(table, sums, thermal_source_term, basis, shares)
     return rezoned_occupancy_shares, thermal_iterate, remaining_defect
 
 

time: 41.7 us -> 39.8 us (0.954)
  waiting for transfers between devices: 4.37 us -> 3.42 us
  Pallas kernels: 6.9 us -> 6.1 us
  blocking collectives: 27.5 us -> 27 us
    ppermute x3, waiting for transfers between devices: 4.37 us -> 3.42 us  [swap(): return lax.ppermute(part, 'col', [(c, c ^ mask) for c in range(col_count)])]
    pallas_call x1, Pallas kernels: 1.31 us -> 0.68 us  [per_device(): pl.pallas_call(functools.partial(basis_kernel, col_count, height, breadth...]
    all_to_all x1, blocking collectives: 9.77 us -> 9.25 us  [per_device(): lax.all_to_all(sums, ('row', 'col'), split_axis=0, concat_axis=0, tiled=T...]
    pallas_call x1 -> x2, Pallas kernels: 1.29 us -> 1.14 us  [the longest x1 0.64 us: per_device(): pl.pallas_call(functools.partial(regroup_kernel, row_count, col_count, fa...]
  transfers between devices with their start and end apart: 3 -> 3, of which waited for: 2 -> 2; matrix products, arithmetic and copies ran while one was open for 0% -> 0% of each run, Pallas kernels for 0% -> 2%
where the time goes in v4:
time: 39.8 us; the launch traced here: 39.5 us
  blocking collectives  27 us (68%)
  Pallas kernels  6.1 us (15%)
  waiting for transfers between devices  3.42 us (9%)
  starting transfers between devices  2.27 us (6%)
  between operations  0.69 us (2%)
    all_to_all x1, blocking collectives, per_device(): lax.all_to_all(outgoing, 'row', split_axis=0, concat_axis=0, tiled=True)  17.8 us
    all_to_all x1, blocking collectives, per_device(): lax.all_to_all(sums, ('row', 'col'), split_axis=0, concat_axis=0, tiled=T...  9.25 us
    ppermute x3, waiting for transfers between devices, swap(): return lax.ppermute(part, 'col', [(c, c ^ mask) for c in range(col_count)])  3.42 us
    pallas_call x1, Pallas kernels, per_device(): pl.pallas_call(functools.partial(rezone_kernel, row_count), out_shape=out...  3.27 us
    ppermute x3, starting transfers between devices, swap(): return lax.ppermute(part, 'col', [(c, c ^ mask) for c in range(col_count)])  2.27 us
    pallas_call x1, Pallas kernels, per_device(): pl.pallas_call(finish_kernel, out_shape=[jax.ShapeDtypeStruct((zlayers, h...  0.87 us
  transfers between devices with their start and end apart: 3, of which 2 were waited for; matrix products, arithmetic and copies ran while one was open for 0% of the time, Pallas kernels for 2%

profile of v4, /device:TPU:0, one launch (start us, length us, event | category | flops | bytes accessed | tf_op | source)
XLA Modules:
  0.0 39.5 jit_solution(5738179970051970438)
XLA Ops:
  0.6 3.3 %rezone.1 = f32[8,72,128]{2,1,0:T(8,128)} custom-call(s32[513]{0:T(1024)} %xs_hbm.1, s32[385]{0:T(512)} %xt_hbm.1, s32[513]{0:T(1024)} %ys_hbm.1, s32[385]{0:T(512)} %yt_hbm.1, f32[3,64,512]{2,1,0:T(8,128)} %frac_hbm.1, f32[2,48,96]{2,1,0:T(8,128)} %field_ref.5), custom_call_target="tpu_custom_call" | custom-call | tf_op jit(solution)/shard_map/rezone/pallas_call | solution.py:433
  3.9 0.0 copy-start
  3.9 17.8 %all_to_all.10.got_ref = f32[8,72,128]{2,1,0:T(8,128)S(1)} all-to-all(f32[8,72,128]{2,1,0:T(8,128)} %rezone.1), channel_id=1, replica_groups=mesh['row'=8,'col'=4] {'row'}, dimensions={0} | all-to-all | bytes 589824 | tf_op jit(solution)/shard_map/all_to_all | solution.py:451
  21.7 0.0 copy-done
  21.7 0.6 %regroup_far.1 = (f32[2,56,128]{2,1,0:T(8,128)S(1)}, f32[3,56,128]{2,1,0:T(8,128)S(1)}, f32[3,56,128]{2,1,0:T(8,128)S(1)}) custom-call(f32[8,72,128]{2,1,0:T(8,128)S(1)} %all_to_all.10.got_ref, f32[2,48,96]{2,1,0:T(8,128)S(1)} %copy-done), custom_call_target="tpu_custom_call" | custom-call | tf_op jit(solution)/shard_map/regroup_far/pallas_call | solution.py:463
  22.3 1.6 %collective-permute-start.1 = (f32[3,56,128]{2,1,0:T(8,128)S(1)}, f32[3,56,128]{2,1,0:T(8,128)S(1)}, u32[]{:S(2)}, u32[]{:S(2)}) collective-permute-start(f32[3,56,128]{2,1,0:T(8,128)S(1)} %get-tuple-element.17), channel_id=1, source_target_pairs={{0,2},{1,3},{2,0},{3,1},{4,6},{5,7},{6,4},{7,5},{8,10},{9,11},{10,... | collective-permute-start | bytes 258056 | tf_op jit(solution)/shard_map/ppermute | solution.py:473
  23.9 0.0 collective-permute-start.2
  23.9 0.5 %regroup_near.1 = (f32[3,56,128]{2,1,0:T(8,128)S(1)}, f32[3,56,128]{2,1,0:T(8,128)S(1)}) custom-call(f32[8,72,128]{2,1,0:T(8,128)S(1)} %all_to_all.10.got_ref, f32[2,48,96]{2,1,0:T(8,128)S(1)} %copy-done, f32[2,56,128]{2,1,0:T(8,128)S(1)} %get-tuple-element.14.refs_0_.ext_ref), custom_call_target="tpu_custom_call" | custom-call | flops 1000000 | bytes 2000000 | tf_op jit(solution)/shard_map/regroup_near/pallas_call | solution.py:476
  24.4 0.0 copy-start.1
  24.4 0.0 copy-start.2
  24.4 0.7 %collective-permute-start = (f32[3,56,128]{2,1,0:T(8,128)S(1)}, f32[3,56,128]{2,1,0:T(8,128)S(1)}, u32[]{:S(2)}, u32[]{:S(2)}) collective-permute-start(f32[3,56,128]{2,1,0:T(8,128)S(1)} %get-tuple-element.16), channel_id=1, source_target_pairs={{0,1},{1,0},{2,3},{3,2},{4,5},{5,4},{6,7},{7,6},{8,9},{9,8},{10,11... | collective-permute-start | bytes 258056 | tf_op jit(solution)/shard_map/ppermute | solution.py:473
  25.1 0.0 copy-done.1
  25.1 0.0 copy-done.2
  25.1 0.1 table.1.table_ref
  25.3 1.6 %collective-permute-done.1.refs_2_ = f32[3,56,128]{2,1,0:T(8,128)S(1)} collective-permute-done((f32[3,56,128]{2,1,0:T(8,128)S(1)}, f32[3,56,128]{2,1,0:T(8,128)S(1)}, u32[]{:S(2)}, u32[]{:S(2)}) %collective-permute-start.1) | collective-permute-done | bytes 86048 | tf_op jit(solution)/shard_map/ppermute | solution.py:473
  26.9 1.8 %collective-permute-done.2.refs_3_ = f32[3,56,128]{2,1,0:T(8,128)S(1)} collective-permute-done((f32[3,56,128]{2,1,0:T(8,128)S(1)}, f32[3,56,128]{2,1,0:T(8,128)S(1)}, u32[]{:S(2)}, u32[]{:S(2)}) %collective-permute-start.2) | collective-permute-done | bytes 86048 | tf_op jit(solution)/shard_map/ppermute | solution.py:473
  28.7 0.0 collective-permute-done.refs_1_
  28.7 0.7 %basis.1 = (f32[12,48,96]{2,1,0:T(8,128)S(1)}, f32[3,2,48,96]{3,2,1,0:T(8,128)S(1)}, f32[32,1,128]{2,1,0:T(1,128)S(1)}) custom-call(f32[16,128]{1,0:T(8,128)S(1)} %table.1.table_ref, f32[2,56,128]{2,1,0:T(8,128)S(1)} %get-tuple-element.14.refs_0_.ext_ref, f32[3,56,128]{2,1,0:T(8,128)S(1)} %get-tuple-element.15.refs_0_, ...), custom_call_target="tpu_custom_call" | custom-call | tf_op jit(solution)/shard_map/basis/pallas_call | solution.py:486
  29.4 9.3 %all_to_all.11.sums_ref = f32[32,1,128]{2,1,0:T(1,128)S(1)} all-to-all(f32[32,1,128]{2,1,0:T(1,128)S(1)} %get-tuple-element.19), channel_id=1, replica_groups=mesh['row'=8,'col'=4] {'row','col'}, dimensions={0} | all-to-all | bytes 32768 | tf_op jit(solution)/shard_map/all_to_all | solution.py:499
  38.6 0.9 %finish.1 = (f32[2,48,96]{2,1,0:T(8,128)}, f32[2,48,96]{2,1,0:T(8,128)}, f32[12,48,96]{2,1,0:T(8,128)}) custom-call(f32[16,128]{1,0:T(8,128)S(1)} %table.1.table_ref, f32[32,1,128]{2,1,0:T(1,128)S(1)} %all_to_all.11.sums_ref, f32[2,48,96]{2,1,0:T(8,128)S(1)} %copy-done, f32[3,2,48,96]{3,2,1,0:T(8,128)S(1)} %get-tuple-element.20.basis_ref, ...), custom_call_target="tpu_custom_call" | custom-call | tf_op jit(solution)/shard_map/finish/pallas_call | solution.py:500
Async XLA Ops:
  3.9 17.8 %copy-start = (f32[2,48,96]{2,1,0:T(8,128)S(1)}, f32[2,48,96]{2,1,0:T(8,128)}, u32[]{:S(2)}) copy-start(f32[2,48,96]{2,1,0:T(8,128)} %field_ref.5) | copy-start | bytes 110596
  22.3 4.6 %collective-permute-start.1 = (f32[3,56,128]{2,1,0:T(8,128)S(1)}, f32[3,56,128]{2,1,0:T(8,128)S(1)}, u32[]{:S(2)}, u32[]{:S(2)}) collective-permute-start(f32[3,56,128]{2,1,0:T(8,128)S(1)} %get-tuple-element.17), channel_id=1, source_target_pairs={{0,2},{1,3},{2,0},{3,1},{4,6},{5,7},{6,4},{7,5},{8,10},{9,11},{10,... | collective-permute-start | bytes 258056 | tf_op jit(solution)/shard_map/ppermute | solution.py:473
  23.9 4.8 %collective-permute-start.2 = (f32[3,56,128]{2,1,0:T(8,128)S(1)}, f32[3,56,128]{2,1,0:T(8,128)S(1)}, u32[]{:S(2)}, u32[]{:S(2)}) collective-permute-start(f32[3,56,128]{2,1,0:T(8,128)S(1)} %get-tuple-element.18), channel_id=1, source_target_pairs={{0,3},{1,2},{2,1},{3,0},{4,7},{5,6},{6,5},{7,4},{8,11},{9,10},{10,... | collective-permute-start | bytes 258056 | tf_op jit(solution)/shard_map/ppermute | solution.py:473
  24.4 0.7 %copy-start.1 = (s32[6]{0:T(128)S(1)}, s32[6]{0:T(128)}, u32[]{:S(2)}) copy-start(s32[6]{0:T(128)} %cond_ref.1) | copy-start | bytes 76
  24.4 0.7 %copy-start.2 = (f32[6]{0:T(128)S(1)}, f32[6]{0:T(128)}, u32[]{:S(2)}) copy-start(f32[6]{0:T(128)} %heat_ref.1) | copy-start | bytes 76
  24.4 4.3 %collective-permute-start = (f32[3,56,128]{2,1,0:T(8,128)S(1)}, f32[3,56,128]{2,1,0:T(8,128)S(1)}, u32[]{:S(2)}, u32[]{:S(2)}) collective-permute-start(f32[3,56,128]{2,1,0:T(8,128)S(1)} %get-tuple-element.16), channel_id=1, source_target_pairs={{0,1},{1,0},{2,3},{3,2},{4,5},{5,4},{6,7},{7,6},{8,9},{9,8},{10,11... | collective-permute-start | bytes 258056 | tf_op jit(solution)/shard_map/ppermute | solution.py:473

commit v5 on v4

--- a/solution.py
+++ b/solution.py
@@ -20,7 +20,7 @@
 FULL = 63 * 1024 * 1024
 TINY = 1e-30
 F32 = jnp.float32
-EXACT = lax.Precision.HIGHEST
+EXACT = lax.Precision.HIGH
 
 
 def tiles(cells):
@@ -51,6 +51,7 @@
     frac_ref,
     field_ref,
     edges_ref,
+    wide_ref,
     along_ref,
     out_ref,
     sems,
@@ -92,14 +93,18 @@
     columns = jnp.concatenate([start[:, 0:LANES] for start in starts] + [spare], axis=0)
     columns = jnp.transpose(columns)[0 : ROWS + 8]
     ends = pltpu.roll(columns, ROWS + 7, 0)
-    row = lax.broadcasted_iota(jnp.int32, (ROWS, columns.shape[1]), 0)
-    block = lax.broadcasted_iota(jnp.int32, (ROWS, columns.shape[1]), 1)
-    inside = (row < jnp.where(block == row_count - 1, TBLK, TBLK + RIM)) | (
-        (row >= ROWS - RIM) & (block > 0)
-    )
-    tgt_lo = jnp.where(inside, pltpu.roll(columns[0:ROWS], ROWS - RIM, 0), 0.0)
-    tgt_hi = jnp.where(inside, pltpu.roll(ends[0:ROWS], ROWS - RIM, 0), 0.0)
-    inverse = 1.0 / jnp.maximum(tgt_hi - tgt_lo, 1.0)
+    for r in range(row_count):
+        wide_ref[r, 8 : ROWS + 16] = jnp.broadcast_to(columns[:, r : r + 1], (ROWS + 8, LANES))
+    row = lax.broadcasted_iota(jnp.int32, (ROWS, LANES), 0)
+
+    def turned(r, ahead):
+        start = 8 + RIM + ahead
+        last = jnp.where(
+            row[0:8] < 8 - RIM,
+            wide_ref[r, start + ROWS - 8 : start + ROWS],
+            wide_ref[r, start - 8 : start],
+        )
+        return jnp.concatenate([wide_ref[r, start : start + ROWS - 8], last], axis=0)
 
     def weights(src_lo, src_hi, low, high, scale):
         shared = jnp.maximum(jnp.minimum(src_hi, high) - jnp.maximum(src_lo, low), 0.0)
@@ -112,25 +117,6 @@
     weight_x = weights(
         x_lo[:, 0:SBLK], x_hi[:, 0:SBLK], x_tgt_lo, x_tgt_hi, 1.0 / (x_tgt_hi - x_tgt_lo)
     )
-    moves[4].wait()
-    for p in range(pairs):
-        along_ref[p * TBLK : (p + 1) * TBLK, :] = jnp.dot(
-            weight_x, frac_ref[p], precision=EXACT, preferred_element_type=F32
-        )
-    width = 4 * SBLK
-    weights_y = []
-    for q, rows in enumerate(window_rows(row_count)):
-        src_lo = edges_ref[3:4, 2 * q * SBLK : 2 * q * SBLK + width]
-        src_hi = edges_ref[3:4, 2 * q * SBLK + 1 : 2 * q * SBLK + width + 1]
-        weights_y.append(
-            jnp.concatenate(
-                [
-                    weights(src_lo, src_hi, *(a[:, r : r + 1] for a in (tgt_lo, tgt_hi, inverse)))
-                    for r in rows
-                ],
-                axis=0,
-            )
-        )
     moves[5].wait()
     zlayers, height, breadth = field_ref.shape
     base = ROWS + 8
@@ -145,6 +131,27 @@
                 )
                 at = base + 8 * t + RIM * layer
                 out_ref[r, at : at + RIM, 0 : hi - lo] = rim
+    moves[4].wait()
+    for p in range(pairs):
+        along_ref[p * TBLK : (p + 1) * TBLK, :] = jnp.dot(
+            weight_x, frac_ref[p], precision=EXACT, preferred_element_type=F32
+        )
+    width = 4 * SBLK
+    weights_y = []
+    for q, rows in enumerate(window_rows(row_count)):
+        parts = []
+        for r in rows:
+            low, high = turned(r, 0), turned(r, 1)
+            inside = row < (TBLK if r + 1 == row_count else TBLK + RIM)
+            if r:
+                inside = inside | (row >= ROWS - RIM)
+            scale = jnp.where(inside, 1.0 / jnp.maximum(high - low, 1.0), 0.0)
+            wide = []
+            for at in range(2 * q * SBLK, 2 * q * SBLK + width, LANES):
+                src_lo, src_hi = edges_ref[3:4, at : at + LANES], edges_ref[3:4, at + 1 : at + 1 + LANES]
+                wide.append(weights(src_lo, src_hi, low, high, scale))
+            parts.append(jnp.concatenate(wide, axis=1))
+        weights_y.append(jnp.concatenate(parts, axis=0))
     leaving = []
     for q, rows in enumerate(window_rows(row_count)):
         block = lax.dot_general(
@@ -440,6 +447,7 @@
             pltpu.VMEM(fractions_source.shape, F32),
             pltpu.VMEM(thermal_source_term.shape, F32),
             pltpu.VMEM((8, LANES * (tiles(source_cells + 1) + 1)), F32),
+            pltpu.VMEM((row_count, ROWS + 16, LANES), F32),
             pltpu.VMEM((along_rows, source_cells), F32),
             pltpu.VMEM(outgoing.shape, F32),
             pltpu.SemaphoreType.DMA((6,)),

time: 39.8 us -> 39.2 us (0.985)
  Pallas kernels: 6.1 us -> 5.53 us
    pallas_call x1, Pallas kernels: 3.27 us -> 2.7 us  [per_device(): pl.pallas_call(functools.partial(rezone_kernel, row_count), out_shape=out...]
where the time goes in v5:
time: 39.2 us; the launch traced here: 38.9 us
  blocking collectives  27 us (69%)
  Pallas kernels  5.53 us (14%)
  waiting for transfers between devices  3.42 us (9%)
  starting transfers between devices  2.27 us (6%)
  between operations  0.69 us (2%)
    all_to_all x1, blocking collectives, per_device(): lax.all_to_all(outgoing, 'row', split_axis=0, concat_axis=0, tiled=True)  17.8 us
    all_to_all x1, blocking collectives, per_device(): lax.all_to_all(sums, ('row', 'col'), split_axis=0, concat_axis=0, tiled=T...  9.25 us
    ppermute x3, waiting for transfers between devices, swap(): return lax.ppermute(part, 'col', [(c, c ^ mask) for c in range(col_count)])  3.42 us
    pallas_call x1, Pallas kernels, per_device(): pl.pallas_call(functools.partial(rezone_kernel, row_count), out_shape=out...  2.7 us
    ppermute x3, starting transfers between devices, swap(): return lax.ppermute(part, 'col', [(c, c ^ mask) for c in range(col_count)])  2.27 us
    pallas_call x1, Pallas kernels, per_device(): pl.pallas_call(finish_kernel, out_shape=[jax.ShapeDtypeStruct((zlayers, h...  0.87 us
  transfers between devices with their start and end apart: 3, of which 2 were waited for; matrix products, arithmetic and copies ran while one was open for 0% of the time, Pallas kernels for 2%

profile of v5, /device:TPU:0, one launch (start us, length us, event | category | flops | bytes accessed | tf_op | source)
XLA Modules:
  0.0 38.9 jit_solution(4840337126070723335)
XLA Ops:
  0.6 2.7 %rezone.1 = f32[8,72,128]{2,1,0:T(8,128)} custom-call(s32[513]{0:T(1024)} %xs_hbm.1, s32[385]{0:T(512)} %xt_hbm.1, s32[513]{0:T(1024)} %ys_hbm.1, s32[385]{0:T(512)} %yt_hbm.1, f32[3,64,512]{2,1,0:T(8,128)} %frac_hbm.1, f32[2,48,96]{2,1,0:T(8,128)} %field_ref.5), custom_call_target="tpu_custom_call" | custom-call | tf_op jit(solution)/shard_map/rezone/pallas_call | solution.py:440
  3.3 0.0 copy-start
  3.3 17.8 %all_to_all.10.got_ref = f32[8,72,128]{2,1,0:T(8,128)S(1)} all-to-all(f32[8,72,128]{2,1,0:T(8,128)} %rezone.1), channel_id=1, replica_groups=mesh['row'=8,'col'=4] {'row'}, dimensions={0} | all-to-all | bytes 589824 | tf_op jit(solution)/shard_map/all_to_all | solution.py:459
  21.1 0.0 copy-done
  21.1 0.6 %regroup_far.1 = (f32[2,56,128]{2,1,0:T(8,128)S(1)}, f32[3,56,128]{2,1,0:T(8,128)S(1)}, f32[3,56,128]{2,1,0:T(8,128)S(1)}) custom-call(f32[8,72,128]{2,1,0:T(8,128)S(1)} %all_to_all.10.got_ref, f32[2,48,96]{2,1,0:T(8,128)S(1)} %copy-done), custom_call_target="tpu_custom_call" | custom-call | tf_op jit(solution)/shard_map/regroup_far/pallas_call | solution.py:471
  21.8 1.6 %collective-permute-start.1 = (f32[3,56,128]{2,1,0:T(8,128)S(1)}, f32[3,56,128]{2,1,0:T(8,128)S(1)}, u32[]{:S(2)}, u32[]{:S(2)}) collective-permute-start(f32[3,56,128]{2,1,0:T(8,128)S(1)} %get-tuple-element.17), channel_id=1, source_target_pairs={{0,2},{1,3},{2,0},{3,1},{4,6},{5,7},{6,4},{7,5},{8,10},{9,11},{10,... | collective-permute-start | bytes 258056 | tf_op jit(solution)/shard_map/ppermute | solution.py:481
  23.3 0.0 collective-permute-start.2
  23.3 0.5 %regroup_near.1 = (f32[3,56,128]{2,1,0:T(8,128)S(1)}, f32[3,56,128]{2,1,0:T(8,128)S(1)}) custom-call(f32[8,72,128]{2,1,0:T(8,128)S(1)} %all_to_all.10.got_ref, f32[2,48,96]{2,1,0:T(8,128)S(1)} %copy-done, f32[2,56,128]{2,1,0:T(8,128)S(1)} %get-tuple-element.14.refs_0_.ext_ref), custom_call_target="tpu_custom_call" | custom-call | flops 1000000 | bytes 2000000 | tf_op jit(solution)/shard_map/regroup_near/pallas_call | solution.py:484
  23.8 0.0 copy-start.1
  23.8 0.0 copy-start.2
  23.8 0.7 %collective-permute-start = (f32[3,56,128]{2,1,0:T(8,128)S(1)}, f32[3,56,128]{2,1,0:T(8,128)S(1)}, u32[]{:S(2)}, u32[]{:S(2)}) collective-permute-start(f32[3,56,128]{2,1,0:T(8,128)S(1)} %get-tuple-element.16), channel_id=1, source_target_pairs={{0,1},{1,0},{2,3},{3,2},{4,5},{5,4},{6,7},{7,6},{8,9},{9,8},{10,11... | collective-permute-start | bytes 258056 | tf_op jit(solution)/shard_map/ppermute | solution.py:481
  24.6 0.0 copy-done.1
  24.6 0.0 copy-done.2
  24.6 0.1 table.1.table_ref
  24.7 1.6 %collective-permute-done.1.refs_2_ = f32[3,56,128]{2,1,0:T(8,128)S(1)} collective-permute-done((f32[3,56,128]{2,1,0:T(8,128)S(1)}, f32[3,56,128]{2,1,0:T(8,128)S(1)}, u32[]{:S(2)}, u32[]{:S(2)}) %collective-permute-start.1) | collective-permute-done | bytes 86048 | tf_op jit(solution)/shard_map/ppermute | solution.py:481
  26.3 1.8 %collective-permute-done.2.refs_3_ = f32[3,56,128]{2,1,0:T(8,128)S(1)} collective-permute-done((f32[3,56,128]{2,1,0:T(8,128)S(1)}, f32[3,56,128]{2,1,0:T(8,128)S(1)}, u32[]{:S(2)}, u32[]{:S(2)}) %collective-permute-start.2) | collective-permute-done | bytes 86048 | tf_op jit(solution)/shard_map/ppermute | solution.py:481
  28.1 0.0 collective-permute-done.refs_1_
  28.1 0.7 %basis.1 = (f32[12,48,96]{2,1,0:T(8,128)S(1)}, f32[3,2,48,96]{3,2,1,0:T(8,128)S(1)}, f32[32,1,128]{2,1,0:T(1,128)S(1)}) custom-call(f32[16,128]{1,0:T(8,128)S(1)} %table.1.table_ref, f32[2,56,128]{2,1,0:T(8,128)S(1)} %get-tuple-element.14.refs_0_.ext_ref, f32[3,56,128]{2,1,0:T(8,128)S(1)} %get-tuple-element.15.refs_0_, ...), custom_call_target="tpu_custom_call" | custom-call | tf_op jit(solution)/shard_map/basis/pallas_call | solution.py:494
  28.8 9.3 %all_to_all.11.sums_ref = f32[32,1,128]{2,1,0:T(1,128)S(1)} all-to-all(f32[32,1,128]{2,1,0:T(1,128)S(1)} %get-tuple-element.19), channel_id=1, replica_groups=mesh['row'=8,'col'=4] {'row','col'}, dimensions={0} | all-to-all | bytes 32768 | tf_op jit(solution)/shard_map/all_to_all | solution.py:507
  38.1 0.9 %finish.1 = (f32[2,48,96]{2,1,0:T(8,128)}, f32[2,48,96]{2,1,0:T(8,128)}, f32[12,48,96]{2,1,0:T(8,128)}) custom-call(f32[16,128]{1,0:T(8,128)S(1)} %table.1.table_ref, f32[32,1,128]{2,1,0:T(1,128)S(1)} %all_to_all.11.sums_ref, f32[2,48,96]{2,1,0:T(8,128)S(1)} %copy-done, f32[3,2,48,96]{3,2,1,0:T(8,128)S(1)} %get-tuple-element.20.basis_ref, ...), custom_call_target="tpu_custom_call" | custom-call | tf_op jit(solution)/shard_map/finish/pallas_call | solution.py:508
Async XLA Ops:
  3.3 17.8 %copy-start = (f32[2,48,96]{2,1,0:T(8,128)S(1)}, f32[2,48,96]{2,1,0:T(8,128)}, u32[]{:S(2)}) copy-start(f32[2,48,96]{2,1,0:T(8,128)} %field_ref.5) | copy-start | bytes 110596
  21.8 4.6 %collective-permute-start.1 = (f32[3,56,128]{2,1,0:T(8,128)S(1)}, f32[3,56,128]{2,1,0:T(8,128)S(1)}, u32[]{:S(2)}, u32[]{:S(2)}) collective-permute-start(f32[3,56,128]{2,1,0:T(8,128)S(1)} %get-tuple-element.17), channel_id=1, source_target_pairs={{0,2},{1,3},{2,0},{3,1},{4,6},{5,7},{6,4},{7,5},{8,10},{9,11},{10,... | collective-permute-start | bytes 258056 | tf_op jit(solution)/shard_map/ppermute | solution.py:481
  23.3 4.8 %collective-permute-start.2 = (f32[3,56,128]{2,1,0:T(8,128)S(1)}, f32[3,56,128]{2,1,0:T(8,128)S(1)}, u32[]{:S(2)}, u32[]{:S(2)}) collective-permute-start(f32[3,56,128]{2,1,0:T(8,128)S(1)} %get-tuple-element.18), channel_id=1, source_target_pairs={{0,3},{1,2},{2,1},{3,0},{4,7},{5,6},{6,5},{7,4},{8,11},{9,10},{10,... | collective-permute-start | bytes 258056 | tf_op jit(solution)/shard_map/ppermute | solution.py:481
  23.8 0.7 %copy-start.1 = (s32[6]{0:T(128)S(1)}, s32[6]{0:T(128)}, u32[]{:S(2)}) copy-start(s32[6]{0:T(128)} %cond_ref.1) | copy-start | bytes 76
  23.8 0.7 %copy-start.2 = (f32[6]{0:T(128)S(1)}, f32[6]{0:T(128)}, u32[]{:S(2)}) copy-start(f32[6]{0:T(128)} %heat_ref.1) | copy-start | bytes 76
  23.8 4.3 %collective-permute-start = (f32[3,56,128]{2,1,0:T(8,128)S(1)}, f32[3,56,128]{2,1,0:T(8,128)S(1)}, u32[]{:S(2)}, u32[]{:S(2)}) collective-permute-start(f32[3,56,128]{2,1,0:T(8,128)S(1)} %get-tuple-element.16), channel_id=1, source_target_pairs={{0,1},{1,0},{2,3},{3,2},{4,5},{5,4},{6,7},{7,6},{8,9},{9,8},{10,11... | collective-permute-start | bytes 258056 | tf_op jit(solution)/shard_map/ppermute | solution.py:481

commit v6 on v5

--- a/solution.py
+++ b/solution.py
@@ -14,17 +14,50 @@
 RIM = ITERS
 ROWS = 56
 LANES = 128
-GROUPS = ROWS // 8
-TAIL = LANES // GROUPS // 8 * 8
+EDGE = ROWS - TBLK
+GROUPS = TBLK // 8
+TAIL = 16
+CHUNK = LANES - GROUPS * TAIL
+BODY = ROWS + 8
 VMEM = 48 * 1024 * 1024
 FULL = 63 * 1024 * 1024
 TINY = 1e-30
 F32 = jnp.float32
-EXACT = lax.Precision.HIGH
+EXACT = lax.Precision.HIGHEST
 
 
 def tiles(cells):
     return -(-cells // LANES)
+
+
+def compact(breadth):
+    return breadth == 3 * CHUNK
+
+
+def pack_rims(rims):
+    count = rims.shape[0]
+    side = jnp.zeros((count, LANES - CHUNK), F32)
+    below = jnp.zeros((8 - count, LANES), F32)
+    tail = jnp.concatenate([side, rims[:, 0:CHUNK]], axis=1)
+    edge = jnp.concatenate([side, rims[:, CHUNK : 2 * CHUNK]], axis=1)
+    lines = []
+    for at in (0, RIM):
+        parts = [rims[at + n : at + n + 1, 2 * CHUNK :] for n in range(RIM)]
+        lines.append(jnp.concatenate(parts + [jnp.zeros((1, CHUNK), F32)], axis=1))
+    gap = [jnp.zeros((RIM, LANES), F32)] + lines + [jnp.zeros((EDGE - RIM - 2, LANES), F32)]
+    return (
+        jnp.concatenate([tail, below], axis=0),
+        jnp.concatenate([edge, below], axis=0) + jnp.concatenate(gap, axis=0),
+    )
+
+
+def unpack_rims(tail, edge, count):
+    last = [
+        edge[RIM + n // RIM : RIM + n // RIM + 1, CHUNK * (n % RIM) : CHUNK * (n % RIM + 1)]
+        for n in range(count)
+    ]
+    parts = [tail[0:count, LANES - CHUNK :], edge[0:count, LANES - CHUNK :]]
+    return jnp.concatenate(parts + [jnp.concatenate(last, axis=0)], axis=1)
 
 
 def window_rows(row_count):
@@ -41,6 +74,8 @@
     xt_hbm,
     ys_hbm,
     yt_hbm,
+    cond_hbm,
+    heat_hbm,
     frac_hbm,
     field_hbm,
     out_hbm,
@@ -48,6 +83,8 @@
     xt_ref,
     ys_ref,
     yt_ref,
+    cond_ref,
+    heat_ref,
     frac_ref,
     field_ref,
     edges_ref,
@@ -69,13 +106,16 @@
                 (ys_hbm, ys_ref),
                 (frac_hbm, frac_ref),
                 (field_hbm, field_ref),
+                (cond_hbm, cond_ref),
+                (heat_hbm, heat_ref),
             )
         )
     ]
     for move in moves:
         move.start()
     edges_ref[...] = jnp.zeros_like(edges_ref)
-    along_ref[pairs * TBLK :, :] = jnp.zeros_like(along_ref[pairs * TBLK :, :])
+    used = (pairs + 2) * TBLK
+    along_ref[used:, :] = jnp.zeros_like(along_ref[used:, :])
     for n, ref in enumerate((yt_ref, xt_ref, xs_ref, ys_ref)):
         moves[n].wait()
         edges_ref[n : n + 1, 0 : ref.shape[0]] = ref[...].astype(F32)[None, :]
@@ -111,6 +151,7 @@
         return shared * scale
 
     mine = slice(row_count, row_count + 1)
+    lane = lax.broadcasted_iota(jnp.int32, (1, LANES), 1)
     x_lo = from_here(2, me * SBLK, 0)
     x_hi = pltpu.roll(x_lo, 2 * LANES - 1, 1)
     x_tgt_lo, x_tgt_hi = columns[0:TBLK, mine], ends[0:TBLK, mine]
@@ -118,24 +159,40 @@
         x_lo[:, 0:SBLK], x_hi[:, 0:SBLK], x_tgt_lo, x_tgt_hi, 1.0 / (x_tgt_hi - x_tgt_lo)
     )
     moves[5].wait()
+    moves[6].wait()
+    moves[7].wait()
     zlayers, height, breadth = field_ref.shape
-    base = ROWS + 8
-    for r in range(row_count):
-        for t in range(tiles(breadth)):
-            lo, hi = t * LANES, min((t + 1) * LANES, breadth)
-            for layer in range(zlayers):
-                rim = jnp.where(
-                    r > me,
-                    field_ref[layer, height - RIM :, lo:hi],
-                    field_ref[layer, :RIM, lo:hi],
-                )
-                at = base + 8 * t + RIM * layer
-                out_ref[r, at : at + RIM, 0 : hi - lo] = rim
+    rims = []
+    for rows in (slice(0, RIM), slice(height - RIM, height)):
+        rims.append(jnp.concatenate([field_ref[layer, rows] for layer in range(zlayers)], axis=0))
+    if compact(breadth):
+        rims = [pack_rims(rim) for rim in rims]
+    else:
+        for r in range(row_count):
+            rim = jnp.where(r > me, rims[1], rims[0])
+            for t in range(tiles(breadth)):
+                lo, hi = t * LANES, min((t + 1) * LANES, breadth)
+                at = BODY + 8 * t
+                out_ref[r, at : at + zlayers * RIM, 0 : hi - lo] = rim[:, lo:hi]
+    resistance = 16.0 / cond_ref[...].astype(F32)[None, :]
+    material = lax.broadcasted_iota(jnp.int32, (1, M), 1)
+    factors = []
+    for p in range(pairs):
+        mine = material == lax.rem(lax.axis_index("col") * pairs + p, M)
+        factors.append(
+            [
+                jnp.sum(jnp.where(mine, value, 0.0), axis=1, keepdims=True)
+                for value in (resistance, heat_ref[...][None, :])
+            ]
+        )
     moves[4].wait()
+    partial = [0.0, 0.0]
     for p in range(pairs):
-        along_ref[p * TBLK : (p + 1) * TBLK, :] = jnp.dot(
-            weight_x, frac_ref[p], precision=EXACT, preferred_element_type=F32
-        )
+        along = jnp.dot(weight_x, frac_ref[p], precision=EXACT, preferred_element_type=F32)
+        along_ref[p * TBLK : (p + 1) * TBLK, :] = along
+        partial = [total + factor * along for total, factor in zip(partial, factors[p])]
+    for n, total in enumerate(partial):
+        along_ref[(pairs + n) * TBLK : (pairs + n + 1) * TBLK, :] = total
     width = 4 * SBLK
     weights_y = []
     for q, rows in enumerate(window_rows(row_count)):
@@ -163,11 +220,18 @@
         )
         for n, r in enumerate(rows):
             mine = block[n * ROWS : (n + 1) * ROWS]
-            out_ref[r, 0:ROWS, :] = mine[:, 0:LANES]
-            packed = mine[0:8, LANES:]
+            out_ref[r, 0:TBLK, :] = mine[0:TBLK, 0:LANES]
+            packed = jnp.where(lane < TAIL, mine[0:8, LANES:], 0.0)
             for g in range(1, GROUPS):
-                packed = packed + pltpu.roll(mine[8 * g : 8 * g + 8, LANES:], TAIL * g, 1)
-            out_ref[r, ROWS : ROWS + 8, :] = packed
+                group = jnp.where(lane < TAIL, mine[8 * g : 8 * g + 8, LANES:], 0.0)
+                packed = packed + pltpu.roll(group, TAIL * g, 1)
+            edge = pltpu.roll(mine[TBLK:ROWS, LANES:], LANES - TAIL, 1)
+            edge = jnp.where(lane < 2 * TBLK, edge, 0.0)
+            if compact(breadth):
+                packed = packed + jnp.where(r > me, rims[1][0], rims[0][0])
+                edge = edge + jnp.where(r > me, rims[1][1], rims[0][1])
+            out_ref[r, TBLK : TBLK + 8, :] = packed
+            out_ref[r, ROWS:BODY, :] = edge
         done = pl.ds(rows[0], len(rows))
         leaving.append(pltpu.make_async_copy(out_ref.at[done], out_hbm.at[done], out_sems.at[q]))
         leaving[-1].start()
@@ -189,75 +253,90 @@
 def extend_rows(row_count, got_ref, field_ref, ext_ref):
     my_row = lax.axis_index("row")
     zlayers, height, breadth = field_ref.shape
-    base = ROWS + 8
     ext_ref[...] = jnp.zeros_like(ext_ref)
     below, above = jnp.maximum(my_row - 1, 0), jnp.minimum(my_row + 1, row_count - 1)
+    count = zlayers * RIM
+    for block, there, at in (
+        (above, my_row < row_count - 1, height),
+        (below, my_row > 0, ROWS - RIM),
+    ):
+        if compact(breadth):
+            rims = unpack_rims(got_ref[block, TBLK : TBLK + 8], got_ref[block, ROWS:BODY], count)
+        else:
+            parts = [got_ref[block, BODY + 8 * t : BODY + 8 * t + count] for t in range(tiles(breadth))]
+            rims = jnp.concatenate(parts, axis=1)[:, 0:breadth]
+        rims = jnp.where(there, rims, 0.0)
+        for layer in range(zlayers):
+            ext_ref[layer, at : at + RIM, 0:breadth] = rims[layer * RIM : (layer + 1) * RIM]
     for layer in range(zlayers):
         ext_ref[layer, 0:height, 0:breadth] = field_ref[layer]
-        for t in range(tiles(breadth)):
-            lo, hi = t * LANES, min((t + 1) * LANES, breadth)
-            at = base + 8 * t + RIM * layer
-            after = got_ref[above, at : at + RIM, 0 : hi - lo]
-            before = got_ref[below, at : at + RIM, 0 : hi - lo]
-            ext_ref[layer, height : height + RIM, lo:hi] = jnp.where(
-                my_row < row_count - 1, after, 0.0
-            )
-            ext_ref[layer, ROWS - RIM : ROWS, lo:hi] = jnp.where(my_row > 0, before, 0.0)
 
 
 def regroup_kernel(row_count, col_count, masks, got_ref, field_ref, *refs):
     my_col = lax.axis_index("col")
     zlayers, _, breadth = field_ref.shape
     ext_ref, out_refs = refs[0], refs[1:]
-    pairs, _, width = out_refs[0].shape
+    width = out_refs[0].shape[1]
+    pairs = out_refs[0].shape[0] // TBLK
     per_col = row_count // col_count
     if col_count // 2 in masks:
         extend_rows(row_count, got_ref, field_ref, ext_ref)
 
-    def piece(block, pair, first, last):
-        start = pair * TBLK
-        lo, hi = start + first, start + last
+    def own(block, pair, first, last):
+        lo, hi = pair * TBLK + first, pair * TBLK + last
         parts = []
         if lo < LANES:
-            parts.append(got_ref[block, 0:ROWS, lo : min(hi, LANES)])
+            parts.append(got_ref[block, 0:TBLK, lo : min(hi, LANES)])
         if hi > LANES:
             a, b = max(lo, LANES) - LANES, hi - LANES
-            tail = got_ref[block, ROWS : ROWS + 8, :]
+            tail = got_ref[block, TBLK : TBLK + 8, :]
             parts.append(
                 jnp.concatenate([tail[:, TAIL * g + a : TAIL * g + b] for g in range(GROUPS)], axis=0)
             )
         return parts[0] if len(parts) == 1 else jnp.concatenate(parts, axis=1)
 
+    def edge(block, which, first, last):
+        return got_ref[block, ROWS:BODY, which * TBLK + first : which * TBLK + last]
+
     for mask, out_ref in zip(masks, out_refs):
         c = my_col ^ mask
-        first = c * per_col
-        left, right = jnp.maximum(first - 1, 0), jnp.minimum(first + per_col, row_count - 1)
-        for p in range(pairs):
-            parts = [piece(first + j, p, 0, TBLK) for j in range(per_col)]
-            parts.append(jnp.where(c < col_count - 1, piece(right, p, 0, RIM), 0.0))
-            if p < zlayers and mask:
-                whole = ext_ref[p]
+        start = c * per_col
+        left, right = jnp.maximum(start - 1, 0), jnp.minimum(start + per_col, row_count - 1)
+
+        def line(cells, rows, kind, layer):
+            parts = [cells(start + j, kind, 0, TBLK) for j in range(per_col)]
+            count = parts[0].shape[0]
+            parts.append(jnp.where(c < col_count - 1, cells(right, kind, 0, RIM), 0.0))
+            if layer < zlayers and mask:
+                whole = ext_ref[layer, rows]
                 parts.append(
                     jnp.where(c > my_col, whole[:, breadth - RIM : breadth], whole[:, 0:RIM])
                 )
             else:
-                parts.append(jnp.zeros((ROWS, RIM), F32))
-            parts.append(jnp.zeros((ROWS, width - breadth - 3 * RIM), F32))
-            parts.append(jnp.where(c > 0, piece(left, p, TBLK - RIM, TBLK), 0.0))
-            out_ref[p] = jnp.concatenate(parts, axis=1)
+                parts.append(jnp.zeros((count, RIM), F32))
+            parts.append(jnp.zeros((count, width - breadth - 3 * RIM), F32))
+            parts.append(jnp.where(c > 0, cells(left, kind, TBLK - RIM, TBLK), 0.0))
+            return jnp.concatenate(parts, axis=1)
+
+        for p in range(pairs):
+            out_ref[p * TBLK : (p + 1) * TBLK] = line(own, slice(0, TBLK), p, p)
+        for n in range(2):
+            at = pairs * TBLK + EDGE * n
+            out_ref[at : at + EDGE] = line(edge, slice(TBLK, ROWS), n, n)
 
 
 def basis_kernel(col_count, height, breadth, table_ref, ext_ref, *refs):
     arrivals, refs = refs[:col_count], refs[col_count:]
     shares_ref, basis_ref, sums_ref, got_ref = refs
     my_col = lax.axis_index("col")
+    pairs = arrivals[0].shape[0] // TBLK
     for mask, arrival in enumerate(arrivals):
         got_ref[my_col ^ mask] = arrival[...]
-        for p in range(arrival.shape[0]):
-            at = (my_col ^ mask) * arrival.shape[0] + p
-            shares_ref[at] = arrival[p, 0:height, 0:breadth]
+        for p in range(pairs):
+            at = (my_col ^ mask) * pairs + p
+            shares_ref[at] = arrival[p * TBLK : (p + 1) * TBLK, 0:breadth]
     zlayers = ext_ref.shape[0]
-    pairs, rows, width = got_ref.shape[1:]
+    rows, width = ext_ref.shape[1:]
     lane = lax.broadcasted_iota(jnp.int32, (rows, width), 1)
     before, after = jnp.maximum(my_col - 1, 0), jnp.minimum(my_col + 1, col_count - 1)
 
@@ -273,19 +352,38 @@
     def entry(n):
         return table_ref[n : n + 1, 0:1]
 
+    row = lax.broadcasted_iota(jnp.int32, (rows, width), 0)
+    inside = ((lane < breadth + RIM) | (lane >= width - RIM)) & (
+        (row < TBLK + RIM) | (row >= ROWS - RIM)
+    )
+
     cell_k, heat, field = [], [], []
     for z in range(zlayers):
-        inverse = jnp.zeros((rows, width), F32)
-        total = jnp.zeros((rows, width), F32)
+        inverse, total = 0.0, 0.0
         for m in range(M):
             c, p = divmod(z * M + m, pairs)
-            share = got_ref[c, p]
-            inside = jnp.where((lane < breadth + RIM) | (lane >= width - RIM), share, 0.0)
-            inverse = inverse + inside * entry(m)
-            total = total + inside * entry(M + m)
+            share = got_ref[c, p * TBLK : (p + 1) * TBLK]
+            inverse = inverse + share * entry(m)
+            total = total + share * entry(M + m)
+        edge_inverse, edge_total = 0.0, 0.0
+        for c in range(z * M // pairs, (z + 1) * M // pairs):
+            edge_inverse = edge_inverse + got_ref[c, pairs * TBLK : pairs * TBLK + EDGE]
+            edge_total = edge_total + got_ref[c, pairs * TBLK + EDGE :]
+        inverse = jnp.concatenate([inverse, edge_inverse], axis=0)
+        total = jnp.concatenate([total, edge_total], axis=0)
+        inverse, total = (jnp.where(inside, value, 0.0) for value in (inverse, total))
         cell_k.append(jnp.where(inverse > 0.0, 1.0 / jnp.where(inverse > 0.0, inverse, 1.0), 0.0))
         heat.append(total)
-        left, right = got_ref[before, z], got_ref[after, z]
+        left, right = (
+            jnp.concatenate(
+                [
+                    got_ref[c, z * TBLK : (z + 1) * TBLK],
+                    got_ref[c, pairs * TBLK + EDGE * z : pairs * TBLK + EDGE * (z + 1)],
+                ],
+                axis=0,
+            )
+            for c in (before, after)
+        )
         left = pltpu.roll(left, width - (breadth + 2 * RIM), 1)
         right = pltpu.roll(right, width - RIM, 1)
         value = ext_ref[z]
@@ -429,20 +527,27 @@
     pairs, _, source_cells = fractions_source.shape
     zlayers, height, breadth = thermal_source_term.shape
     width = LANES * tiles(breadth + 4 * RIM)
-    send_rows = ROWS + 8 + 8 * tiles(breadth)
+    send_rows = BODY + (0 if compact(breadth) else 8 * tiles(breadth))
     params = pltpu.CompilerParams(vmem_limit_bytes=VMEM)
 
     vmem = pl.BlockSpec(memory_space=pltpu.VMEM)
     hbm = pl.BlockSpec(memory_space=pltpu.HBM)
-    along_rows = -(-pairs * TBLK // LANES) * LANES
-    edges = [x_source_edges, x_target_edges, y_source_edges, y_target_edges]
+    along_rows = -(-(pairs + 2) * TBLK // LANES) * LANES
+    small = [
+        x_source_edges,
+        x_target_edges,
+        y_source_edges,
+        y_target_edges,
+        conductivity_table,
+        capacity,
+    ]
     outgoing = jax.ShapeDtypeStruct((row_count, send_rows, LANES), F32)
     outgoing = pl.pallas_call(
         functools.partial(rezone_kernel, row_count),
         out_shape=outgoing,
-        in_specs=[hbm] * 6,
+        in_specs=[hbm] * 8,
         out_specs=hbm,
-        scratch_shapes=[pltpu.VMEM(e.shape, e.dtype) for e in edges]
+        scratch_shapes=[pltpu.VMEM(e.shape, e.dtype) for e in small]
         + [
             pltpu.VMEM(fractions_source.shape, F32),
             pltpu.VMEM(thermal_source_term.shape, F32),
@@ -450,12 +555,12 @@
             pltpu.VMEM((row_count, ROWS + 16, LANES), F32),
             pltpu.VMEM((along_rows, source_cells), F32),
             pltpu.VMEM(outgoing.shape, F32),
-            pltpu.SemaphoreType.DMA((6,)),
+            pltpu.SemaphoreType.DMA((8,)),
             pltpu.SemaphoreType.DMA((row_count // 2 - 1,)),
         ],
         compiler_params=pltpu.CompilerParams(vmem_limit_bytes=FULL),
         name="rezone",
-    )(*edges, fractions_source, thermal_source_term)
+    )(*small, fractions_source, thermal_source_term)
     arrived = lax.all_to_all(outgoing, "row", split_axis=0, concat_axis=0, tiled=True)
     table = pl.pallas_call(
         table_kernel,
@@ -465,7 +570,7 @@
         compiler_params=params,
         name="table",
     )(conductivity_table, capacity)
-    message = jax.ShapeDtypeStruct((pairs, ROWS, width), F32)
+    message = jax.ShapeDtypeStruct((pairs * TBLK + 2 * EDGE, width), F32)
     half = col_count // 2
     near, far = range(half), range(half, col_count)
     extended, *far_parts = pl.pallas_call(

time: 39.2 us -> 39 us (level)
  blocking collectives: 27 us -> 26.3 us
  Pallas kernels: 5.53 us -> 6.11 us
    all_to_all x1, blocking collectives: 17.8 us -> 16.3 us  [per_device(): lax.all_to_all(outgoing, 'row', split_axis=0, concat_axis=0, tiled=True)]
    all_to_all x1, blocking collectives: 9.25 us -> 9.95 us  [per_device(): lax.all_to_all(sums, ('row', 'col'), split_axis=0, concat_axis=0, tiled=T...]
    pallas_call x1, Pallas kernels: 2.7 us -> 3.28 us  [per_device(): pl.pallas_call(functools.partial(rezone_kernel, row_count), out_shape=out...]
where the time goes in v6:
time: 39 us; the launch traced here: 38.7 us
  blocking collectives  26.3 us (67%)
  Pallas kernels  6.11 us (16%)
  waiting for transfers between devices  3.32 us (9%)
  starting transfers between devices  2.27 us (6%)
  between operations  0.69 us (2%)
    all_to_all x1, blocking collectives, per_device(): lax.all_to_all(outgoing, 'row', split_axis=0, concat_axis=0, tiled=True)  16.3 us
    all_to_all x1, blocking collectives, per_device(): lax.all_to_all(sums, ('row', 'col'), split_axis=0, concat_axis=0, tiled=T...  9.95 us
    ppermute x3, waiting for transfers between devices, swap(): return lax.ppermute(part, 'col', [(c, c ^ mask) for c in range(col_count)])  3.32 us
    pallas_call x1, Pallas kernels, per_device(): pl.pallas_call(functools.partial(rezone_kernel, row_count), out_shape=out...  3.28 us
    ppermute x3, starting transfers between devices, swap(): return lax.ppermute(part, 'col', [(c, c ^ mask) for c in range(col_count)])  2.27 us
    pallas_call x1, Pallas kernels, per_device(): pl.pallas_call(finish_kernel, out_shape=[jax.ShapeDtypeStruct((zlayers, h...  0.87 us
  transfers between devices with their start and end apart: 3, of which 2 were waited for; matrix products, arithmetic and copies ran while one was open for 0% of the time, Pallas kernels for 2%

profile of v6, /device:TPU:0, one launch (start us, length us, event | category | flops | bytes accessed | tf_op | source)
XLA Modules:
  0.0 38.7 jit_solution(154594342348230295)
XLA Ops:
  0.6 3.3 %rezone.1 = f32[8,64,128]{2,1,0:T(8,128)} custom-call(s32[513]{0:T(1024)} %xs_hbm.1, s32[385]{0:T(512)} %xt_hbm.1, s32[513]{0:T(1024)} %ys_hbm.1, s32[385]{0:T(512)} %yt_hbm.1, s32[6]{0:T(128)} %cond_hbm.1, f32[6]{0:T(128)} %heat_hbm.1, f32[3,64,512]{2,1,0:T(8,128)} %frac_hbm.1, f32[2,48,96]{2,1,0:T(8,128)} %field_ref.5), custom_call_target="tpu_custom_call" | custom-call | tf_op jit(solution)/shard_map/rezone/pallas_call | solution.py:545
  3.9 0.0 copy-start
  3.9 16.3 %all_to_all.10.got_ref = f32[8,64,128]{2,1,0:T(8,128)S(1)} all-to-all(f32[8,64,128]{2,1,0:T(8,128)} %rezone.1), channel_id=1, replica_groups=mesh['row'=8,'col'=4] {'row'}, dimensions={0} | all-to-all | bytes 524288 | tf_op jit(solution)/shard_map/all_to_all | solution.py:564
  20.3 0.0 copy-done
  20.3 0.6 %regroup_far.1 = (f32[2,56,128]{2,1,0:T(8,128)S(1)}, f32[160,128]{1,0:T(8,128)S(1)}, f32[160,128]{1,0:T(8,128)S(1)}) custom-call(f32[8,64,128]{2,1,0:T(8,128)S(1)} %all_to_all.10.got_ref, f32[2,48,96]{2,1,0:T(8,128)S(1)} %copy-done), custom_call_target="tpu_custom_call" | custom-call | tf_op jit(solution)/shard_map/regroup_far/pallas_call | solution.py:576
  20.9 1.6 %collective-permute-start.1 = (f32[160,128]{1,0:T(8,128)S(1)}, f32[160,128]{1,0:T(8,128)S(1)}, u32[]{:S(2)}, u32[]{:S(2)}) collective-permute-start(f32[160,128]{1,0:T(8,128)S(1)} %get-tuple-element.17), channel_id=1, source_target_pairs={{0,2},{1,3},{2,0},{3,1},{4,6},{5,7},{6,4},{7,5},{8,10},{9,11},{10,... | collective-permute-start | bytes 245768 | tf_op jit(solution)/shard_map/ppermute | solution.py:586
  22.5 0.0 collective-permute-start.2
  22.5 0.5 %regroup_near.1 = (f32[160,128]{1,0:T(8,128)S(1)}, f32[160,128]{1,0:T(8,128)S(1)}) custom-call(f32[8,64,128]{2,1,0:T(8,128)S(1)} %all_to_all.10.got_ref, f32[2,48,96]{2,1,0:T(8,128)S(1)} %copy-done, f32[2,56,128]{2,1,0:T(8,128)S(1)} %get-tuple-element.14.refs_0_.ext_ref), custom_call_target="tpu_custom_call" | custom-call | flops 1000000 | bytes 2000000 | tf_op jit(solution)/shard_map/regroup_near/pallas_call | solution.py:589
  23.0 0.0 copy-start.1
  23.0 0.0 copy-start.2
  23.0 0.7 %collective-permute-start = (f32[160,128]{1,0:T(8,128)S(1)}, f32[160,128]{1,0:T(8,128)S(1)}, u32[]{:S(2)}, u32[]{:S(2)}) collective-permute-start(f32[160,128]{1,0:T(8,128)S(1)} %get-tuple-element.16), channel_id=1, source_target_pairs={{0,1},{1,0},{2,3},{3,2},{4,5},{5,4},{6,7},{7,6},{8,9},{9,8},{10,11... | collective-permute-start | bytes 245768 | tf_op jit(solution)/shard_map/ppermute | solution.py:586
  23.7 0.0 copy-done.1
  23.7 0.0 copy-done.2
  23.7 0.1 table.1.table_ref
  23.9 1.6 %collective-permute-done.1.refs_2_ = f32[160,128]{1,0:T(8,128)S(1)} collective-permute-done((f32[160,128]{1,0:T(8,128)S(1)}, f32[160,128]{1,0:T(8,128)S(1)}, u32[]{:S(2)}, u32[]{:S(2)}) %collective-permute-start.1) | collective-permute-done | bytes 81952 | tf_op jit(solution)/shard_map/ppermute | solution.py:586
  25.4 1.8 %collective-permute-done.2.refs_3_ = f32[160,128]{1,0:T(8,128)S(1)} collective-permute-done((f32[160,128]{1,0:T(8,128)S(1)}, f32[160,128]{1,0:T(8,128)S(1)}, u32[]{:S(2)}, u32[]{:S(2)}) %collective-permute-start.2) | collective-permute-done | bytes 81952 | tf_op jit(solution)/shard_map/ppermute | solution.py:586
  27.2 0.0 collective-permute-done.refs_1_
  27.2 0.7 %basis.1 = (f32[12,48,96]{2,1,0:T(8,128)S(1)}, f32[3,2,48,96]{3,2,1,0:T(8,128)S(1)}, f32[32,1,128]{2,1,0:T(1,128)S(1)}) custom-call(f32[16,128]{1,0:T(8,128)S(1)} %table.1.table_ref, f32[2,56,128]{2,1,0:T(8,128)S(1)} %get-tuple-element.14.refs_0_.ext_ref, f32[160,128]{1,0:T(8,128)S(1)} %get-tuple-element.15.refs_0_, ...), custom_call_target="tpu_custom_call" | custom-call | tf_op jit(solution)/shard_map/basis/pallas_call | solution.py:599
  27.9 9.9 %all_to_all.11.sums_ref = f32[32,1,128]{2,1,0:T(1,128)S(1)} all-to-all(f32[32,1,128]{2,1,0:T(1,128)S(1)} %get-tuple-element.19), channel_id=1, replica_groups=mesh['row'=8,'col'=4] {'row','col'}, dimensions={0} | all-to-all | bytes 32768 | tf_op jit(solution)/shard_map/all_to_all | solution.py:612
  37.8 0.9 %finish.1 = (f32[2,48,96]{2,1,0:T(8,128)}, f32[2,48,96]{2,1,0:T(8,128)}, f32[12,48,96]{2,1,0:T(8,128)}) custom-call(f32[16,128]{1,0:T(8,128)S(1)} %table.1.table_ref, f32[32,1,128]{2,1,0:T(1,128)S(1)} %all_to_all.11.sums_ref, f32[2,48,96]{2,1,0:T(8,128)S(1)} %copy-done, f32[3,2,48,96]{3,2,1,0:T(8,128)S(1)} %get-tuple-element.20.basis_ref, ...), custom_call_target="tpu_custom_call" | custom-call | tf_op jit(solution)/shard_map/finish/pallas_call | solution.py:613
Async XLA Ops:
  3.9 16.3 %copy-start = (f32[2,48,96]{2,1,0:T(8,128)S(1)}, f32[2,48,96]{2,1,0:T(8,128)}, u32[]{:S(2)}) copy-start(f32[2,48,96]{2,1,0:T(8,128)} %field_ref.5) | copy-start | bytes 110596
  20.9 4.5 %collective-permute-start.1 = (f32[160,128]{1,0:T(8,128)S(1)}, f32[160,128]{1,0:T(8,128)S(1)}, u32[]{:S(2)}, u32[]{:S(2)}) collective-permute-start(f32[160,128]{1,0:T(8,128)S(1)} %get-tuple-element.17), channel_id=1, source_target_pairs={{0,2},{1,3},{2,0},{3,1},{4,6},{5,7},{6,4},{7,5},{8,10},{9,11},{10,... | collective-permute-start | bytes 245768 | tf_op jit(solution)/shard_map/ppermute | solution.py:586
  22.5 4.7 %collective-permute-start.2 = (f32[160,128]{1,0:T(8,128)S(1)}, f32[160,128]{1,0:T(8,128)S(1)}, u32[]{:S(2)}, u32[]{:S(2)}) collective-permute-start(f32[160,128]{1,0:T(8,128)S(1)} %get-tuple-element.18), channel_id=1, source_target_pairs={{0,3},{1,2},{2,1},{3,0},{4,7},{5,6},{6,5},{7,4},{8,11},{9,10},{10,... | collective-permute-start | bytes 245768 | tf_op jit(solution)/shard_map/ppermute | solution.py:586
  23.0 0.7 %copy-start.1 = (s32[6]{0:T(128)S(1)}, s32[6]{0:T(128)}, u32[]{:S(2)}) copy-start(s32[6]{0:T(128)} %cond_hbm.1) | copy-start | bytes 76
  23.0 0.7 %copy-start.2 = (f32[6]{0:T(128)S(1)}, f32[6]{0:T(128)}, u32[]{:S(2)}) copy-start(f32[6]{0:T(128)} %heat_hbm.1) | copy-start | bytes 76
  23.0 4.2 %collective-permute-start = (f32[160,128]{1,0:T(8,128)S(1)}, f32[160,128]{1,0:T(8,128)S(1)}, u32[]{:S(2)}, u32[]{:S(2)}) collective-permute-start(f32[160,128]{1,0:T(8,128)S(1)} %get-tuple-element.16), channel_id=1, source_target_pairs={{0,1},{1,0},{2,3},{3,2},{4,5},{5,4},{6,7},{7,6},{8,9},{9,8},{10,11... | collective-permute-start | bytes 245768 | tf_op jit(solution)/shard_map/ppermute | solution.py:586

commit v7 on v6

--- a/solution.py
+++ b/solution.py
@@ -23,7 +23,7 @@
 FULL = 63 * 1024 * 1024
 TINY = 1e-30
 F32 = jnp.float32
-EXACT = lax.Precision.HIGHEST
+BF16 = jnp.bfloat16
 
 
 def tiles(cells):
@@ -60,12 +60,26 @@
     return jnp.concatenate(parts + [jnp.concatenate(last, axis=0)], axis=1)
 
 
-def window_rows(row_count):
-    count = row_count // 2 - 1
-    rows = [[2 * q + 1, 2 * q + 2] for q in range(count)]
-    rows[0] = [0] + rows[0]
-    rows[-1] = rows[-1] + [row_count - 1]
-    return rows
+def product(lengths, dense, contract):
+    count = lengths.shape[0]
+    high = lengths.astype(BF16)
+    low = (lengths - high.astype(F32)).astype(BF16)
+    both = jnp.concatenate([high, low], axis=0)
+    first = dense.astype(BF16)
+    rest = dense - first.astype(F32)
+    second = rest.astype(BF16)
+    third = (rest - second.astype(F32)).astype(BF16)
+
+    def dot(left, right):
+        return lax.dot_general(
+            left, right, (((1,), (contract,)), ((), ())), preferred_element_type=F32
+        )
+
+    total = dot(high, third)
+    for piece in (second, first):
+        part = dot(both, piece)
+        total = (total + part[count:]) + part[:count]
+    return total
 
 
 def rezone_kernel(
@@ -88,7 +102,6 @@
     frac_ref,
     field_ref,
     edges_ref,
-    wide_ref,
     along_ref,
     out_ref,
     sems,
@@ -127,37 +140,28 @@
         window = edges_ref[row : row + 1, pl.ds(base, 2 * LANES)]
         return pltpu.roll(window, (lane - (start - base) + 2 * LANES) % (2 * LANES), 1)
 
-    starts = [from_here(0, max(r * TBLK - RIM, 0), 0 if r else RIM) for r in range(row_count)]
-    starts.append(from_here(1, me * TBLK, 0))
-    spare = jnp.zeros((-len(starts) % 8, LANES), F32)
-    columns = jnp.concatenate([start[:, 0:LANES] for start in starts] + [spare], axis=0)
-    columns = jnp.transpose(columns)[0 : ROWS + 8]
-    ends = pltpu.roll(columns, ROWS + 7, 0)
-    for r in range(row_count):
-        wide_ref[r, 8 : ROWS + 16] = jnp.broadcast_to(columns[:, r : r + 1], (ROWS + 8, LANES))
-    row = lax.broadcasted_iota(jnp.int32, (ROWS, LANES), 0)
-
-    def turned(r, ahead):
-        start = 8 + RIM + ahead
-        last = jnp.where(
-            row[0:8] < 8 - RIM,
-            wide_ref[r, start + ROWS - 8 : start + ROWS],
-            wide_ref[r, start - 8 : start],
-        )
-        return jnp.concatenate([wide_ref[r, start : start + ROWS - 8], last], axis=0)
-
-    def weights(src_lo, src_hi, low, high, scale):
-        shared = jnp.maximum(jnp.minimum(src_hi, high) - jnp.maximum(src_lo, low), 0.0)
-        return shared * scale
-
-    mine = slice(row_count, row_count + 1)
+    groups = tiles(row_count * TBLK)
+    mine = from_here(1, me * TBLK, 0)
+    lines = [
+        edges_ref[0:1, LANES * g + ahead : LANES * (g + 1) + ahead]
+        for ahead in (0, 1)
+        for g in range(groups)
+    ] + [turned[:, 0:LANES] for turned in (mine, pltpu.roll(mine, 2 * LANES - 1, 1))]
+    spare = -len(lines) % 8
+    if spare:
+        lines.append(jnp.zeros((spare, LANES), F32))
+    columns = jnp.transpose(jnp.concatenate(lines, axis=0))
+
+    def shared(src_lo, src_hi, low, high):
+        return jnp.maximum(jnp.minimum(src_hi, high) - jnp.maximum(src_lo, low), 0.0)
+
     lane = lax.broadcasted_iota(jnp.int32, (1, LANES), 1)
     x_lo = from_here(2, me * SBLK, 0)
     x_hi = pltpu.roll(x_lo, 2 * LANES - 1, 1)
-    x_tgt_lo, x_tgt_hi = columns[0:TBLK, mine], ends[0:TBLK, mine]
-    weight_x = weights(
-        x_lo[:, 0:SBLK], x_hi[:, 0:SBLK], x_tgt_lo, x_tgt_hi, 1.0 / (x_tgt_hi - x_tgt_lo)
-    )
+    low = columns[0:TBLK, 2 * groups : 2 * groups + 1]
+    high = columns[0:TBLK, 2 * groups + 1 : 2 * groups + 2]
+    shared_x = shared(x_lo[:, 0:SBLK], x_hi[:, 0:SBLK], low, high)
+    scale_x = 1.0 / (high - low)
     moves[5].wait()
     moves[6].wait()
     moves[7].wait()
@@ -188,53 +192,58 @@
     moves[4].wait()
     partial = [0.0, 0.0]
     for p in range(pairs):
-        along = jnp.dot(weight_x, frac_ref[p], precision=EXACT, preferred_element_type=F32)
+        along = product(shared_x, frac_ref[p], 0) * scale_x
         along_ref[p * TBLK : (p + 1) * TBLK, :] = along
         partial = [total + factor * along for total, factor in zip(partial, factors[p])]
     for n, total in enumerate(partial):
         along_ref[(pairs + n) * TBLK : (pairs + n + 1) * TBLK, :] = total
-    width = 4 * SBLK
-    weights_y = []
-    for q, rows in enumerate(window_rows(row_count)):
-        parts = []
-        for r in rows:
-            low, high = turned(r, 0), turned(r, 1)
-            inside = row < (TBLK if r + 1 == row_count else TBLK + RIM)
-            if r:
-                inside = inside | (row >= ROWS - RIM)
-            scale = jnp.where(inside, 1.0 / jnp.maximum(high - low, 1.0), 0.0)
-            wide = []
-            for at in range(2 * q * SBLK, 2 * q * SBLK + width, LANES):
-                src_lo, src_hi = edges_ref[3:4, at : at + LANES], edges_ref[3:4, at + 1 : at + 1 + LANES]
-                wide.append(weights(src_lo, src_hi, low, high, scale))
-            parts.append(jnp.concatenate(wide, axis=1))
-        weights_y.append(jnp.concatenate(parts, axis=0))
-    leaving = []
-    for q, rows in enumerate(window_rows(row_count)):
-        block = lax.dot_general(
-            weights_y[q],
-            along_ref[:, 2 * q * SBLK : 2 * q * SBLK + width],
-            (((1,), (1,)), ((), ())),
-            precision=EXACT,
-            preferred_element_type=F32,
-        )
-        for n, r in enumerate(rows):
-            mine = block[n * ROWS : (n + 1) * ROWS]
-            out_ref[r, 0:TBLK, :] = mine[0:TBLK, 0:LANES]
+    per, unit = 4, 64
+    width = per * SBLK
+    shared_y, scale_y = [], []
+    for q in range(row_count // per):
+        src_lo = edges_ref[3:4, q * width : (q + 1) * width]
+        src_hi = edges_ref[3:4, q * width + 1 : (q + 1) * width + 1]
+        parts, scales = [], []
+        for start in range(q * per * TBLK, (q + 1) * per * TBLK, unit):
+            g, at = divmod(start, LANES)
+            low = columns[at : at + unit, g : g + 1]
+            high = columns[at : at + unit, groups + g : groups + g + 1]
+            parts.append(shared(src_lo, src_hi, low, high))
+            scales.append(1.0 / (high - low))
+        shared_y.append(jnp.concatenate(parts, axis=0))
+        scale_y.append(jnp.concatenate(scales, axis=0))
+    row = lax.broadcasted_iota(jnp.int32, (8, LANES), 0)
+    leaving, firsts, lasts, sent = [], [], [], 0
+    for q in range(row_count // per):
+        block = product(shared_y[q], along_ref[:, q * width : (q + 1) * width], 1) * scale_y[q]
+        for n in range(per):
+            r = q * per + n
+            mine = block[n * TBLK : (n + 1) * TBLK]
+            out_ref[r, 0:TBLK, :] = mine[:, 0:LANES]
             packed = jnp.where(lane < TAIL, mine[0:8, LANES:], 0.0)
             for g in range(1, GROUPS):
                 group = jnp.where(lane < TAIL, mine[8 * g : 8 * g + 8, LANES:], 0.0)
                 packed = packed + pltpu.roll(group, TAIL * g, 1)
-            edge = pltpu.roll(mine[TBLK:ROWS, LANES:], LANES - TAIL, 1)
-            edge = jnp.where(lane < 2 * TBLK, edge, 0.0)
             if compact(breadth):
                 packed = packed + jnp.where(r > me, rims[1][0], rims[0][0])
+            out_ref[r, TBLK : TBLK + 8, :] = packed
+            firsts.append(mine[0:8, LANES:])
+            lasts.append(mine[TBLK - 8 :, LANES:])
+        ready = row_count if r + 1 == row_count else r
+        for r in range(sent, ready):
+            edge = jnp.zeros((8, LANES), F32)
+            if r + 1 < row_count:
+                edge = jnp.where(row < RIM, firsts[r + 1], edge)
+            if r:
+                edge = jnp.where(row >= 8 - RIM, lasts[r - 1], edge)
+            edge = jnp.where(lane < 2 * TBLK, pltpu.roll(edge, LANES - TAIL, 1), 0.0)
+            if compact(breadth):
                 edge = edge + jnp.where(r > me, rims[1][1], rims[0][1])
-            out_ref[r, TBLK : TBLK + 8, :] = packed
             out_ref[r, ROWS:BODY, :] = edge
-        done = pl.ds(rows[0], len(rows))
+        done = pl.ds(sent, ready - sent)
         leaving.append(pltpu.make_async_copy(out_ref.at[done], out_hbm.at[done], out_sems.at[q]))
         leaving[-1].start()
+        sent = ready
     for move in leaving:
         move.wait()
 
@@ -552,11 +561,10 @@
             pltpu.VMEM(fractions_source.shape, F32),
             pltpu.VMEM(thermal_source_term.shape, F32),
             pltpu.VMEM((8, LANES * (tiles(source_cells + 1) + 1)), F32),
-            pltpu.VMEM((row_count, ROWS + 16, LANES), F32),
             pltpu.VMEM((along_rows, source_cells), F32),
             pltpu.VMEM(outgoing.shape, F32),
             pltpu.SemaphoreType.DMA((8,)),
-            pltpu.SemaphoreType.DMA((row_count // 2 - 1,)),
+            pltpu.SemaphoreType.DMA((row_count // 4,)),
         ],
         compiler_params=pltpu.CompilerParams(vmem_limit_bytes=FULL),
         name="rezone",

time: 39 us -> 38.8 us (level)
  no operation moved by 1% of the time
where the time goes in v7:
time: 38.8 us; the launch traced here: 38.5 us
  blocking collectives  26.3 us (68%)
  Pallas kernels  5.88 us (15%)
  waiting for transfers between devices  3.32 us (9%)
  starting transfers between devices  2.27 us (6%)
  between operations  0.69 us (2%)
    all_to_all x1, blocking collectives, per_device(): lax.all_to_all(outgoing, 'row', split_axis=0, concat_axis=0, tiled=True)  16.3 us
    all_to_all x1, blocking collectives, per_device(): lax.all_to_all(sums, ('row', 'col'), split_axis=0, concat_axis=0, tiled=T...  9.95 us
    ppermute x3, waiting for transfers between devices, swap(): return lax.ppermute(part, 'col', [(c, c ^ mask) for c in range(col_count)])  3.32 us
    pallas_call x1, Pallas kernels, per_device(): pl.pallas_call(functools.partial(rezone_kernel, row_count), out_shape=out...  3.06 us
    ppermute x3, starting transfers between devices, swap(): return lax.ppermute(part, 'col', [(c, c ^ mask) for c in range(col_count)])  2.27 us
    pallas_call x1, Pallas kernels, per_device(): pl.pallas_call(finish_kernel, out_shape=[jax.ShapeDtypeStruct((zlayers, h...  0.87 us
  transfers between devices with their start and end apart: 3, of which 2 were waited for; matrix products, arithmetic and copies ran while one was open for 0% of the time, Pallas kernels for 2%

profile of v7, /device:TPU:0, one launch (start us, length us, event | category | flops | bytes accessed | tf_op | source)
XLA Modules:
  0.0 38.5 jit_solution(9206391019965047850)
XLA Ops:
  0.6 3.1 %rezone.1 = f32[8,64,128]{2,1,0:T(8,128)} custom-call(s32[513]{0:T(1024)} %xs_hbm.1, s32[385]{0:T(512)} %xt_hbm.1, s32[513]{0:T(1024)} %ys_hbm.1, s32[385]{0:T(512)} %yt_hbm.1, s32[6]{0:T(128)} %cond_hbm.1, f32[6]{0:T(128)} %heat_hbm.1, f32[3,64,512]{2,1,0:T(8,128)} %frac_hbm.1, f32[2,48,96]{2,1,0:T(8,128)} %field_ref.5), custom_call_target="tpu_custom_call" | custom-call | tf_op jit(solution)/shard_map/rezone/pallas_call | solution.py:554
  3.7 0.0 copy-start
  3.7 16.3 %all_to_all.10.got_ref = f32[8,64,128]{2,1,0:T(8,128)S(1)} all-to-all(f32[8,64,128]{2,1,0:T(8,128)} %rezone.1), channel_id=1, replica_groups=mesh['row'=8,'col'=4] {'row'}, dimensions={0} | all-to-all | bytes 524288 | tf_op jit(solution)/shard_map/all_to_all | solution.py:572
  20.0 0.0 copy-done
  20.1 0.6 %regroup_far.1 = (f32[2,56,128]{2,1,0:T(8,128)S(1)}, f32[160,128]{1,0:T(8,128)S(1)}, f32[160,128]{1,0:T(8,128)S(1)}) custom-call(f32[8,64,128]{2,1,0:T(8,128)S(1)} %all_to_all.10.got_ref, f32[2,48,96]{2,1,0:T(8,128)S(1)} %copy-done), custom_call_target="tpu_custom_call" | custom-call | tf_op jit(solution)/shard_map/regroup_far/pallas_call | solution.py:584
  20.7 1.6 %collective-permute-start.1 = (f32[160,128]{1,0:T(8,128)S(1)}, f32[160,128]{1,0:T(8,128)S(1)}, u32[]{:S(2)}, u32[]{:S(2)}) collective-permute-start(f32[160,128]{1,0:T(8,128)S(1)} %get-tuple-element.17), channel_id=1, source_target_pairs={{0,2},{1,3},{2,0},{3,1},{4,6},{5,7},{6,4},{7,5},{8,10},{9,11},{10,... | collective-permute-start | bytes 245768 | tf_op jit(solution)/shard_map/ppermute | solution.py:594
  22.3 0.0 collective-permute-start.2
  22.3 0.5 %regroup_near.1 = (f32[160,128]{1,0:T(8,128)S(1)}, f32[160,128]{1,0:T(8,128)S(1)}) custom-call(f32[8,64,128]{2,1,0:T(8,128)S(1)} %all_to_all.10.got_ref, f32[2,48,96]{2,1,0:T(8,128)S(1)} %copy-done, f32[2,56,128]{2,1,0:T(8,128)S(1)} %get-tuple-element.14.refs_0_.ext_ref), custom_call_target="tpu_custom_call" | custom-call | flops 1000000 | bytes 2000000 | tf_op jit(solution)/shard_map/regroup_near/pallas_call | solution.py:597
  22.8 0.0 copy-start.1
  22.8 0.0 copy-start.2
  22.8 0.7 %collective-permute-start = (f32[160,128]{1,0:T(8,128)S(1)}, f32[160,128]{1,0:T(8,128)S(1)}, u32[]{:S(2)}, u32[]{:S(2)}) collective-permute-start(f32[160,128]{1,0:T(8,128)S(1)} %get-tuple-element.16), channel_id=1, source_target_pairs={{0,1},{1,0},{2,3},{3,2},{4,5},{5,4},{6,7},{7,6},{8,9},{9,8},{10,11... | collective-permute-start | bytes 245768 | tf_op jit(solution)/shard_map/ppermute | solution.py:594
  23.5 0.0 copy-done.1
  23.5 0.0 copy-done.2
  23.5 0.1 table.1.table_ref
  23.6 1.6 %collective-permute-done.1.refs_2_ = f32[160,128]{1,0:T(8,128)S(1)} collective-permute-done((f32[160,128]{1,0:T(8,128)S(1)}, f32[160,128]{1,0:T(8,128)S(1)}, u32[]{:S(2)}, u32[]{:S(2)}) %collective-permute-start.1) | collective-permute-done | bytes 81952 | tf_op jit(solution)/shard_map/ppermute | solution.py:594
  25.2 1.8 %collective-permute-done.2.refs_3_ = f32[160,128]{1,0:T(8,128)S(1)} collective-permute-done((f32[160,128]{1,0:T(8,128)S(1)}, f32[160,128]{1,0:T(8,128)S(1)}, u32[]{:S(2)}, u32[]{:S(2)}) %collective-permute-start.2) | collective-permute-done | bytes 81952 | tf_op jit(solution)/shard_map/ppermute | solution.py:594
  27.0 0.0 collective-permute-done.refs_1_
  27.0 0.7 %basis.1 = (f32[12,48,96]{2,1,0:T(8,128)S(1)}, f32[3,2,48,96]{3,2,1,0:T(8,128)S(1)}, f32[32,1,128]{2,1,0:T(1,128)S(1)}) custom-call(f32[16,128]{1,0:T(8,128)S(1)} %table.1.table_ref, f32[2,56,128]{2,1,0:T(8,128)S(1)} %get-tuple-element.14.refs_0_.ext_ref, f32[160,128]{1,0:T(8,128)S(1)} %get-tuple-element.15.refs_0_, ...), custom_call_target="tpu_custom_call" | custom-call | tf_op jit(solution)/shard_map/basis/pallas_call | solution.py:607
  27.7 9.9 %all_to_all.11.sums_ref = f32[32,1,128]{2,1,0:T(1,128)S(1)} all-to-all(f32[32,1,128]{2,1,0:T(1,128)S(1)} %get-tuple-element.19), channel_id=1, replica_groups=mesh['row'=8,'col'=4] {'row','col'}, dimensions={0} | all-to-all | bytes 32768 | tf_op jit(solution)/shard_map/all_to_all | solution.py:620
  37.6 0.9 %finish.1 = (f32[2,48,96]{2,1,0:T(8,128)}, f32[2,48,96]{2,1,0:T(8,128)}, f32[12,48,96]{2,1,0:T(8,128)}) custom-call(f32[16,128]{1,0:T(8,128)S(1)} %table.1.table_ref, f32[32,1,128]{2,1,0:T(1,128)S(1)} %all_to_all.11.sums_ref, f32[2,48,96]{2,1,0:T(8,128)S(1)} %copy-done, f32[3,2,48,96]{3,2,1,0:T(8,128)S(1)} %get-tuple-element.20.basis_ref, ...), custom_call_target="tpu_custom_call" | custom-call | tf_op jit(solution)/shard_map/finish/pallas_call | solution.py:621
Async XLA Ops:
  3.7 16.4 %copy-start = (f32[2,48,96]{2,1,0:T(8,128)S(1)}, f32[2,48,96]{2,1,0:T(8,128)}, u32[]{:S(2)}) copy-start(f32[2,48,96]{2,1,0:T(8,128)} %field_ref.5) | copy-start | bytes 110596
  20.7 4.5 %collective-permute-start.1 = (f32[160,128]{1,0:T(8,128)S(1)}, f32[160,128]{1,0:T(8,128)S(1)}, u32[]{:S(2)}, u32[]{:S(2)}) collective-permute-start(f32[160,128]{1,0:T(8,128)S(1)} %get-tuple-element.17), channel_id=1, source_target_pairs={{0,2},{1,3},{2,0},{3,1},{4,6},{5,7},{6,4},{7,5},{8,10},{9,11},{10,... | collective-permute-start | bytes 245768 | tf_op jit(solution)/shard_map/ppermute | solution.py:594
  22.3 4.7 %collective-permute-start.2 = (f32[160,128]{1,0:T(8,128)S(1)}, f32[160,128]{1,0:T(8,128)S(1)}, u32[]{:S(2)}, u32[]{:S(2)}) collective-permute-start(f32[160,128]{1,0:T(8,128)S(1)} %get-tuple-element.18), channel_id=1, source_target_pairs={{0,3},{1,2},{2,1},{3,0},{4,7},{5,6},{6,5},{7,4},{8,11},{9,10},{10,... | collective-permute-start | bytes 245768 | tf_op jit(solution)/shard_map/ppermute | solution.py:594
  22.8 0.7 %copy-start.1 = (s32[6]{0:T(128)S(1)}, s32[6]{0:T(128)}, u32[]{:S(2)}) copy-start(s32[6]{0:T(128)} %cond_hbm.1) | copy-start | bytes 76
  22.8 0.7 %copy-start.2 = (f32[6]{0:T(128)S(1)}, f32[6]{0:T(128)}, u32[]{:S(2)}) copy-start(f32[6]{0:T(128)} %heat_hbm.1) | copy-start | bytes 76
  22.8 4.2 %collective-permute-start = (f32[160,128]{1,0:T(8,128)S(1)}, f32[160,128]{1,0:T(8,128)S(1)}, u32[]{:S(2)}, u32[]{:S(2)}) collective-permute-start(f32[160,128]{1,0:T(8,128)S(1)} %get-tuple-element.16), channel_id=1, source_target_pairs={{0,1},{1,0},{2,3},{3,2},{4,5},{5,4},{6,7},{7,6},{8,9},{9,8},{10,11... | collective-permute-start | bytes 245768 | tf_op jit(solution)/shard_map/ppermute | solution.py:594

commit v8 on v7

--- a/solution.py
+++ b/solution.py
@@ -15,10 +15,10 @@
 ROWS = 56
 LANES = 128
 EDGE = ROWS - TBLK
-GROUPS = TBLK // 8
-TAIL = 16
-CHUNK = LANES - GROUPS * TAIL
-BODY = ROWS + 8
+HALF = TBLK // 2
+KEPT = 2 * TBLK + HALF
+CHUNK = LANES - 2 * TBLK
+BODY = ROWS
 VMEM = 48 * 1024 * 1024
 FULL = 63 * 1024 * 1024
 TINY = 1e-30
@@ -35,29 +35,34 @@
 
 
 def pack_rims(rims):
-    count = rims.shape[0]
-    side = jnp.zeros((count, LANES - CHUNK), F32)
+    count, spare = rims.shape[0], LANES - KEPT
     below = jnp.zeros((8 - count, LANES), F32)
-    tail = jnp.concatenate([side, rims[:, 0:CHUNK]], axis=1)
-    edge = jnp.concatenate([side, rims[:, CHUNK : 2 * CHUNK]], axis=1)
+    side = jnp.zeros((count, KEPT), F32)
+    own = []
+    for at in range(CHUNK, 2 * CHUNK, spare):
+        own += [jnp.concatenate([side, rims[:, at : at + spare]], axis=1), below]
+    own.append(jnp.zeros((TBLK - 8 * CHUNK // spare, LANES), F32))
+    edge = jnp.concatenate([jnp.zeros((count, LANES - CHUNK), F32), rims[:, 0:CHUNK]], axis=1)
     lines = []
     for at in (0, RIM):
         parts = [rims[at + n : at + n + 1, 2 * CHUNK :] for n in range(RIM)]
         lines.append(jnp.concatenate(parts + [jnp.zeros((1, CHUNK), F32)], axis=1))
     gap = [jnp.zeros((RIM, LANES), F32)] + lines + [jnp.zeros((EDGE - RIM - 2, LANES), F32)]
     return (
-        jnp.concatenate([tail, below], axis=0),
+        jnp.concatenate(own, axis=0),
         jnp.concatenate([edge, below], axis=0) + jnp.concatenate(gap, axis=0),
     )
 
 
-def unpack_rims(tail, edge, count):
+def unpack_rims(own, edge, count):
+    spare = LANES - KEPT
     last = [
         edge[RIM + n // RIM : RIM + n // RIM + 1, CHUNK * (n % RIM) : CHUNK * (n % RIM + 1)]
         for n in range(count)
     ]
-    parts = [tail[0:count, LANES - CHUNK :], edge[0:count, LANES - CHUNK :]]
-    return jnp.concatenate(parts + [jnp.concatenate(last, axis=0)], axis=1)
+    middle = [own[8 * n : 8 * n + count, KEPT:] for n in range(CHUNK // spare)]
+    parts = [edge[0:count, LANES - CHUNK :]] + middle + [jnp.concatenate(last, axis=0)]
+    return jnp.concatenate(parts, axis=1)
 
 
 def product(lengths, dense, contract):
@@ -127,8 +132,8 @@
     for move in moves:
         move.start()
     edges_ref[...] = jnp.zeros_like(edges_ref)
-    used = (pairs + 2) * TBLK
-    along_ref[used:, :] = jnp.zeros_like(along_ref[used:, :])
+    for rows in (slice(KEPT, LANES), slice(LANES + 2 * TBLK, along_ref.shape[0])):
+        along_ref[rows, :] = jnp.zeros_like(along_ref[rows, :])
     for n, ref in enumerate((yt_ref, xt_ref, xs_ref, ys_ref)):
         moves[n].wait()
         edges_ref[n : n + 1, 0 : ref.shape[0]] = ref[...].astype(F32)[None, :]
@@ -193,10 +198,14 @@
     partial = [0.0, 0.0]
     for p in range(pairs):
         along = product(shared_x, frac_ref[p], 0) * scale_x
-        along_ref[p * TBLK : (p + 1) * TBLK, :] = along
+        if p + 1 < pairs:
+            along_ref[p * TBLK : (p + 1) * TBLK, :] = along
+        else:
+            even = lax.rem(lax.axis_index("col"), 2) == 0
+            along_ref[KEPT - HALF : KEPT, :] = jnp.where(even, along[0:HALF], along[HALF:])
         partial = [total + factor * along for total, factor in zip(partial, factors[p])]
     for n, total in enumerate(partial):
-        along_ref[(pairs + n) * TBLK : (pairs + n + 1) * TBLK, :] = total
+        along_ref[LANES + n * TBLK : LANES + (n + 1) * TBLK, :] = total
     per, unit = 4, 64
     width = per * SBLK
     shared_y, scale_y = [], []
@@ -219,14 +228,10 @@
         for n in range(per):
             r = q * per + n
             mine = block[n * TBLK : (n + 1) * TBLK]
-            out_ref[r, 0:TBLK, :] = mine[:, 0:LANES]
-            packed = jnp.where(lane < TAIL, mine[0:8, LANES:], 0.0)
-            for g in range(1, GROUPS):
-                group = jnp.where(lane < TAIL, mine[8 * g : 8 * g + 8, LANES:], 0.0)
-                packed = packed + pltpu.roll(group, TAIL * g, 1)
+            mine_own = mine[:, 0:LANES]
             if compact(breadth):
-                packed = packed + jnp.where(r > me, rims[1][0], rims[0][0])
-            out_ref[r, TBLK : TBLK + 8, :] = packed
+                mine_own = mine_own + jnp.where(r > me, rims[1][0], rims[0][0])
+            out_ref[r, 0:TBLK, :] = mine_own
             firsts.append(mine[0:8, LANES:])
             lasts.append(mine[TBLK - 8 :, LANES:])
         ready = row_count if r + 1 == row_count else r
@@ -236,10 +241,10 @@
                 edge = jnp.where(row < RIM, firsts[r + 1], edge)
             if r:
                 edge = jnp.where(row >= 8 - RIM, lasts[r - 1], edge)
-            edge = jnp.where(lane < 2 * TBLK, pltpu.roll(edge, LANES - TAIL, 1), 0.0)
+            edge = jnp.where(lane < 2 * TBLK, edge, 0.0)
             if compact(breadth):
                 edge = edge + jnp.where(r > me, rims[1][1], rims[0][1])
-            out_ref[r, ROWS:BODY, :] = edge
+            out_ref[r, TBLK:ROWS, :] = edge
         done = pl.ds(sent, ready - sent)
         leaving.append(pltpu.make_async_copy(out_ref.at[done], out_hbm.at[done], out_sems.at[q]))
         leaving[-1].start()
@@ -270,7 +275,7 @@
         (below, my_row > 0, ROWS - RIM),
     ):
         if compact(breadth):
-            rims = unpack_rims(got_ref[block, TBLK : TBLK + 8], got_ref[block, ROWS:BODY], count)
+            rims = unpack_rims(got_ref[block, 0:TBLK], got_ref[block, TBLK:ROWS], count)
         else:
             parts = [got_ref[block, BODY + 8 * t : BODY + 8 * t + count] for t in range(tiles(breadth))]
             rims = jnp.concatenate(parts, axis=1)[:, 0:breadth]
@@ -292,20 +297,17 @@
         extend_rows(row_count, got_ref, field_ref, ext_ref)
 
     def own(block, pair, first, last):
-        lo, hi = pair * TBLK + first, pair * TBLK + last
-        parts = []
-        if lo < LANES:
-            parts.append(got_ref[block, 0:TBLK, lo : min(hi, LANES)])
-        if hi > LANES:
-            a, b = max(lo, LANES) - LANES, hi - LANES
-            tail = got_ref[block, TBLK : TBLK + 8, :]
-            parts.append(
-                jnp.concatenate([tail[:, TAIL * g + a : TAIL * g + b] for g in range(GROUPS)], axis=0)
-            )
-        return parts[0] if len(parts) == 1 else jnp.concatenate(parts, axis=1)
+        start = pair * TBLK
+        if pair + 1 < pairs:
+            return got_ref[block, 0:TBLK, start + first : start + last]
+        if last - first == TBLK:
+            half = got_ref[block, 0:TBLK, start : start + HALF]
+            return jnp.concatenate([half, half], axis=1)
+        first = first % HALF
+        return got_ref[block, 0:TBLK, start + first : start + first + RIM]
 
     def edge(block, which, first, last):
-        return got_ref[block, ROWS:BODY, which * TBLK + first : which * TBLK + last]
+        return got_ref[block, TBLK:ROWS, which * TBLK + first : which * TBLK + last]
 
     for mask, out_ref in zip(masks, out_refs):
         c = my_col ^ mask
@@ -341,9 +343,6 @@
     pairs = arrivals[0].shape[0] // TBLK
     for mask, arrival in enumerate(arrivals):
         got_ref[my_col ^ mask] = arrival[...]
-        for p in range(pairs):
-            at = (my_col ^ mask) * pairs + p
-            shares_ref[at] = arrival[p * TBLK : (p + 1) * TBLK, 0:breadth]
     zlayers = ext_ref.shape[0]
     rows, width = ext_ref.shape[1:]
     lane = lax.broadcasted_iota(jnp.int32, (rows, width), 1)
@@ -362,16 +361,29 @@
         return table_ref[n : n + 1, 0:1]
 
     row = lax.broadcasted_iota(jnp.int32, (rows, width), 0)
-    inside = ((lane < breadth + RIM) | (lane >= width - RIM)) & (
-        (row < TBLK + RIM) | (row >= ROWS - RIM)
-    )
+    to_right = (lane >= breadth) & (lane < breadth + RIM)
+    to_left = lane >= width - RIM
+    inside = (lane < breadth) | (to_right & (my_col < col_count - 1)) | (to_left & (my_col > 0))
+    inside = inside & ((row < TBLK + RIM) | (row >= ROWS - RIM))
+    early = ((lane < breadth) & (lax.rem(lane, TBLK) < HALF)) | to_right
+    early = early[0:TBLK]
 
     cell_k, heat, field = [], [], []
     for z in range(zlayers):
         inverse, total = 0.0, 0.0
+        shares = []
         for m in range(M):
             c, p = divmod(z * M + m, pairs)
-            share = got_ref[c, p * TBLK : (p + 1) * TBLK]
+            shares.append(got_ref[c, p * TBLK : (p + 1) * TBLK])
+        known = jnp.where(early, shares[pairs - 1], shares[M - 1])
+        missing = 1.0 - known
+        for m in range(M):
+            if m not in (pairs - 1, M - 1):
+                missing = missing - shares[m]
+        shares[pairs - 1] = jnp.where(early, known, missing)
+        shares[M - 1] = jnp.where(early, missing, known)
+        for m, share in enumerate(shares):
+            shares_ref[z * M + m] = share[:, 0:breadth]
             inverse = inverse + share * entry(m)
             total = total + share * entry(M + m)
         edge_inverse, edge_total = 0.0, 0.0
@@ -453,9 +465,9 @@
     field_ref,
     basis_ref,
     shares_ref,
+    shares_hbm,
     iterate_hbm,
     defect_hbm,
-    shares_hbm,
     iterate_ref,
     defect_ref,
     sems,
@@ -541,7 +553,7 @@
 
     vmem = pl.BlockSpec(memory_space=pltpu.VMEM)
     hbm = pl.BlockSpec(memory_space=pltpu.HBM)
-    along_rows = -(-(pairs + 2) * TBLK // LANES) * LANES
+    along_rows = 2 * LANES
     small = [
         x_source_edges,
         x_target_edges,
@@ -618,10 +630,10 @@
         name="basis",
     )(table, extended, *parts)
     sums = lax.all_to_all(sums, ("row", "col"), split_axis=0, concat_axis=0, tiled=True)
-    thermal_iterate, remaining_defect, rezoned_occupancy_shares = pl.pallas_call(
+    rezoned_occupancy_shares, thermal_iterate, remaining_defect = pl.pallas_call(
         finish_kernel,
-        out_shape=[jax.ShapeDtypeStruct((zlayers, height, breadth), F32)] * 2
-        + [jax.ShapeDtypeStruct(shares.shape, F32)],
+        out_shape=[jax.ShapeDtypeStruct(shares.shape, F32)]
+        + [jax.ShapeDtypeStruct((zlayers, height, breadth), F32)] * 2,
         in_specs=[vmem] * 5,
         out_specs=[hbm] * 3,
         scratch_shapes=[pltpu.VMEM((zlayers, height, breadth), F32)] * 2

time: 38.8 us -> 37.8 us (0.974)
  blocking collectives: 26.3 us -> 25.6 us
    all_to_all x1, blocking collectives: 16.3 us -> 15.9 us  [per_device(): lax.all_to_all(outgoing, 'row', split_axis=0, concat_axis=0, tiled=True)]
  transfers between devices with their start and end apart: 3 -> 3, of which waited for: 2 -> 2; matrix products, arithmetic and copies ran while one was open for 0% -> 0% of each run, Pallas kernels for 2% -> 1%
where the time goes in v8:
time: 37.8 us; the launch traced here: 37.5 us
  blocking collectives  25.6 us (68%)
  Pallas kernels  5.52 us (15%)
  waiting for transfers between devices  3.42 us (9%)
  starting transfers between devices  2.27 us (6%)
  between operations  0.69 us (2%)
    all_to_all x1, blocking collectives, per_device(): lax.all_to_all(outgoing, 'row', split_axis=0, concat_axis=0, tiled=True)  15.9 us
    all_to_all x1, blocking collectives, per_device(): lax.all_to_all(sums, ('row', 'col'), split_axis=0, concat_axis=0, tiled=T...  9.73 us
    ppermute x3, waiting for transfers between devices, swap(): return lax.ppermute(part, 'col', [(c, c ^ mask) for c in range(col_count)])  3.42 us
    pallas_call x1, Pallas kernels, per_device(): pl.pallas_call(functools.partial(rezone_kernel, row_count), out_shape=out...  2.93 us
    ppermute x3, starting transfers between devices, swap(): return lax.ppermute(part, 'col', [(c, c ^ mask) for c in range(col_count)])  2.27 us
    pallas_call x1, Pallas kernels, per_device(): pl.pallas_call(finish_kernel, out_shape=[jax.ShapeDtypeStruct(shares.shap...  0.87 us
  transfers between devices with their start and end apart: 3, of which 2 were waited for; matrix products, arithmetic and copies ran while one was open for 0% of the time, Pallas kernels for 1%

profile of v8, /device:TPU:0, one launch (start us, length us, event | category | flops | bytes accessed | tf_op | source)
XLA Modules:
  0.0 37.5 jit_solution(1867692630462434104)
XLA Ops:
  0.6 2.9 %rezone.1 = f32[8,56,128]{2,1,0:T(8,128)} custom-call(s32[513]{0:T(1024)} %xs_hbm.1, s32[385]{0:T(512)} %xt_hbm.1, s32[513]{0:T(1024)} %ys_hbm.1, s32[385]{0:T(512)} %yt_hbm.1, s32[6]{0:T(128)} %cond_hbm.1, f32[6]{0:T(128)} %heat_hbm.1, f32[3,64,512]{2,1,0:T(8,128)} %frac_hbm.1, f32[2,48,96]{2,1,0:T(8,128)} %field_ref.5), custom_call_target="tpu_custom_call" | custom-call | tf_op jit(solution)/shard_map/rezone/pallas_call | solution.py:566
  3.6 0.0 copy-start
  3.6 15.9 %all_to_all.10.got_ref = f32[8,56,128]{2,1,0:T(8,128)S(1)} all-to-all(f32[8,56,128]{2,1,0:T(8,128)} %rezone.1), channel_id=1, replica_groups=mesh['row'=8,'col'=4] {'row'}, dimensions={0} | all-to-all | bytes 458752 | tf_op jit(solution)/shard_map/all_to_all | solution.py:584
  19.4 0.0 copy-done
  19.4 0.5 %regroup_far.1 = (f32[2,56,128]{2,1,0:T(8,128)S(1)}, f32[160,128]{1,0:T(8,128)S(1)}, f32[160,128]{1,0:T(8,128)S(1)}) custom-call(f32[8,56,128]{2,1,0:T(8,128)S(1)} %all_to_all.10.got_ref, f32[2,48,96]{2,1,0:T(8,128)S(1)} %copy-done), custom_call_target="tpu_custom_call" | custom-call | tf_op jit(solution)/shard_map/regroup_far/pallas_call | solution.py:596
  20.0 1.6 %collective-permute-start.1 = (f32[160,128]{1,0:T(8,128)S(1)}, f32[160,128]{1,0:T(8,128)S(1)}, u32[]{:S(2)}, u32[]{:S(2)}) collective-permute-start(f32[160,128]{1,0:T(8,128)S(1)} %get-tuple-element.14), channel_id=1, source_target_pairs={{0,2},{1,3},{2,0},{3,1},{4,6},{5,7},{6,4},{7,5},{8,10},{9,11},{10,... | collective-permute-start | bytes 245768 | tf_op jit(solution)/shard_map/ppermute | solution.py:606
  21.5 0.0 collective-permute-start.2
  21.5 0.4 %regroup_near.1 = (f32[160,128]{1,0:T(8,128)S(1)}, f32[160,128]{1,0:T(8,128)S(1)}) custom-call(f32[8,56,128]{2,1,0:T(8,128)S(1)} %all_to_all.10.got_ref, f32[2,48,96]{2,1,0:T(8,128)S(1)} %copy-done, f32[2,56,128]{2,1,0:T(8,128)S(1)} %get-tuple-element.11.refs_0_.ext_ref), custom_call_target="tpu_custom_call" | custom-call | flops 1000000 | bytes 2000000 | tf_op jit(solution)/shard_map/regroup_near/pallas_call | solution.py:609
  21.9 0.0 copy-start.1
  21.9 0.0 copy-start.2
  21.9 0.7 %collective-permute-start = (f32[160,128]{1,0:T(8,128)S(1)}, f32[160,128]{1,0:T(8,128)S(1)}, u32[]{:S(2)}, u32[]{:S(2)}) collective-permute-start(f32[160,128]{1,0:T(8,128)S(1)} %get-tuple-element.13), channel_id=1, source_target_pairs={{0,1},{1,0},{2,3},{3,2},{4,5},{5,4},{6,7},{7,6},{8,9},{9,8},{10,11... | collective-permute-start | bytes 245768 | tf_op jit(solution)/shard_map/ppermute | solution.py:606
  22.7 0.0 copy-done.1
  22.7 0.0 copy-done.2
  22.7 0.1 table.1.table_ref
  22.8 1.7 %collective-permute-done.1.refs_2_ = f32[160,128]{1,0:T(8,128)S(1)} collective-permute-done((f32[160,128]{1,0:T(8,128)S(1)}, f32[160,128]{1,0:T(8,128)S(1)}, u32[]{:S(2)}, u32[]{:S(2)}) %collective-permute-start.1) | collective-permute-done | bytes 81952 | tf_op jit(solution)/shard_map/ppermute | solution.py:606
  24.5 1.8 %collective-permute-done.2.refs_3_ = f32[160,128]{1,0:T(8,128)S(1)} collective-permute-done((f32[160,128]{1,0:T(8,128)S(1)}, f32[160,128]{1,0:T(8,128)S(1)}, u32[]{:S(2)}, u32[]{:S(2)}) %collective-permute-start.2) | collective-permute-done | bytes 81952 | tf_op jit(solution)/shard_map/ppermute | solution.py:606
  26.2 0.0 collective-permute-done.refs_1_
  26.2 0.7 %basis.1 = (f32[12,48,96]{2,1,0:T(8,128)S(1)}, f32[3,2,48,96]{3,2,1,0:T(8,128)S(1)}, f32[32,1,128]{2,1,0:T(1,128)S(1)}) custom-call(f32[16,128]{1,0:T(8,128)S(1)} %table.1.table_ref, f32[2,56,128]{2,1,0:T(8,128)S(1)} %get-tuple-element.11.refs_0_.ext_ref, f32[160,128]{1,0:T(8,128)S(1)} %get-tuple-element.12.refs_0_, ...), custom_call_target="tpu_custom_call" | custom-call | tf_op jit(solution)/shard_map/basis/pallas_call | solution.py:619
  26.9 9.7 %all_to_all.11.sums_ref = f32[32,1,128]{2,1,0:T(1,128)S(1)} all-to-all(f32[32,1,128]{2,1,0:T(1,128)S(1)} %get-tuple-element.16), channel_id=1, replica_groups=mesh['row'=8,'col'=4] {'row','col'}, dimensions={0} | all-to-all | bytes 32768 | tf_op jit(solution)/shard_map/all_to_all | solution.py:632
  36.6 0.9 %finish.1 = (f32[12,48,96]{2,1,0:T(8,128)}, f32[2,48,96]{2,1,0:T(8,128)}, f32[2,48,96]{2,1,0:T(8,128)}) custom-call(f32[16,128]{1,0:T(8,128)S(1)} %table.1.table_ref, f32[32,1,128]{2,1,0:T(1,128)S(1)} %all_to_all.11.sums_ref, f32[2,48,96]{2,1,0:T(8,128)S(1)} %copy-done, f32[3,2,48,96]{3,2,1,0:T(8,128)S(1)} %get-tuple-element.17.basis_ref, ...), custom_call_target="tpu_custom_call" | custom-call | tf_op jit(solution)/shard_map/finish/pallas_call | solution.py:633
Async XLA Ops:
  3.6 15.9 %copy-start = (f32[2,48,96]{2,1,0:T(8,128)S(1)}, f32[2,48,96]{2,1,0:T(8,128)}, u32[]{:S(2)}) copy-start(f32[2,48,96]{2,1,0:T(8,128)} %field_ref.5) | copy-start | bytes 110596
  20.0 4.5 %collective-permute-start.1 = (f32[160,128]{1,0:T(8,128)S(1)}, f32[160,128]{1,0:T(8,128)S(1)}, u32[]{:S(2)}, u32[]{:S(2)}) collective-permute-start(f32[160,128]{1,0:T(8,128)S(1)} %get-tuple-element.14), channel_id=1, source_target_pairs={{0,2},{1,3},{2,0},{3,1},{4,6},{5,7},{6,4},{7,5},{8,10},{9,11},{10,... | collective-permute-start | bytes 245768 | tf_op jit(solution)/shard_map/ppermute | solution.py:606
  21.5 4.7 %collective-permute-start.2 = (f32[160,128]{1,0:T(8,128)S(1)}, f32[160,128]{1,0:T(8,128)S(1)}, u32[]{:S(2)}, u32[]{:S(2)}) collective-permute-start(f32[160,128]{1,0:T(8,128)S(1)} %get-tuple-element.15), channel_id=1, source_target_pairs={{0,3},{1,2},{2,1},{3,0},{4,7},{5,6},{6,5},{7,4},{8,11},{9,10},{10,... | collective-permute-start | bytes 245768 | tf_op jit(solution)/shard_map/ppermute | solution.py:606
  21.9 0.7 %copy-start.1 = (s32[6]{0:T(128)S(1)}, s32[6]{0:T(128)}, u32[]{:S(2)}) copy-start(s32[6]{0:T(128)} %cond_hbm.1) | copy-start | bytes 76
  21.9 0.7 %copy-start.2 = (f32[6]{0:T(128)S(1)}, f32[6]{0:T(128)}, u32[]{:S(2)}) copy-start(f32[6]{0:T(128)} %heat_hbm.1) | copy-start | bytes 76
  21.9 4.3 %collective-permute-start = (f32[160,128]{1,0:T(8,128)S(1)}, f32[160,128]{1,0:T(8,128)S(1)}, u32[]{:S(2)}, u32[]{:S(2)}) collective-permute-start(f32[160,128]{1,0:T(8,128)S(1)} %get-tuple-element.13), channel_id=1, source_target_pairs={{0,1},{1,0},{2,3},{3,2},{4,5},{5,4},{6,7},{7,6},{8,9},{9,8},{10,11... | collective-permute-start | bytes 245768 | tf_op jit(solution)/shard_map/ppermute | solution.py:606

commit v9 on v8

--- a/solution.py
+++ b/solution.py
@@ -286,12 +286,11 @@
         ext_ref[layer, 0:height, 0:breadth] = field_ref[layer]
 
 
-def regroup_kernel(row_count, col_count, masks, got_ref, field_ref, *refs):
+def regroup_kernel(row_count, col_count, pairs, masks, got_ref, field_ref, *refs):
     my_col = lax.axis_index("col")
     zlayers, _, breadth = field_ref.shape
     ext_ref, out_refs = refs[0], refs[1:]
     width = out_refs[0].shape[1]
-    pairs = out_refs[0].shape[0] // TBLK
     per_col = row_count // col_count
     if col_count // 2 in masks:
         extend_rows(row_count, got_ref, field_ref, ext_ref)
@@ -313,6 +312,37 @@
         c = my_col ^ mask
         start = c * per_col
         left, right = jnp.maximum(start - 1, 0), jnp.minimum(start + per_col, row_count - 1)
+
+        def short(cells, kind, extra):
+            parts = [cells(start + j, kind, 0, TBLK) for j in range(per_col)]
+            count = parts[0].shape[0]
+            parts.append(jnp.where(c < col_count - 1, cells(right, kind, 0, RIM), 0.0))
+            parts.append(extra)
+            used = breadth + 2 * RIM + extra.shape[1]
+            parts.append(jnp.zeros((count, width - used), F32))
+            parts.append(jnp.where(c > 0, cells(left, kind, TBLK - RIM, TBLK), 0.0))
+            return jnp.concatenate(parts, axis=1)
+
+        if compact(breadth):
+            last = (pairs - 1) * TBLK
+            for p in range(pairs - 1):
+                extra = got_ref[start + p, 0:TBLK, last : last + HALF]
+                out_ref[p * TBLK : (p + 1) * TBLK] = short(own, p, extra)
+            for n in range(2):
+                at = last + EDGE * n
+                out_ref[at : at + EDGE] = short(edge, n, jnp.zeros((EDGE, RIM), F32))
+            even = lax.rem(my_col, 2) == 0
+            rim = jnp.where(
+                even, own(right, pairs - 1, 0, RIM), own(left, pairs - 1, TBLK - RIM, TBLK)
+            )
+            parts = [rim[8 * g : 8 * g + 8] for g in range(TBLK // 8)]
+            for layer in range(zlayers if mask else 0):
+                whole = ext_ref[layer]
+                cols = jnp.where(c > my_col, whole[:, breadth - RIM : breadth], whole[:, 0:RIM])
+                parts += [cols[8 * g : 8 * g + 8] for g in range(ROWS // 8)]
+            parts.append(jnp.zeros((8, width - RIM * len(parts)), F32))
+            out_ref[last + 2 * EDGE :] = jnp.concatenate(parts, axis=1)
+            continue
 
         def line(cells, rows, kind, layer):
             parts = [cells(start + j, kind, 0, TBLK) for j in range(per_col)]
@@ -336,15 +366,30 @@
             out_ref[at : at + EDGE] = line(edge, slice(TBLK, ROWS), n, n)
 
 
-def basis_kernel(col_count, height, breadth, table_ref, ext_ref, *refs):
+def basis_kernel(col_count, pairs, height, breadth, table_ref, ext_ref, *refs):
     arrivals, refs = refs[:col_count], refs[col_count:]
     shares_ref, basis_ref, sums_ref, got_ref = refs
     my_col = lax.axis_index("col")
-    pairs = arrivals[0].shape[0] // TBLK
+    rows, width = ext_ref.shape[1:]
+    last = (pairs - 1) * TBLK
+    end = pairs * TBLK + 2 * EDGE
     for mask, arrival in enumerate(arrivals):
-        got_ref[my_col ^ mask] = arrival[...]
+        c = my_col ^ mask
+        if not compact(breadth):
+            got_ref[c] = arrival[...]
+            continue
+        got_ref[c, 0:last] = arrival[0:last]
+        got_ref[c, pairs * TBLK :] = arrival[last:]
+        parts = []
+        for p in range(pairs - 1):
+            at = breadth + RIM
+            parts += [arrival[p * TBLK : (p + 1) * TBLK, at : at + HALF]] * 2
+        tile = arrival[last + 2 * EDGE :]
+        rim = [tile[:, RIM * g : RIM * (g + 1)] for g in range(TBLK // 8)]
+        rim = jnp.concatenate(rim, axis=0)
+        parts += [rim, jnp.zeros((TBLK, width - breadth - 2 * RIM), F32), rim]
+        got_ref[c, last : pairs * TBLK] = jnp.concatenate(parts, axis=1)
     zlayers = ext_ref.shape[0]
-    rows, width = ext_ref.shape[1:]
     lane = lax.broadcasted_iota(jnp.int32, (rows, width), 1)
     before, after = jnp.maximum(my_col - 1, 0), jnp.minimum(my_col + 1, col_count - 1)
 
@@ -389,24 +434,43 @@
         edge_inverse, edge_total = 0.0, 0.0
         for c in range(z * M // pairs, (z + 1) * M // pairs):
             edge_inverse = edge_inverse + got_ref[c, pairs * TBLK : pairs * TBLK + EDGE]
-            edge_total = edge_total + got_ref[c, pairs * TBLK + EDGE :]
+            edge_total = edge_total + got_ref[c, pairs * TBLK + EDGE : end]
         inverse = jnp.concatenate([inverse, edge_inverse], axis=0)
         total = jnp.concatenate([total, edge_total], axis=0)
         inverse, total = (jnp.where(inside, value, 0.0) for value in (inverse, total))
         cell_k.append(jnp.where(inverse > 0.0, 1.0 / jnp.where(inverse > 0.0, inverse, 1.0), 0.0))
         heat.append(total)
-        left, right = (
-            jnp.concatenate(
+        if compact(breadth):
+            sides = []
+            for c in (before, after):
+                at = RIM * (TBLK // 8 + z * ROWS // 8)
+                parts = [
+                    got_ref[c, end : end + 8, at + RIM * g : at + RIM * (g + 1)]
+                    for g in range(ROWS // 8)
+                ]
+                sides.append(jnp.concatenate(parts, axis=0))
+            left = jnp.concatenate([jnp.zeros((rows, width - RIM), F32), sides[0]], axis=1)
+            right = jnp.concatenate(
                 [
-                    got_ref[c, z * TBLK : (z + 1) * TBLK],
-                    got_ref[c, pairs * TBLK + EDGE * z : pairs * TBLK + EDGE * (z + 1)],
+                    jnp.zeros((rows, breadth), F32),
+                    sides[1],
+                    jnp.zeros((rows, width - breadth - RIM), F32),
                 ],
-                axis=0,
+                axis=1,
             )
-            for c in (before, after)
-        )
-        left = pltpu.roll(left, width - (breadth + 2 * RIM), 1)
-        right = pltpu.roll(right, width - RIM, 1)
+        else:
+            left, right = (
+                jnp.concatenate(
+                    [
+                        got_ref[c, z * TBLK : (z + 1) * TBLK],
+                        got_ref[c, pairs * TBLK + EDGE * z : pairs * TBLK + EDGE * (z + 1)],
+                    ],
+                    axis=0,
+                )
+                for c in (before, after)
+            )
+            left = pltpu.roll(left, width - (breadth + 2 * RIM), 1)
+            right = pltpu.roll(right, width - RIM, 1)
         value = ext_ref[z]
         value = jnp.where(
             (lane >= breadth) & (lane < breadth + RIM) & (my_col < col_count - 1), right, value
@@ -590,11 +654,12 @@
         compiler_params=params,
         name="table",
     )(conductivity_table, capacity)
-    message = jax.ShapeDtypeStruct((pairs * TBLK + 2 * EDGE, width), F32)
+    plain = pairs * TBLK + 2 * EDGE
+    message = jax.ShapeDtypeStruct((plain + 8 - TBLK if compact(breadth) else plain, width), F32)
     half = col_count // 2
     near, far = range(half), range(half, col_count)
     extended, *far_parts = pl.pallas_call(
-        functools.partial(regroup_kernel, row_count, col_count, far),
+        functools.partial(regroup_kernel, row_count, col_count, pairs, far),
         out_shape=[jax.ShapeDtypeStruct((zlayers, ROWS, width), F32)] + [message] * half,
         in_specs=[vmem] * 2,
         out_specs=[vmem] * (1 + half),
@@ -607,7 +672,7 @@
 
     far_parts = [swap(part, mask) for part, mask in zip(far_parts, far)]
     near_parts = pl.pallas_call(
-        functools.partial(regroup_kernel, row_count, col_count, near),
+        functools.partial(regroup_kernel, row_count, col_count, pairs, near),
         out_shape=[message] * half,
         in_specs=[vmem] * 3,
         out_specs=[vmem] * half,
@@ -617,7 +682,7 @@
     )(arrived, thermal_source_term, extended)
     parts = [swap(part, mask) if mask else part for part, mask in zip(near_parts, near)] + far_parts
     shares, basis, sums = pl.pallas_call(
-        functools.partial(basis_kernel, col_count, height, breadth),
+        functools.partial(basis_kernel, col_count, pairs, height, breadth),
         out_shape=[
             jax.ShapeDtypeStruct((zlayers * M, height, breadth), F32),
             jax.ShapeDtypeStruct((ITERS, zlayers, height, breadth), F32),
@@ -625,7 +690,7 @@
         ],
         in_specs=[vmem] * (2 + col_count),
         out_specs=[vmem] * 3,
-        scratch_shapes=[pltpu.VMEM((col_count, *message.shape), F32)],
+        scratch_shapes=[pltpu.VMEM((col_count, plain + 8 * compact(breadth), width), F32)],
         compiler_params=params,
         name="basis",
     )(table, extended, *parts)

time: 37.8 us -> 37.3 us (0.987)
  waiting for transfers between devices: 3.42 us -> 2.84 us
    ppermute x3, waiting for transfers between devices: 3.42 us -> 2.84 us  [swap(): return lax.ppermute(part, 'col', [(c, c ^ mask) for c in range(col_count)])]
where the time goes in v9:
time: 37.3 us; the launch traced here: 37 us
  blocking collectives  25.6 us (69%)
  Pallas kernels  5.59 us (15%)
  waiting for transfers between devices  2.84 us (8%)
  starting transfers between devices  2.27 us (6%)
  between operations  0.69 us (2%)
    all_to_all x1, blocking collectives, per_device(): lax.all_to_all(outgoing, 'row', split_axis=0, concat_axis=0, tiled=True)  15.9 us
    all_to_all x1, blocking collectives, per_device(): lax.all_to_all(sums, ('row', 'col'), split_axis=0, concat_axis=0, tiled=T...  9.73 us
    pallas_call x1, Pallas kernels, per_device(): pl.pallas_call(functools.partial(rezone_kernel, row_count), out_shape=out...  2.93 us
    ppermute x3, waiting for transfers between devices, swap(): return lax.ppermute(part, 'col', [(c, c ^ mask) for c in range(col_count)])  2.84 us
    ppermute x3, starting transfers between devices, swap(): return lax.ppermute(part, 'col', [(c, c ^ mask) for c in range(col_count)])  2.27 us
    pallas_call x1, Pallas kernels, per_device(): pl.pallas_call(functools.partial(basis_kernel, col_count, pairs, height,...  0.95 us
    pallas_call x1, Pallas kernels, per_device(): pl.pallas_call(finish_kernel, out_shape=[jax.ShapeDtypeStruct(shares.shap...  0.87 us
  transfers between devices with their start and end apart: 3, of which 2 were waited for; matrix products, arithmetic and copies ran while one was open for 0% of the time, Pallas kernels for 1%

profile of v9, /device:TPU:0, one launch (start us, length us, event | category | flops | bytes accessed | tf_op | source)
XLA Modules:
  0.0 37.0 jit_solution(12475997438007456083)
XLA Ops:
  0.6 2.9 %rezone.1 = f32[8,56,128]{2,1,0:T(8,128)} custom-call(s32[513]{0:T(1024)} %xs_hbm.1, s32[385]{0:T(512)} %xt_hbm.1, s32[513]{0:T(1024)} %ys_hbm.1, s32[385]{0:T(512)} %yt_hbm.1, s32[6]{0:T(128)} %cond_hbm.1, f32[6]{0:T(128)} %heat_hbm.1, f32[3,64,512]{2,1,0:T(8,128)} %frac_hbm.1, f32[2,48,96]{2,1,0:T(8,128)} %field_ref.5), custom_call_target="tpu_custom_call" | custom-call | tf_op jit(solution)/shard_map/rezone/pallas_call | solution.py:630
  3.6 0.0 copy-start
  3.6 15.9 %all_to_all.10.got_ref = f32[8,56,128]{2,1,0:T(8,128)S(1)} all-to-all(f32[8,56,128]{2,1,0:T(8,128)} %rezone.1), channel_id=1, replica_groups=mesh['row'=8,'col'=4] {'row'}, dimensions={0} | all-to-all | bytes 458752 | tf_op jit(solution)/shard_map/all_to_all | solution.py:648
  19.4 0.0 copy-done
  19.4 0.4 %regroup_far.1 = (f32[2,56,128]{2,1,0:T(8,128)S(1)}, f32[120,128]{1,0:T(8,128)S(1)}, f32[120,128]{1,0:T(8,128)S(1)}) custom-call(f32[8,56,128]{2,1,0:T(8,128)S(1)} %all_to_all.10.got_ref, f32[2,48,96]{2,1,0:T(8,128)S(1)} %copy-done), custom_call_target="tpu_custom_call" | custom-call | tf_op jit(solution)/shard_map/regroup_far/pallas_call | solution.py:661
  19.8 1.6 %collective-permute-start.1 = (f32[120,128]{1,0:T(8,128)S(1)}, f32[120,128]{1,0:T(8,128)S(1)}, u32[]{:S(2)}, u32[]{:S(2)}) collective-permute-start(f32[120,128]{1,0:T(8,128)S(1)} %get-tuple-element.14), channel_id=1, source_target_pairs={{0,2},{1,3},{2,0},{3,1},{4,6},{5,7},{6,4},{7,5},{8,10},{9,11},{10,... | collective-permute-start | bytes 184328 | tf_op jit(solution)/shard_map/ppermute | solution.py:671
  21.4 0.0 collective-permute-start.2
  21.4 0.3 regroup_near.1
  21.7 0.0 copy-start.1
  21.7 0.0 copy-start.2
  21.7 0.7 %collective-permute-start = (f32[120,128]{1,0:T(8,128)S(1)}, f32[120,128]{1,0:T(8,128)S(1)}, u32[]{:S(2)}, u32[]{:S(2)}) collective-permute-start(f32[120,128]{1,0:T(8,128)S(1)} %get-tuple-element.13), channel_id=1, source_target_pairs={{0,1},{1,0},{2,3},{3,2},{4,5},{5,4},{6,7},{7,6},{8,9},{9,8},{10,11... | collective-permute-start | bytes 184328 | tf_op jit(solution)/shard_map/ppermute | solution.py:671
  22.4 0.0 copy-done.1
  22.5 0.0 copy-done.2
  22.5 0.1 table.1.table_ref
  22.6 1.5 %collective-permute-done.1.refs_2_ = f32[120,128]{1,0:T(8,128)S(1)} collective-permute-done((f32[120,128]{1,0:T(8,128)S(1)}, f32[120,128]{1,0:T(8,128)S(1)}, u32[]{:S(2)}, u32[]{:S(2)}) %collective-permute-start.1) | collective-permute-done | bytes 61472 | tf_op jit(solution)/shard_map/ppermute | solution.py:671
  24.1 1.3 %collective-permute-done.2.refs_3_ = f32[120,128]{1,0:T(8,128)S(1)} collective-permute-done((f32[120,128]{1,0:T(8,128)S(1)}, f32[120,128]{1,0:T(8,128)S(1)}, u32[]{:S(2)}, u32[]{:S(2)}) %collective-permute-start.2) | collective-permute-done | bytes 61472 | tf_op jit(solution)/shard_map/ppermute | solution.py:671
  25.4 0.0 collective-permute-done.refs_1_
  25.4 0.9 %basis.1 = (f32[12,48,96]{2,1,0:T(8,128)S(1)}, f32[3,2,48,96]{3,2,1,0:T(8,128)S(1)}, f32[32,1,128]{2,1,0:T(1,128)S(1)}) custom-call(f32[16,128]{1,0:T(8,128)S(1)} %table.1.table_ref, f32[2,56,128]{2,1,0:T(8,128)S(1)} %get-tuple-element.11.refs_0_.ext_ref, f32[120,128]{1,0:T(8,128)S(1)} %get-tuple-element.12.refs_0_, ...), custom_call_target="tpu_custom_call" | custom-call | tf_op jit(solution)/shard_map/basis/pallas_call | solution.py:684
  26.4 9.7 %all_to_all.11.sums_ref = f32[32,1,128]{2,1,0:T(1,128)S(1)} all-to-all(f32[32,1,128]{2,1,0:T(1,128)S(1)} %get-tuple-element.16), channel_id=1, replica_groups=mesh['row'=8,'col'=4] {'row','col'}, dimensions={0} | all-to-all | bytes 32768 | tf_op jit(solution)/shard_map/all_to_all | solution.py:697
  36.1 0.9 %finish.1 = (f32[12,48,96]{2,1,0:T(8,128)}, f32[2,48,96]{2,1,0:T(8,128)}, f32[2,48,96]{2,1,0:T(8,128)}) custom-call(f32[16,128]{1,0:T(8,128)S(1)} %table.1.table_ref, f32[32,1,128]{2,1,0:T(1,128)S(1)} %all_to_all.11.sums_ref, f32[2,48,96]{2,1,0:T(8,128)S(1)} %copy-done, f32[3,2,48,96]{3,2,1,0:T(8,128)S(1)} %get-tuple-element.17.basis_ref, ...), custom_call_target="tpu_custom_call" | custom-call | tf_op jit(solution)/shard_map/finish/pallas_call | solution.py:698
Async XLA Ops:
  3.6 15.9 %copy-start = (f32[2,48,96]{2,1,0:T(8,128)S(1)}, f32[2,48,96]{2,1,0:T(8,128)}, u32[]{:S(2)}) copy-start(f32[2,48,96]{2,1,0:T(8,128)} %field_ref.5) | copy-start | bytes 110596
  19.8 4.3 %collective-permute-start.1 = (f32[120,128]{1,0:T(8,128)S(1)}, f32[120,128]{1,0:T(8,128)S(1)}, u32[]{:S(2)}, u32[]{:S(2)}) collective-permute-start(f32[120,128]{1,0:T(8,128)S(1)} %get-tuple-element.14), channel_id=1, source_target_pairs={{0,2},{1,3},{2,0},{3,1},{4,6},{5,7},{6,4},{7,5},{8,10},{9,11},{10,... | collective-permute-start | bytes 184328 | tf_op jit(solution)/shard_map/ppermute | solution.py:671
  21.4 4.1 %collective-permute-start.2 = (f32[120,128]{1,0:T(8,128)S(1)}, f32[120,128]{1,0:T(8,128)S(1)}, u32[]{:S(2)}, u32[]{:S(2)}) collective-permute-start(f32[120,128]{1,0:T(8,128)S(1)} %get-tuple-element.15), channel_id=1, source_target_pairs={{0,3},{1,2},{2,1},{3,0},{4,7},{5,6},{6,5},{7,4},{8,11},{9,10},{10,... | collective-permute-start | bytes 184328 | tf_op jit(solution)/shard_map/ppermute | solution.py:671
  21.7 0.7 %copy-start.1 = (s32[6]{0:T(128)S(1)}, s32[6]{0:T(128)}, u32[]{:S(2)}) copy-start(s32[6]{0:T(128)} %cond_hbm.1) | copy-start | bytes 76
  21.7 0.7 %copy-start.2 = (f32[6]{0:T(128)S(1)}, f32[6]{0:T(128)}, u32[]{:S(2)}) copy-start(f32[6]{0:T(128)} %heat_hbm.1) | copy-start | bytes 76
  21.7 3.7 %collective-permute-start = (f32[120,128]{1,0:T(8,128)S(1)}, f32[120,128]{1,0:T(8,128)S(1)}, u32[]{:S(2)}, u32[]{:S(2)}) collective-permute-start(f32[120,128]{1,0:T(8,128)S(1)} %get-tuple-element.13), channel_id=1, source_target_pairs={{0,1},{1,0},{2,3},{3,2},{4,5},{5,4},{6,7},{7,6},{8,9},{9,8},{10,11... | collective-permute-start | bytes 184328 | tf_op jit(solution)/shard_map/ppermute | solution.py:671
